TPU v7x, 32 devices: a whole 2x2x4 slice. The times are simulated.
32 devices in a mesh: pb: 4 (over y, core), pa: 8 (over z, x).
Axes of the slice: x: 2, y: 2, z: 4, core: 2. Of those that a mesh axis runs over, the one named last changes fastest.
Arguments:
- questions: bfloat16 [256, 64, 768], P(('pb', 'pa')), may hold values from -6 to 6
- passages: bfloat16 [128, 256, 768], P(('pb', 'pa')), may hold values from -6 to 6
- cot_questions: bfloat16 [256, 64, 768], P(('pb', 'pa')), may hold values from -2.390625 to 2.390625
- cot_passages: bfloat16 [128, 256, 768], P(('pb', 'pa')), may hold values from -2.390625 to 2.390625
- question_lengths: int32 [256], P(('pb', 'pa')), may hold values from 16 to 64
- segment_lengths: int32 [128, 4], P(('pb', 'pa')), may hold values from 1 to 128, 256 in all within a row
- positives: int32 [256], P('pb'), may hold values from 0 to 511
- w_qkv: bfloat16 [2, 768, 2304], P(None, 'pb', 'pa'), may hold values from -0.21875 to 0.21875
- w_out: bfloat16 [2, 768, 768], P(None, 'pb', 'pa'), may hold values from -1.25 to 1.25
- w_up: bfloat16 [2, 768, 3072], P(None, 'pb', 'pa'), may hold values from -0.21875 to 0.21875
- w_down: bfloat16 [2, 3072, 768], P(None, 'pb', 'pa'), may hold values from -0.109375 to 0.109375
- norm_bias: bfloat16 [2, 8, 768], P(None, 'pb', 'pa'), may hold values from -0.59765625 to 1.4453125, as said below
- bias_up: bfloat16 [2, 3072], P(None, ('pb', 'pa')), may hold values from -1.1953125 to 1.1953125
Outputs:
- question_encodings: bfloat16 [256, 64, 768], P(('pb', 'pa'))
- passage_encodings: bfloat16 [128, 256, 768], P(('pb', 'pa'))
- question_losses: float32 [256], P(('pb', 'pa'))
- grad_questions: float32 [256, 64, 768], P(('pb', 'pa'))
- grad_passages: float32 [128, 256, 768], P(('pb', 'pa'))
- grad_w_qkv: float32 [2, 768, 2304], P(None, 'pb', 'pa')
- grad_w_out: float32 [2, 768, 768], P(None, 'pb', 'pa')
- grad_w_up: float32 [2, 768, 3072], P(None, 'pb', 'pa')
- grad_w_down: float32 [2, 3072, 768], P(None, 'pb', 'pa')
- grad_norm_bias: float32 [2, 8, 768], P(None, 'pb', 'pa')
- grad_bias_up: float32 [2, 3072], P(None, ('pb', 'pa'))
Inputs may be any that keep to these rules, and one draw needn't show every extreme that they name: `segment_lengths`: the 4 lengths of every row sum to 256. `norm_bias`: per encoder, rows 0 and 2 are norm gains near one, the other rows shifts and biases.
All inputs are finite; a program needn't handle non-finite values.
Results may differ from a plain program's by a relative error of at most 0.019.
Values may be sent and summed in bfloat16 or wider, within the bound.
No kernel may reach another device: no remote copies, remote signals or barrier semaphores. Data moves between devices by JAX's collectives and lax.ppermute only.
A program may use at most 320 MiB of HBM per device.

v0:
```python
import math

import jax
import jax.numpy as jnp
from jax import lax
from jax.sharding import PartitionSpec as P

HD = 64


NEG_FILL = -1000000000.0
EPSILON = 1e-06
ROOT_HALF = 0.7071067811865476
INV_ROOT_TWO_PI = 0.3989422804014327


def gelu_value(pre_act):
    return 0.5 * pre_act * (1.0 + lax.erf(pre_act * ROOT_HALF))


def gelu_slope(pre_act):
    return (
        0.5 * (1.0 + lax.erf(pre_act * ROOT_HALF))
        + pre_act * jnp.exp(-0.5 * pre_act * pre_act) * INV_ROOT_TWO_PI
    )


def norm_rows(summed, gain_vec, shift_vec):
    row_mean = jnp.mean(summed, axis=-1, keepdims=True)
    centred = summed - row_mean
    inverse = lax.rsqrt(jnp.mean(centred * centred, axis=-1, keepdims=True) + EPSILON)
    normed = centred * inverse
    return (normed * gain_vec + shift_vec, normed, inverse)


def norm_back(grad_out, gain_vec, normed, inverse):
    scaled = grad_out * gain_vec
    inner_part = (
        scaled
        - jnp.mean(scaled, axis=-1, keepdims=True)
        - normed * jnp.mean(scaled * normed, axis=-1, keepdims=True)
    )
    return (inverse * inner_part, jnp.sum(grad_out * normed, axis=0), jnp.sum(grad_out, axis=0))


def attention_scores(queries, key_rows, allowed):
    raw_scores = jnp.einsum(
        "bqhd,bkhd->bhqk", queries, key_rows, preferred_element_type=jnp.float32
    ) * HD ** (-0.5)
    return jnp.where(allowed[:, None], raw_scores, NEG_FILL)


def gather_weights(shards):
    by_rows = (
        lax.all_gather(shards[0], "pb", axis=1, tiled=True),
        lax.all_gather(shards[1], "pb", axis=1, tiled=True),
        lax.all_gather(shards[2], "pb", axis=1, tiled=True),
        lax.all_gather(shards[3], "pb", axis=1, tiled=True),
        lax.all_gather(shards[4], "pb", axis=1, tiled=True),
        lax.all_gather(shards[5].reshape(2, 1, -1), "pb", axis=1, tiled=True),
    )
    whole_set = (
        lax.all_gather(by_rows[0], "pa", axis=2, tiled=True),
        lax.all_gather(by_rows[1], "pa", axis=2, tiled=True),
        lax.all_gather(by_rows[2], "pa", axis=2, tiled=True),
        lax.all_gather(by_rows[3], "pa", axis=2, tiled=True),
        lax.all_gather(by_rows[4], "pa", axis=2, tiled=True),
        lax.all_gather(by_rows[5], "pa", axis=2, tiled=True),
    )
    return whole_set[:5] + (whole_set[5].reshape(2, -1),)


def encoder_slice(full_weights, encoder):
    return tuple((member[encoder] for member in full_weights))


def forward_layer(inputs, allowed, weights):
    w_qkv, w_out, w_up, w_down, vectors, bias_up = weights
    seq_count, seq_len, model_dim = inputs.shape
    head_count = model_dim // HD
    token_count = seq_count * seq_len
    head_shape = (seq_count, seq_len, head_count, HD)
    flat_in = inputs.reshape(token_count, model_dim)
    vec_rows = vectors.astype(jnp.float32)
    projected = jnp.dot(flat_in, w_qkv, preferred_element_type=jnp.float32)
    queries = (projected[:, :model_dim] + vec_rows[4]).astype(jnp.bfloat16).reshape(head_shape)
    key_rows = projected[:, model_dim : 2 * model_dim].astype(jnp.bfloat16).reshape(head_shape)
    values = (projected[:, 2 * model_dim :] + vec_rows[5]).astype(jnp.bfloat16).reshape(head_shape)
    scores = attention_scores(queries, key_rows, allowed)
    row_peak = jnp.max(scores, axis=-1, keepdims=True)
    log_total = row_peak + jnp.log(jnp.sum(jnp.exp(scores - row_peak), axis=-1, keepdims=True))
    prob_low = jnp.exp(scores - log_total).astype(jnp.bfloat16)
    attended = (
        jnp.einsum("bhqk,bkhd->bqhd", prob_low, values, preferred_element_type=jnp.float32)
        .astype(jnp.bfloat16)
        .reshape(token_count, model_dim)
    )
    branch = jnp.dot(attended, w_out, preferred_element_type=jnp.float32) + vec_rows[6]
    first_norm, normed_one, inverse_one = norm_rows(
        flat_in.astype(jnp.float32) + branch, vec_rows[0], vec_rows[1]
    )
    first_low = first_norm.astype(jnp.bfloat16)
    hidden = jnp.dot(first_low, w_up, preferred_element_type=jnp.float32) + bias_up.astype(
        jnp.float32
    )
    gelu_low = gelu_value(hidden).astype(jnp.bfloat16)
    down_part = jnp.dot(gelu_low, w_down, preferred_element_type=jnp.float32) + vec_rows[7]
    result, normed_two, inverse_two = norm_rows(first_norm + down_part, vec_rows[2], vec_rows[3])
    kept_state = (
        queries,
        key_rows,
        values,
        log_total,
        attended,
        normed_one,
        inverse_one,
        first_low,
        hidden,
        gelu_low,
        normed_two,
        inverse_two,
    )
    return (result, kept_state)


def backward_layer(grad_out, inputs, allowed, weights, kept_state):
    w_qkv, w_out, w_up, w_down, vectors, bias_up = weights
    (
        queries,
        key_rows,
        values,
        log_total,
        attended,
        normed_one,
        inverse_one,
        first_low,
        hidden,
        gelu_low,
        normed_two,
        inverse_two,
    ) = kept_state
    seq_count, seq_len, model_dim = inputs.shape
    head_count = model_dim // HD
    token_count = seq_count * seq_len
    vec_rows = vectors.astype(jnp.float32)
    grad_two, gain_two_grad, shift_two_grad = norm_back(
        grad_out, vec_rows[2], normed_two, inverse_two
    )
    down_grad = grad_two.astype(jnp.bfloat16)
    w_down_grad = jnp.dot(gelu_low.T, down_grad, preferred_element_type=jnp.float32)
    hidden_grad = (
        jnp.dot(down_grad, w_down.T, preferred_element_type=jnp.float32) * gelu_slope(hidden)
    ).astype(jnp.bfloat16)
    w_up_grad = jnp.dot(first_low.T, hidden_grad, preferred_element_type=jnp.float32)
    first_grad = jnp.dot(hidden_grad, w_up.T, preferred_element_type=jnp.float32) + grad_two
    grad_one, gain_one_grad, shift_one_grad = norm_back(
        first_grad, vec_rows[0], normed_one, inverse_one
    )
    branch_grad = grad_one.astype(jnp.bfloat16)
    w_out_grad = jnp.dot(attended.T, branch_grad, preferred_element_type=jnp.float32)
    attended_grad = (
        jnp.dot(branch_grad, w_out.T, preferred_element_type=jnp.float32)
        .astype(jnp.bfloat16)
        .reshape(seq_count, seq_len, head_count, HD)
    )
    scores = attention_scores(queries, key_rows, allowed)
    prob_full = jnp.exp(scores - log_total)
    prob_grad = jnp.einsum(
        "bqhd,bkhd->bhqk", attended_grad, values, preferred_element_type=jnp.float32
    )
    score_grad = (
        prob_full * (prob_grad - jnp.sum(prob_full * prob_grad, axis=-1, keepdims=True))
    ).astype(jnp.bfloat16)
    query_grad = (
        (
            jnp.einsum("bhqk,bkhd->bqhd", score_grad, key_rows, preferred_element_type=jnp.float32)
            * HD ** (-0.5)
        )
        .astype(jnp.bfloat16)
        .reshape(token_count, model_dim)
    )
    key_grad = (
        (
            jnp.einsum("bhqk,bqhd->bkhd", score_grad, queries, preferred_element_type=jnp.float32)
            * HD ** (-0.5)
        )
        .astype(jnp.bfloat16)
        .reshape(token_count, model_dim)
    )
    value_grad = (
        jnp.einsum(
            "bhqk,bqhd->bkhd",
            prob_full.astype(jnp.bfloat16),
            attended_grad,
            preferred_element_type=jnp.float32,
        )
        .astype(jnp.bfloat16)
        .reshape(token_count, model_dim)
    )
    proj_grad = jnp.concatenate([query_grad, key_grad, value_grad], axis=1)
    flat_in = inputs.reshape(token_count, model_dim)
    w_qkv_grad = jnp.dot(flat_in.T, proj_grad, preferred_element_type=jnp.float32)
    input_grad = jnp.dot(proj_grad, w_qkv.T, preferred_element_type=jnp.float32) + grad_one
    vector_grad = jnp.stack(
        [
            gain_one_grad,
            shift_one_grad,
            gain_two_grad,
            shift_two_grad,
            jnp.sum(query_grad, axis=0, dtype=jnp.float32),
            jnp.sum(value_grad, axis=0, dtype=jnp.float32),
            jnp.sum(branch_grad, axis=0, dtype=jnp.float32),
            jnp.sum(down_grad, axis=0, dtype=jnp.float32),
        ]
    )
    bias_up_grad = jnp.sum(hidden_grad, axis=0, dtype=jnp.float32)
    return (
        input_grad.reshape(inputs.shape),
        (w_qkv_grad, w_out_grad, w_up_grad, w_down_grad, vector_grad, bias_up_grad),
    )


def body(
    questions,
    passages,
    cot_questions,
    cot_passages,
    question_lengths,
    segment_lengths,
    positives,
    w_qkv,
    w_out,
    w_up,
    w_down,
    norm_bias,
    bias_up,
):
    q_count, q_len, model_dim = questions.shape
    row_count = passages.shape[0]
    row_len = passages.shape[1]
    seg_count = segment_lengths.shape[1]
    size_pa = lax.axis_size("pa")
    size_pb = lax.axis_size("pb")
    index_pa = lax.axis_index("pa")
    key_index = jnp.arange(q_len, dtype=jnp.int32)
    allowed_q = jnp.broadcast_to(
        (key_index[None, :] < question_lengths[:, None])[:, None, :], (q_count, q_len, q_len)
    )
    starts = jnp.cumsum(segment_lengths, axis=1) - segment_lengths
    positions = jnp.arange(row_len, dtype=jnp.int32)
    seg_ids = jnp.sum((positions[None, None, :] >= starts[:, :, None]).astype(jnp.int32), axis=1)
    allowed_p = seg_ids[:, :, None] == seg_ids[:, None, :]
    shards = (w_qkv, w_out, w_up, w_down, norm_bias, bias_up)
    full_weights = gather_weights(shards)
    q_result, q_kept = forward_layer(questions, allowed_q, encoder_slice(full_weights, 0))
    p_result, p_kept = forward_layer(passages, allowed_p, encoder_slice(full_weights, 1))
    q_enc = q_result.astype(jnp.bfloat16).reshape(questions.shape)
    p_enc = p_result.astype(jnp.bfloat16).reshape(passages.shape)
    q_cls = q_enc[:, 0, :]
    p_cls = jnp.take_along_axis(p_enc, starts[:, :, None], axis=1).reshape(
        row_count * seg_count, model_dim
    )
    q_block = lax.all_gather(q_cls, "pa", axis=0, tiled=True)
    p_block = lax.all_gather(p_cls, "pb", axis=0, tiled=True)
    score_scale = 3.0 / math.sqrt(model_dim)
    score_tile = jnp.dot(q_block, p_block.T, preferred_element_type=jnp.float32) * score_scale
    per_device = row_count * seg_count
    column_pos = jnp.arange(per_device * size_pb, dtype=jnp.int32)
    column_ids = (
        column_pos // per_device * size_pa + index_pa
    ) * per_device + column_pos % per_device
    target_hits = column_ids[None, :] == positives[:, None]
    local_positive = jnp.sum(jnp.where(target_hits, score_tile, 0.0), axis=1)
    row_peak = lax.pmax(jnp.max(score_tile, axis=1), "pa")
    row_total, row_positive = lax.psum(
        (jnp.sum(jnp.exp(score_tile - row_peak[:, None]), axis=1), local_positive), "pa"
    )
    log_norm = row_peak + jnp.log(row_total)
    block_losses = log_norm - row_positive
    own_losses = lax.dynamic_slice_in_dim(block_losses, index_pa * q_count, q_count)
    tile_grad = jnp.exp(score_tile - log_norm[:, None]) - target_hits.astype(jnp.float32)
    q_part = (
        jnp.dot(tile_grad, p_block.astype(jnp.float32), precision=lax.Precision.HIGHEST)
        * score_scale
    )
    p_part = (
        jnp.dot(tile_grad.T, q_block.astype(jnp.float32), precision=lax.Precision.HIGHEST)
        * score_scale
    )
    q_cls_grad = lax.psum_scatter(
        q_part.astype(jnp.bfloat16), "pa", scatter_dimension=0, tiled=True
    ).astype(jnp.float32)
    p_cls_grad = lax.psum_scatter(
        p_part.astype(jnp.bfloat16), "pb", scatter_dimension=0, tiled=True
    ).astype(jnp.float32)
    cls_hits = (positions[None, None, :] == starts[:, :, None]).astype(jnp.float32)
    q_grad_out = cot_questions.astype(jnp.float32).at[:, 0, :].add(q_cls_grad)
    p_grad_out = cot_passages.astype(jnp.float32) + jnp.einsum(
        "rsl,rsd->rld",
        cls_hits,
        p_cls_grad.reshape(row_count, seg_count, model_dim),
        precision=lax.Precision.HIGHEST,
    )
    shards, q_grad_out, p_grad_out, questions, passages = lax.optimization_barrier(
        (shards, q_grad_out, p_grad_out, questions, passages)
    )
    full_weights = gather_weights(shards)
    q_kept = forward_layer(questions, allowed_q, encoder_slice(full_weights, 0))[1]
    p_kept = forward_layer(passages, allowed_p, encoder_slice(full_weights, 1))[1]
    q_in_grad, q_weight_grads = backward_layer(
        q_grad_out.reshape(-1, model_dim),
        questions,
        allowed_q,
        encoder_slice(full_weights, 0),
        q_kept,
    )
    p_in_grad, p_weight_grads = backward_layer(
        p_grad_out.reshape(-1, model_dim),
        passages,
        allowed_p,
        encoder_slice(full_weights, 1),
        p_kept,
    )
    stacked = tuple(
        (
            jnp.stack([first_item, second_item])
            for first_item, second_item in zip(q_weight_grads, p_weight_grads)
        )
    )
    by_columns = (
        lax.psum_scatter(
            stacked[0].astype(jnp.bfloat16), "pa", scatter_dimension=2, tiled=True
        ).astype(jnp.float32),
        lax.psum_scatter(
            stacked[1].astype(jnp.bfloat16), "pa", scatter_dimension=2, tiled=True
        ).astype(jnp.float32),
        lax.psum_scatter(
            stacked[2].astype(jnp.bfloat16), "pa", scatter_dimension=2, tiled=True
        ).astype(jnp.float32),
        lax.psum_scatter(
            stacked[3].astype(jnp.bfloat16), "pa", scatter_dimension=2, tiled=True
        ).astype(jnp.float32),
        lax.psum_scatter(
            stacked[4].astype(jnp.bfloat16), "pa", scatter_dimension=2, tiled=True
        ).astype(jnp.float32),
        lax.psum_scatter(
            stacked[5].reshape(2, size_pb, -1).astype(jnp.bfloat16),
            "pa",
            scatter_dimension=2,
            tiled=True,
        ).astype(jnp.float32),
    )
    owned_grads = (
        lax.psum_scatter(
            by_columns[0].astype(jnp.bfloat16), "pb", scatter_dimension=1, tiled=True
        ).astype(jnp.float32),
        lax.psum_scatter(
            by_columns[1].astype(jnp.bfloat16), "pb", scatter_dimension=1, tiled=True
        ).astype(jnp.float32),
        lax.psum_scatter(
            by_columns[2].astype(jnp.bfloat16), "pb", scatter_dimension=1, tiled=True
        ).astype(jnp.float32),
        lax.psum_scatter(
            by_columns[3].astype(jnp.bfloat16), "pb", scatter_dimension=1, tiled=True
        ).astype(jnp.float32),
        lax.psum_scatter(
            by_columns[4].astype(jnp.bfloat16), "pb", scatter_dimension=1, tiled=True
        ).astype(jnp.float32),
        lax.psum_scatter(
            by_columns[5].astype(jnp.bfloat16), "pb", scatter_dimension=1, tiled=True
        ).astype(jnp.float32),
    )
    owned_grads = owned_grads[:5] + (owned_grads[5].reshape(2, -1),)
    return (
        q_enc,
        p_enc,
        own_losses,
        q_in_grad,
        p_in_grad,
        owned_grads[0],
        owned_grads[1],
        owned_grads[2],
        owned_grads[3],
        owned_grads[4],
        owned_grads[5],
    )


def solution(mesh):
    in_specs = (
        P(("pb", "pa"), None, None),
        P(("pb", "pa"), None, None),
        P(("pb", "pa"), None, None),
        P(("pb", "pa"), None, None),
        P(("pb", "pa")),
        P(("pb", "pa"), None),
        P("pb"),
        P(None, "pb", "pa"),
        P(None, "pb", "pa"),
        P(None, "pb", "pa"),
        P(None, "pb", "pa"),
        P(None, "pb", "pa"),
        P(None, ("pb", "pa")),
    )
    out_specs = (
        P(("pb", "pa"), None, None),
        P(("pb", "pa"), None, None),
        P(("pb", "pa")),
        P(("pb", "pa"), None, None),
        P(("pb", "pa"), None, None),
        P(None, "pb", "pa"),
        P(None, "pb", "pa"),
        P(None, "pb", "pa"),
        P(None, "pb", "pa"),
        P(None, "pb", "pa"),
        P(None, ("pb", "pa")),
    )
    return jax.shard_map(body, mesh=mesh, in_specs=in_specs, out_specs=out_specs, check_vma=False)
```

profile of v0, /device:TPU:0, one launch (start us, length us, event | category | flops | bytes accessed | tf_op | source)
XLA Modules:
  0.0 2526.1 jit_solution(14512373072738840565)
XLA Ops:
  9.7 7.9 all_gather.82
  20.1 15.4 all_gather.78
  39.1 14.1 all-gather.26.cloned.1.call-done
  64.8 32.2 %all_gather.87 = bf16[2,4,768]{1,0,2:T(2,128)(2,1)S(1)} all-gather(bf16[2,4,96]{1,0,2:T(2,128)(2,1)S(1)} %copy.405), channel_id=1, replica_groups=mesh['pb'=4,'pa'=8] {'pa'}, dimensions={2}, use_global_device_ids=true | all-gather | bytes 13824 | tf_op jit(solution)/shard_map/all_gather | solution.py:68
  98.7 32.2 %all_gather.81 = bf16[2,8,768]{1,0,2:T(2,128)(2,1)S(1)} all-gather(bf16[2,8,96]{1,0,2:T(2,128)(2,1)S(1)} %copy.392), channel_id=1, replica_groups=mesh['pb'=4,'pa'=8] {'pa'}, dimensions={2}, use_global_device_ids=true | all-gather | bytes 27648 | tf_op jit(solution)/shard_map/all_gather | solution.py:67
  133.5 20.0 slice_reduce_fusion.15
  153.5 20.0 slice_reduce_fusion.23
  173.5 7.9 fusion.201
  192.2 31.3 %all-gather.18.cloned.1.call-done = bf16[2,768,2304]{1,0,2:T(2,128)(2,1)} async-done(((bf16[2,768,288]{1,0,2:T(2,128)(2,1)}), bf16[2,768,2304]{1,0,2:T(2,128)(2,1)}) %all-gather.18.cloned.1.call-update) | async-done | bytes 7077904 | tf_op jit(solution)/shard_map/all_gather | solution.py:63
  223.5 15.1 fusion.199
  238.6 16.0 copy.521
  254.5 16.1 copy.518
  332.6 29.2 %all-gather.24.cloned.1.call-done = bf16[2,768,3072]{2,1,0:T(8,128)(2,1)} async-done(((bf16[2,768,384]{2,1,0:T(8,128)(2,1)}), bf16[2,768,3072]{2,1,0:T(8,128)(2,1)}) %all-gather.24.cloned.1.call-update) | async-done | bytes 9437200 | tf_op jit(solution)/shard_map/all_gather | solution.py:65
  367.9 132.2 %all-gather.28.cloned.1.call-done = bf16[2,3072,768]{1,2,0:T(8,128)(2,1)} async-done(((bf16[2,3072,96]{1,2,0:T(8,128)(2,1)}), bf16[2,3072,768]{1,2,0:T(8,128)(2,1)}) %all-gather.28.cloned.1.call-update) | async-done | bytes 9437200 | tf_op jit(solution)/shard_map/all_gather | solution.py:66
  506.9 30.7 %all-gather.1 = bf16[64,1,768]{2,0,1:T(8,128)(2,1)S(1)} all-gather(bf16[8,1,768]{2,0,1:T(8,128)(2,1)S(1)} %copy.524), channel_id=3, replica_groups=mesh['pb'=4,'pa'=8] {'pa'}, dimensions={0}, use_global_device_ids=true | all-gather | bytes 110592 | tf_op jit(solution)/shard_map/all_gather | solution.py:263
  537.6 16.2 fusion.207
  563.1 18.5 pmax.7
  581.6 17.8 all-reduce.5
  602.1 16.6 reduce-scatter.25.cloned.1.call-done
  621.7 58.5 %reduce-scatter.23.cloned.1.call-done = bf16[8,768]{1,0:T(8,128)(2,1)} async-done(((bf16[64,768]{1,0:T(8,128)(2,1)}), bf16[8,768]{1,0:T(8,128)(2,1)}) %reduce-scatter.23.cloned.1.call-update) | async-done | bytes 12304 | tf_op jit(solution)/shard_map/reduce_scatter | solution.py:290
  693.6 11.3 all_gather.92
  710.6 8.0 all-gather.38.cloned.1.call-done
  729.3 32.2 %all_gather.95 = bf16[2,8,768]{1,0,2:T(2,128)(2,1)S(1)} all-gather(bf16[2,8,96]{1,0,2:T(2,128)(2,1)S(1)} %copy.425), channel_id=1, replica_groups=mesh['pb'=4,'pa'=8] {'pa'}, dimensions={2}, use_global_device_ids=true | all-gather | bytes 27648 | tf_op jit(solution)/shard_map/all_gather | solution.py:67
  762.1 39.8 %slice_reduce_fusion = (f32[768]{0:T(1024)S(1)}, f32[768]{0:T(1024)}, f32[768]{0:T(1024)}, f32[768]{0:T(1024)}, f32[768]{0:T(1024)S(1)}, /*index=5*/f32[768]{0:T...) fusion(f32[1,8,768]{1,0,2:T(1,128)S(1)} %get-tuple-element.194,, ...), kind=kLoop, calls=%fused_computation.246 | loop fusion | bytes 86016 | tf_op jit(solution)/shard_map/slice | solution.py:147
  806.6 32.6 %all_gather.101 = bf16[2,4,768]{1,0,2:T(2,128)(2,1)S(1)} all-gather(bf16[2,4,96]{1,0,2:T(2,128)(2,1)S(1)} %copy.437), channel_id=1, replica_groups=mesh['pb'=4,'pa'=8] {'pa'}, dimensions={2}, use_global_device_ids=true | all-gather | bytes 13824 | tf_op jit(solution)/shard_map/all_gather | solution.py:68
  841.5 7.8 fusion.200
  860.2 29.5 %all-gather.30.cloned.1.call-done = bf16[2,768,2304]{1,0,2:T(2,128)(2,1)} async-done(((bf16[2,768,288]{1,0,2:T(2,128)(2,1)}), bf16[2,768,2304]{1,0,2:T(2,128)(2,1)}) %all-gather.30.cloned.1.call-update) | async-done | bytes 7077904 | tf_op jit(solution)/shard_map/all_gather | solution.py:63
  889.8 15.0 fusion.198
  904.8 16.0 copy.528
  920.8 16.0 copy.525
  1021.6 7.1 all-gather.36.cloned.1.call-done
  1028.7 7.5 multiply_convert_fusion.3
  1036.2 130.8 %all-gather.40.cloned.1.call-done = bf16[2,3072,768]{1,2,0:T(8,128)(2,1)} async-done(((bf16[2,3072,96]{1,2,0:T(8,128)(2,1)}), bf16[2,3072,768]{1,2,0:T(8,128)(2,1)}) %all-gather.40.cloned.1.call-update) | async-done | bytes 9437200 | tf_op jit(solution)/shard_map/all_gather | solution.py:66
  1181.4 8.0 fusion.220
  1215.8 9.7 multiply_convert_fusion.1
  1225.4 10.0 fusion.214
  1241.0 7.0 fusion.29
  1248.0 14.2 fusion.219
  1262.1 9.2 multiply_reduce_fusion.1
  1284.7 9.5 fusion.216
  1294.2 10.7 multiply_reduce_fusion
  1304.9 7.3 multiply_convert_fusion
  1348.4 8.3 pad_maximum_fusion.1
  1356.7 24.1 copy.478
  1384.1 7.1 copy.477
  1407.9 18.2 copy.476
  1426.7 7.4 fusion.25
  1434.1 10.3 fusion.28
  1444.4 8.3 pad_maximum_fusion
  1452.7 23.8 copy.503
  1476.5 9.4 copy.541
  1491.3 503.0 %all-reduce.10.cloned.1.call-done = (bf16[2,768,2304]{1,0,2:T(2,128)(2,1)}, bf16[2,768,768]{1,0,2:T(2,128)(2,1)}, bf16[2,3072,768]{1,0,2:T(2,128)(2,1)}) async-done(((bf16[2,768,2304]{1,0,2:T(2,128)(2,1)}, bf16[2,768,768]{1,0,2:T(2,128)(2,1)}, bf16[2,3072,768]{1,0,2:T(2,128)(2,1)}), (bf16[2,768,2304]{1,0,2:T(2,128)(2,1)}, bf16[2,768,768]{1,0,2:T(2,128)(2,1)}, ...) | async-done | bytes 18874384
  1995.5 29.6 %copy.501 = bf16[2,768,96]{0,2,1:T(8,128)(2,1)} copy(bf16[2,768,96]{1,0,2:T(2,128)(2,1)S(1)} %constant_dynamic-slice_fusion.3) | data formatting | bytes 589824
  2025.1 29.1 %reshape.595 = bf16[768,192]{1,0:T(8,128)(2,1)} reshape(bf16[768,96,2]{2,1,0:T(8,128)(2,1)} %bitcast.329) | data formatting | bytes 589824
  2056.8 42.8 %copy.499 = bf16[2,768,288]{0,2,1:T(8,128)(2,1)} copy(bf16[2,768,288]{1,0,2:T(2,128)(2,1)S(1)} %constant_dynamic-slice_fusion.4) | data formatting | bytes 1769472
  2099.6 82.5 %reshape.593 = bf16[768,576]{1,0:T(8,128)(2,1)} reshape(bf16[768,288,2]{2,1,0:T(8,128)(2,1)} %bitcast.326) | data formatting | bytes 1769472
  2184.2 60.5 %copy.505 = bf16[2,3072,96]{0,2,1:T(8,128)(2,1)} copy(bf16[2,3072,96]{1,0,2:T(2,128)(2,1)S(1)} %constant_dynamic-slice_fusion.2) | data formatting | bytes 2359296
  2244.7 111.0 %reshape.599 = bf16[3072,192]{1,0:T(8,128)(2,1)} reshape(bf16[3072,96,2]{2,1,0:T(8,128)(2,1)} %bitcast.65) | data formatting | bytes 2359296
  2370.4 8.3 fusion.58
  2389.3 11.8 reshape.596
  2407.7 29.4 %reshape.594 = bf16[192,288,2]{2,1,0:T(8,128)(2,1)} reshape(bf16[192,576]{1,0:T(8,128)(2,1)} %reduce-scatter.29.cloned.1.call-done) | data formatting | bytes 442368
  2437.1 14.9 copy.500
  2453.1 41.2 %reshape.600 = bf16[768,96,2]{2,1,0:T(8,128)(2,1)} reshape(bf16[768,192]{1,0:T(8,128)(2,1)} %reduce-scatter.35.cloned.1.call-done) | data formatting | bytes 589824
  2494.3 22.0 copy.506
  (545 shorter events, 417.5 us)
Async XLA Ops:
  7.2 31.3 %all-gather.22.cloned.1.call-start = ((), (), s32[]{:S(2)}) async-start(), calls=%async_computation.11 | async-start | bytes 1474560 | tf_op jit(solution)/shard_map/all_gather | solution.py:57
  7.9 45.2 %all-gather.26.cloned.1.call-start = ((), (), s32[]{:S(2)}) async-start(), calls=%async_computation.13 | async-start | bytes 1474560 | tf_op jit(solution)/shard_map/all_gather | solution.py:58
  8.7 164.8 %all-gather.20.cloned.1.call-start = ((), (), s32[]{:S(2)}) async-start(), calls=%async_computation.10 | async-start | bytes 2654208 | tf_op jit(solution)/shard_map/all_gather | solution.py:64
  18.7 204.8 %all-gather.18.cloned.1.call-start = ((), (), s32[]{:S(2)}) async-start(), calls=%async_computation.9 | async-start | bytes 7962624 | tf_op jit(solution)/shard_map/all_gather | solution.py:63
  20.0 33.2 %copy-start.70 = (bf16[2,2,96]{2,1,0:T(2,128)(2,1)S(1)}, bf16[2,2,96]{2,1,0:T(2,128)(2,1)}, u32[]{:S(2)}) copy-start(bf16[2,2,96]{2,1,0:T(2,128)(2,1)} %param.26) | copy-start | bytes 2308
  20.0 33.2 %copy-start.77 = (bf16[2,96]{1,0:T(2,128)(2,1)S(1)}, bf16[2,96]{1,0:T(2,128)(2,1)}, u32[]{:S(2)}) copy-start(bf16[2,96]{1,0:T(2,128)(2,1)} %param.27) | copy-start | bytes 1156
  20.1 38.6 %copy-start.63 = (s32[4,4]{1,0:T(4,128)S(1)}, s32[4,4]{1,0:T(4,128)}, u32[]{:S(2)}) copy-start(s32[4,4]{1,0:T(4,128)} %param.20) | copy-start | bytes 196
  38.4 92.6 %copy-start.94 = (s32[8]{0:T(128)S(1)}, s32[8]{0:T(128)}, u32[]{:S(2)}) copy-start(s32[8]{0:T(128)} %param.19) | copy-start | bytes 100
  38.4 323.4 %all-gather.24.cloned.1.call-start = ((), (), s32[]{:S(2)}) async-start(), calls=%async_computation.12 | async-start | bytes 10616832 | tf_op jit(solution)/shard_map/all_gather | solution.py:65
  39.0 461.1 %all-gather.28.cloned.1.call-start = ((), (), s32[]{:S(2)}) async-start(), calls=%async_computation.14 | async-start | bytes 10616832 | tf_op jit(solution)/shard_map/all_gather | solution.py:66
  53.2 78.7 %copy-start.39 = (bf16[8,64,768]{2,1,0:T(8,128)(2,1)S(1)}, bf16[8,64,768]{2,1,0:T(8,128)(2,1)}, u32[]{:S(2)}) copy-start(bf16[8,64,768]{2,1,0:T(8,128)(2,1)} %param.17) | copy-start | bytes 2359300
  53.2 565.5 %reduce-scatter.25.cloned.1.call-start = ((), (), s32[]{:S(2)}) async-start(), calls=%async_computation.16 | async-start | bytes 122880 | tf_op jit(solution)/shard_map/reduce_scatter | solution.py:293
  254.5 16.1 copy-start.89
  506.9 30.8 %copy-start.38 = (bf16[512,768]{1,0:T(8,128)(2,1)}, bf16[512,768]{1,0:T(8,128)(2,1)S(1)}, u32[]{:S(2)}) copy-start(bf16[512,768]{1,0:T(8,128)(2,1)S(1)} %add_convert_fusion.1) | copy-start | bytes 2359300
  554.3 27.2 %copy-start.67 = (s32[64]{0:T(128)S(1)}, s32[64]{0:T(128)}, u32[]{:S(2)}) copy-start(s32[64]{0:T(128)} %param.21) | copy-start | bytes 772
  600.9 79.2 %reduce-scatter.23.cloned.1.call-start = ((), (), s32[]{:S(2)}) async-start(), calls=%async_computation.15 | async-start | bytes 110592 | tf_op jit(solution)/shard_map/reduce_scatter | solution.py:290
  602.0 107.9 %all-gather.34.cloned.1.call-start = ((), (), s32[]{:S(2)}) async-start(), calls=%async_computation.19 | async-start | bytes 1474560 | tf_op jit(solution)/shard_map/all_gather | solution.py:57
  621.7 180.3 %copy-start.1 = (f32[4,256,768]{2,1,0:T(8,128)}, f32[4,256,768]{2,1,0:T(8,128)S(1)}, u32[]{:S(2)}) copy-start(f32[4,256,768]{2,1,0:T(8,128)S(1)} %convert_add_fusion) | copy-start | bytes 9437188
  681.5 37.2 %all-gather.38.cloned.1.call-start = ((), (), s32[]{:S(2)}) async-start(), calls=%async_computation.21 | async-start | bytes 1474560 | tf_op jit(solution)/shard_map/all_gather | solution.py:58
  682.1 159.4 %all-gather.32.cloned.1.call-start = ((), (), s32[]{:S(2)}) async-start(), calls=%async_computation.18 | async-start | bytes 2654208 | tf_op jit(solution)/shard_map/all_gather | solution.py:64
  692.3 197.5 %all-gather.30.cloned.1.call-start = ((), (), s32[]{:S(2)}) async-start(), calls=%async_computation.17 | async-start | bytes 7962624 | tf_op jit(solution)/shard_map/all_gather | solution.py:63
  693.6 25.1 copy-start.71
  693.6 25.2 copy-start.78
  709.8 318.8 %all-gather.36.cloned.1.call-start = ((), (), s32[]{:S(2)}) async-start(), calls=%async_computation.20 | async-start | bytes 10616832 | tf_op jit(solution)/shard_map/all_gather | solution.py:65
  710.6 456.4 %all-gather.40.cloned.1.call-start = ((), (), s32[]{:S(2)}) async-start(), calls=%async_computation.22 | async-start | bytes 10616832 | tf_op jit(solution)/shard_map/all_gather | solution.py:66
  718.7 1275.6 %all-reduce.10.cloned.1.call-start = ((), (), s32[]{:S(2)}) async-start(), calls=%async_computation.30 | async-start | bytes 37748736
  762.1 41.4 %copy-start.3 = (f32[8,64,768]{2,0,1:T(8,128)S(1)}, f32[8,64,768]{2,0,1:T(8,128)}, u32[]{:S(2)}) copy-start(f32[8,64,768]{2,0,1:T(8,128)} %fusion.149) | copy-start | bytes 4718596
  920.8 16.0 copy-start.91
  1001.7 5.6 copy-start
  1167.0 7.0 copy-start.4
  1167.0 14.4 slice-start.9
  1167.0 14.4 slice-start.10
  1177.0 4.3 slice-start.11
  1177.0 12.4 slice-start.3
  1177.0 12.4 slice-start.4
  1181.4 8.1 copy-start.17
  1181.4 8.1 copy-start.43
  1181.4 8.1 copy-start.49
  1181.4 8.1 copy-start.55
  1181.4 8.1 slice-start.5
  1201.9 13.8 slice-start.6
  1206.1 9.6 slice-start.7
  1209.2 6.5 slice-start.8
  1215.8 9.7 copy-start.75
  1225.4 10.1 copy-start.99
  1284.7 9.5 copy-start.9
  1284.7 20.2 slice-start
  1294.2 10.7 slice-start.1
  1294.2 10.7 slice-start.2
  1304.9 7.3 copy-start.10
  1426.1 8.0 copy-start.48
  1426.1 8.0 copy-start.73
  1426.1 929.8 %reduce-scatter.33.cloned.1.call-start = ((), (), s32[]{:S(2)}) async-start(), calls=%async_computation.26 | async-start | bytes 10616832
  1486.1 892.6 %reduce-scatter.39.cloned.1.call-start = ((), (), s32[]{:S(2)}) async-start(), calls=%async_computation.29 | async-start | bytes 221184
  1489.8 889.8 %reduce-scatter.37.cloned.1.call-start = ((), (), s32[]{:S(2)}) async-start(), calls=%async_computation.28 | async-start | bytes 221184
  1491.3 898.0 %reduce-scatter.31.cloned.1.call-start = ((), (), s32[]{:S(2)}) async-start(), calls=%async_computation.25 | async-start | bytes 491520
  2054.3 353.4 %reduce-scatter.29.cloned.1.call-start = ((), (), s32[]{:S(2)}) async-start(), calls=%async_computation.24 | async-start | bytes 1228800
  2182.1 271.0 %reduce-scatter.35.cloned.1.call-start = ((), (), s32[]{:S(2)}) async-start(), calls=%async_computation.27 | async-start | bytes 1966080
  2355.8 6.7 copy-start.95
  2355.8 7.9 copy-start.84
  2355.8 8.5 copy-start.15
  2355.8 161.3 %reduce-scatter.27.cloned.1.call-start = ((), (), s32[]{:S(2)}) async-start(), calls=%async_computation.23 | async-start | bytes 1474560 | tf_op jit(solution)/shard_map/reduce_scatter | solution.py:360
  2364.3 6.0 copy-start.21
  2364.3 6.0 copy-start.27
  (72 other events, 155.0 us)
Sparse Core Ops, SparseCore 0:
  9.6 24.8 all-gather.21
  36.0 17.0 all-gather.25
  55.9 57.6 all-gather.19
  116.2 107.1 all-gather.17
  225.4 136.3 all-gather.23
  363.8 136.2 all-gather.27
  601.1 17.5 reduce-scatter.24
  622.5 57.5 reduce-scatter.22
  681.7 16.5 all-gather.33
  699.7 18.9 all-gather.37
  721.4 54.1 all-gather.31
  778.2 111.4 all-gather.29
  891.8 136.7 all-gather.35
  1030.7 136.2 all-gather.39
  1426.2 568.0 all-reduce.9
  1997.8 162.4 reduce-scatter.32
  2163.9 60.1 reduce-scatter.38
  2227.8 60.0 reduce-scatter.36
  2291.0 19.8 reduce-scatter.30
  2313.3 24.4 reduce-scatter.28
  2355.9 27.1 reduce-scatter.34
  2385.7 25.7 reduce-scatter.26
where the time goes:
time: 2540 us; the launch traced here: 2530 us
  waiting for transfers between devices  964 us (38%)
  local copies, waits for them, and re-layouts  942 us (37%)
  blocking collectives  271 us (11%)
  matrix products  252 us (10%)
  other arithmetic  77.9 us (3%)
    unnamed x287, local copies, waits for them, and re-layouts  644 us
    unnamed x29, waiting for transfers between devices  506 us
    all_gather x2, waiting for transfers between devices, gather_weights(): lax.all_gather(by_rows[3], 'pa', axis=2, tiled=True)  263 us
    all_gather x2, blocking collectives, gather_weights(): lax.all_gather(by_rows[5], 'pa', axis=2, tiled=True)  64.8 us
    all_gather x2, blocking collectives, gather_weights(): lax.all_gather(by_rows[4], 'pa', axis=2, tiled=True)  64.4 us
    all_gather x2, waiting for transfers between devices, gather_weights(): lax.all_gather(by_rows[0], 'pa', axis=2, tiled=True)  60.8 us
    reduce_scatter x1, waiting for transfers between devices, body(): lax.psum_scatter(q_part.astype(jnp.bfloat16), 'pa', scatter_dimension=0,...  58.5 us
  transfers between devices with their start and end apart: 22, of which 11 were waited for; matrix products, arithmetic and copies ran while one was open for 39% of the time, Pallas kernels for 0%

commit v1 on v0

v1 whole, which is shorter than its diff:
```python
import functools
import math

import jax
import jax.numpy as jnp
from jax import lax
from jax.experimental import pallas as pl
from jax.experimental.pallas import tpu as pltpu
from jax.sharding import PartitionSpec as P

HD = 64
EXTRA = 16
ROW = 256
NEG_FILL = -1000000000.0
EPSILON = 1e-06
ROOT_HALF = 0.7071067811865476
INV_ROOT_TWO_PI = 0.3989422804014327
F32 = jnp.float32
BF16 = jnp.bfloat16
MIB = 1 << 20
ANY = pl.BlockSpec(memory_space=pl.ANY)


def mm(left, right):
    return lax.dot_general(left, right, (((1,), (0,)), ((), ())), preferred_element_type=F32)


def mm_nt(left, right):
    return lax.dot_general(left, right, (((1,), (1,)), ((), ())), preferred_element_type=F32)


def mm_tn(left, right):
    return lax.dot_general(left, right, (((0,), (0,)), ((), ())), preferred_element_type=F32)


def whole(shape):
    return pl.BlockSpec(shape, lambda i: (0,) * len(shape), pipeline_mode=pl.Buffered(1))


def norm_rows(summed):
    centred = summed - jnp.mean(summed, axis=-1, keepdims=True)
    inverse = lax.rsqrt(jnp.mean(centred * centred, axis=-1, keepdims=True) + EPSILON)
    return centred * inverse, inverse


def norm_back(grad_out, gain, normed, inverse):
    scaled = grad_out * gain
    inner = (
        scaled
        - jnp.mean(scaled, axis=-1, keepdims=True)
        - normed * jnp.mean(scaled * normed, axis=-1, keepdims=True)
    )
    return inverse * inner


def col_sum(block):
    return jnp.sum(block, axis=0, keepdims=True)


def attn_fwd_kernel(dims, pack, x_ref, segc_ref, segr_ref, qkv_ref, att_ref, xhat_ref, inv_ref, wqkv_ref, wout_ref,
                    vec_ref, bup_ref, held, sem):
    npb, npa, r, wq, wo, rows_per, w1, w2 = dims
    d = x_ref.shape[1]

    @pl.when(pl.program_id(0) == 0)
    def _():
        copy = pltpu.make_async_copy(pack, held, sem)
        copy.start()
        copy.wait()
        for b in range(npb):
            rows = pl.ds(b * r, r)
            wqkv_ref[rows, :] = jnp.concatenate([held[b, a, :r, :wq] for a in range(npa)], axis=1)
            wout_ref[rows, :] = jnp.concatenate([held[b, a, :r, wq:] for a in range(npa)], axis=1)
            extra = [held[b, a, r:, :].astype(F32) for a in range(npa)]
            vec_ref[pl.ds(b * rows_per, rows_per), :] = jnp.concatenate(
                [part[:rows_per, :w1] for part in extra], axis=1)
            bup_ref[b : b + 1, :] = jnp.concatenate(
                [part[rows_per : rows_per + 1, :w2] for part in extra], axis=1)

    flat = x_ref[...]
    qkv_ref[:, :d] = ((mm(flat, wqkv_ref[:, :d]) + vec_ref[4:5, :]).astype(BF16) * BF16(HD ** -0.5))
    qkv_ref[:, d : 2 * d] = mm(flat, wqkv_ref[:, d : 2 * d]).astype(BF16)
    qkv_ref[:, 2 * d :] = (mm(flat, wqkv_ref[:, 2 * d :]) + vec_ref[5:6, :]).astype(BF16)
    blocked = jnp.where(segc_ref[0][:, 0:1] == segr_ref[0][1:2, :], 0.0, NEG_FILL)
    low_half = lax.broadcasted_iota(jnp.int32, (1, 2 * HD), 1) < HD
    keep = (low_half.astype(F32).astype(BF16), (1.0 - low_half.astype(F32)).astype(BF16))
    for p in range(d // (2 * HD)):
        lanes = slice(p * 2 * HD, (p + 1) * 2 * HD)
        q2 = qkv_ref[:, lanes]
        k2 = qkv_ref[:, d + p * 2 * HD : d + (p + 1) * 2 * HD]
        v2 = qkv_ref[:, 2 * d + p * 2 * HD : 2 * d + (p + 1) * 2 * HD]
        parts = []
        for h in range(2):
            scores = mm_nt(q2 * keep[h], k2) + blocked
            terms = jnp.exp(scores - jnp.max(scores, axis=-1, keepdims=True))
            total = jnp.sum(terms, axis=-1, keepdims=True)
            prob = (terms / total).astype(BF16)
            parts.append(mm(prob, v2))
        att_ref[:, lanes] = jnp.where(low_half, parts[0], parts[1]).astype(BF16)
    branch = mm(att_ref[...], wout_ref[...]) + vec_ref[6:7, :]
    normed, inverse = norm_rows(flat.astype(F32) + branch)
    xhat_ref[...] = normed
    inv_ref[...] = inverse


def attn_fwd(dims, pack, x, segc, segr):
    npb, npa, r, wq, wo, rows_per, w1, w2 = dims
    tokens, d = x.shape
    steps = tokens // ROW
    ff = w2 * npa * npb
    row = lambda width: pl.BlockSpec((ROW, width), lambda i: (i, 0))
    return pl.pallas_call(
        functools.partial(attn_fwd_kernel, dims),
        grid=(steps,),
        in_specs=[ANY, row(d), pl.BlockSpec((1, ROW, 2), lambda i: (i, 0, 0)),
                  pl.BlockSpec((1, 2, ROW), lambda i: (i, 0, 0))],
        out_specs=[row(3 * d), row(d), row(d), row(1), whole((d, 3 * d)), whole((d, d)), whole((8, d)),
                   whole((npb, ff // npb))],
        out_shape=[
            jax.ShapeDtypeStruct((tokens, 3 * d), BF16),
            jax.ShapeDtypeStruct((tokens, d), BF16),
            jax.ShapeDtypeStruct((tokens, d), F32),
            jax.ShapeDtypeStruct((tokens, 1), F32),
            jax.ShapeDtypeStruct((d, 3 * d), BF16),
            jax.ShapeDtypeStruct((d, d), BF16),
            jax.ShapeDtypeStruct((8, d), F32),
            jax.ShapeDtypeStruct((npb, ff // npb), F32),
        ],
        scratch_shapes=[pltpu.VMEM(pack.shape, BF16), pltpu.SemaphoreType.DMA],
        compiler_params=pltpu.CompilerParams(vmem_limit_bytes=58 * MIB),
        cost_estimate=pl.CostEstimate(flops=2 * tokens * d * (4 * d + 8 * ROW), transcendentals=0,
                                      bytes_accessed=40 * MIB),
        name="attn_fwd",
    )(pack, x, segc, segr)


def load_ffn(pack, up, down, sems):
    npb, npa, _, rows, c = pack.shape
    r = up.shape[0] // npb
    dr = up.shape[0] // npa
    dc = up.shape[1] // npb
    for b in range(npb):
        for a in range(npa):
            pltpu.make_async_copy(pack.at[b, a, 0], up.at[pl.ds(b * r, r), pl.ds(a * c, c)], sems.at[0]).start()
    for b in range(npb):
        for a in range(npa):
            for j in range(dc // c):
                pltpu.make_async_copy(
                    pack.at[b, a, 1, pl.ds(j * dr, dr), :],
                    down.at[pl.ds(a * dr, dr), pl.ds(b * dc + j * c, c)], sems.at[1]).start()
    pltpu.make_async_copy(up, up, sems.at[0]).wait()
    pltpu.make_async_copy(down, down, sems.at[1]).wait()


def ffn_fwd_kernel(spot_ref, pack, xhat_ref, vec_ref, bup_ref, act_ref, slope_ref, norm_ref, inv_ref, enc_ref, cls_ref,
                   up, down, held, sems):
    step = pl.program_id(0)

    @pl.when(step == 0)
    def _():
        load_ffn(pack, up, down, sems)

    ff = up.shape[1]
    tiles = bup_ref.shape[0]
    width = ff // tiles
    first_norm = xhat_ref[...] * vec_ref[0:1, :] + vec_ref[1:2, :]
    first_low = first_norm.astype(BF16)
    total = first_norm + vec_ref[7:8, :]
    for t in range(tiles):
        cols = slice(t * width, (t + 1) * width)
        hidden = mm(first_low, up[:, cols]) + bup_ref[t : t + 1, :]
        cdf = 0.5 + 0.5 * lax.erf(hidden * ROOT_HALF)
        act = (hidden * cdf).astype(BF16)
        act_ref[:, cols] = act
        slope_ref[:, cols] = (cdf + hidden * (jnp.exp(-0.5 * hidden * hidden) * INV_ROOT_TWO_PI)).astype(BF16)
        total = total + mm_nt(act, down[:, cols])
    normed, inverse = norm_rows(total)
    norm_ref[...] = normed
    inv_ref[...] = inverse
    enc = (normed * vec_ref[2:3, :] + vec_ref[3:4, :]).astype(BF16)
    enc_ref[...] = enc
    held[...] = enc.astype(F32)
    for j in range(cls_ref.shape[1]):
        cls_ref[0, j : j + 1, :] = held[pl.ds(spot_ref[step, j], 1), :]


def ffn_fwd(spots, pack, xhat, vec, bup):
    tokens, d = xhat.shape
    steps, per_row = spots.shape
    ff = bup.shape[0] * bup.shape[1]
    row = lambda width: pl.BlockSpec((ROW, width), lambda i: (i, 0))
    return pl.pallas_call(
        ffn_fwd_kernel,
        grid=(steps,),
        in_specs=[pl.BlockSpec(memory_space=pltpu.SMEM), ANY, row(d), whole(vec.shape), whole(bup.shape)],
        out_specs=[row(ff), row(ff), row(d), row(1), row(d), pl.BlockSpec((1, per_row, d), lambda i: (i, 0, 0))],
        out_shape=[
            jax.ShapeDtypeStruct((tokens, ff), BF16),
            jax.ShapeDtypeStruct((tokens, ff), BF16),
            jax.ShapeDtypeStruct((tokens, d), F32),
            jax.ShapeDtypeStruct((tokens, 1), F32),
            jax.ShapeDtypeStruct((tokens, d), BF16),
            jax.ShapeDtypeStruct((steps, per_row, d), F32),
        ],
        scratch_shapes=[pltpu.VMEM((d, ff), BF16), pltpu.VMEM((d, ff), BF16), pltpu.VMEM((ROW, d), F32),
                        pltpu.SemaphoreType.DMA((2,))],
        compiler_params=pltpu.CompilerParams(vmem_limit_bytes=58 * MIB),
        cost_estimate=pl.CostEstimate(flops=4 * tokens * d * ff, transcendentals=0, bytes_accessed=40 * MIB),
        name="ffn_fwd",
    )(spots, pack, xhat, vec, bup)


def loss_kernel(scale, q_all, p_all, q_own, p_own, hit_all, hit_own, loss_ref, gq_ref, gp_ref):
    def split_mm(dot, left, right):
        high = left.astype(BF16)
        rest = left - high.astype(F32)
        mid = rest.astype(BF16)
        tail = (rest - mid.astype(F32)).astype(BF16)
        return dot(high, right) + dot(mid, right) + dot(tail, right)

    def log_norm(scores):
        peak = jnp.max(scores, axis=1, keepdims=True)
        return peak + jnp.log(jnp.sum(jnp.exp(scores - peak), axis=1, keepdims=True))

    full = mm_nt(q_all[...], p_all[...]) * scale
    norm_all = log_norm(full)
    own_rows = mm_nt(q_own[...], p_all[...]) * scale
    norm_own = log_norm(own_rows)
    hits = lax.broadcasted_iota(jnp.int32, own_rows.shape, 1) == hit_own[...]
    loss_ref[...] = norm_own - jnp.sum(jnp.where(hits, own_rows, 0.0), axis=1, keepdims=True)
    tile = jnp.exp(own_rows - norm_own) - jnp.where(hits, 1.0, 0.0)
    gq_ref[...] = split_mm(mm, tile, p_all[...]) * scale
    own_cols = mm_nt(q_all[...], p_own[...]) * scale
    hits = lax.broadcasted_iota(jnp.int32, own_cols.shape, 1) == hit_all[...]
    tile = jnp.exp(own_cols - norm_all) - jnp.where(hits, 1.0, 0.0)
    gp_ref[...] = split_mm(mm_tn, tile, q_all[...]) * scale


def loss_part(q_all, p_all, q_own, p_own, hit_all, hit_own):
    d = q_all.shape[1]
    return pl.pallas_call(
        functools.partial(loss_kernel, 3.0 / math.sqrt(d)),
        out_shape=[
            jax.ShapeDtypeStruct((q_own.shape[0], 1), F32),
            jax.ShapeDtypeStruct(q_own.shape, F32),
            jax.ShapeDtypeStruct(p_own.shape, F32),
        ],
        compiler_params=pltpu.CompilerParams(vmem_limit_bytes=58 * MIB),
        name="loss_part",
    )(q_all, p_all, q_own, p_own, hit_all, hit_own)


def ffn_bwd_kernel(steps, spot_ref, pack, cot_ref, gcls_ref, norm_ref, inv2_ref, act_ref, slope_ref, xhat_ref, inv1_ref,
                   vec_ref, dh_ref, dup_ref, ddown_ref, gvec_ref, gbup_ref,
                   up, down, held, first_t, down_t, hidden_all, act_all, sems):
    step = pl.program_id(0)
    tiles = gbup_ref.shape[0]
    ff = up.shape[1]
    width = ff // tiles

    @pl.when(step == 0)
    def _():
        load_ffn(pack, up, down, sems)
        gvec_ref[...] = jnp.zeros_like(gvec_ref)
        gbup_ref[...] = jnp.zeros_like(gbup_ref)

    @pl.when(step < steps)
    def _():
        held[...] = cot_ref[...].astype(F32)
        for j in range(gcls_ref.shape[1]):
            spot = pl.ds(spot_ref[step, j], 1)
            held[spot, :] = held[spot, :] + gcls_ref[0, j : j + 1, :]
        grad_out = held[...]
        normed = norm_ref[...]
        gvec_ref[2:3, :] += col_sum(grad_out * normed)
        gvec_ref[3:4, :] += col_sum(grad_out)
        grad_two = norm_back(grad_out, vec_ref[2:3, :], normed, inv2_ref[...])
        down_low = grad_two.astype(BF16)
        gvec_ref[7:8, :] += col_sum(down_low.astype(F32))
        tok = pl.ds(pl.multiple_of(step * ROW, ROW), ROW)
        total = grad_two
        for t in range(tiles):
            cols = slice(t * width, (t + 1) * width)
            hidden = (mm(down_low, down[:, cols]) * slope_ref[:, cols].astype(F32)).astype(BF16)
            hidden_all[tok, cols] = hidden
            gbup_ref[t : t + 1, :] += col_sum(hidden.astype(F32))
            total = total + mm_nt(hidden, up[:, cols])
        act_all[tok, :] = act_ref[...]
        xhat = xhat_ref[...]
        gvec_ref[0:1, :] += col_sum(total * xhat)
        gvec_ref[1:2, :] += col_sum(total)
        dh_ref[...] = norm_back(total, vec_ref[0:1, :], xhat, inv1_ref[...])
        first_low = (xhat * vec_ref[0:1, :] + vec_ref[1:2, :]).astype(BF16)
        for s in range(steps):
            @pl.when(step == s)
            def _():
                first_t[:, s * ROW : (s + 1) * ROW] = first_low.T
                down_t[:, s * ROW : (s + 1) * ROW] = down_low.T

    npb, npa, r, c = (dup_ref.shape[0], ddown_ref.shape[1], dup_ref.shape[2], dup_ref.shape[3])
    rows = ddown_ref.shape[2]
    d = up.shape[0]
    dr = d // npa
    part = ff // npb

    for b in range(npb):
        @pl.when(step == steps + b)
        def _():
            cols = slice(b * part, (b + 1) * part)
            got = mm(first_t[...], hidden_all[:, cols]).astype(BF16)
            for j in range(part // c):
                for e in range(npb):
                    dup_ref[e, j] = got[e * r : (e + 1) * r, j * c : (j + 1) * c]
            got = mm(down_t[...], act_all[:, cols]).astype(BF16)
            for j in range(part // c):
                for a in range(npa):
                    ddown_ref[0, a, j * dr : (j + 1) * dr, :] = got[a * dr : (a + 1) * dr, j * c : (j + 1) * c]


def ffn_bwd(spots, pack, cot, gcls, norm2, inv2, act, slope, xhat, inv1, vec, bup_shape):
    tokens, d = xhat.shape
    steps, per_row = spots.shape
    npb, npa, _, rows, c = pack.shape
    ff = act.shape[1]
    last = lambda i: jnp.minimum(i, steps - 1)
    row = lambda width: pl.BlockSpec((ROW, width), lambda i: (last(i), 0))
    after = lambda i: jnp.maximum(i - steps, 0)
    return pl.pallas_call(
        functools.partial(ffn_bwd_kernel, steps),
        grid=(steps + npb,),
        in_specs=[pl.BlockSpec(memory_space=pltpu.SMEM), ANY, row(d),
                  pl.BlockSpec((1, per_row, d), lambda i: (last(i), 0, 0)), row(d), row(1), row(ff), row(ff), row(d), row(1),
                  whole(vec.shape)],
        out_specs=[row(d), pl.BlockSpec((npb, npa // npb, rows, c), lambda i: (0, after(i), 0, 0)),
                   pl.BlockSpec((1, npa, rows, c), lambda i: (after(i), 0, 0, 0)), whole(vec.shape), whole(bup_shape)],
        out_shape=[
            jax.ShapeDtypeStruct((tokens, d), F32),
            jax.ShapeDtypeStruct((npb, npa, rows, c), BF16),
            jax.ShapeDtypeStruct((npb, npa, rows, c), BF16),
            jax.ShapeDtypeStruct(vec.shape, F32),
            jax.ShapeDtypeStruct(bup_shape, F32),
        ],
        scratch_shapes=[pltpu.VMEM((d, ff), BF16), pltpu.VMEM((d, ff), BF16), pltpu.VMEM((ROW, d), F32),
                        pltpu.VMEM((d, tokens), BF16), pltpu.VMEM((d, tokens), BF16), pltpu.VMEM((tokens, ff), BF16),
                        pltpu.VMEM((tokens, ff), BF16), pltpu.SemaphoreType.DMA((2,))],
        compiler_params=pltpu.CompilerParams(vmem_limit_bytes=60 * MIB),
        cost_estimate=pl.CostEstimate(flops=8 * tokens * d * ff, transcendentals=0, bytes_accessed=60 * MIB),
        name="ffn_bwd",
    )(spots, pack, cot, gcls, norm2, inv2, act, slope, xhat, inv1, vec)


def attn_bwd_kernel(dims, steps, dh_ref, qkv_ref, att_ref, x_ref, segc_ref, segr_ref, wqkv_ref, wout_ref, gvec_in, gbup_in,
                    gx_ref, dpack_ref, x_t, att_t, proj, branch, gvec):
    npb, npa, r, wq, wo, rows_per, w1, w2 = dims
    step = pl.program_id(0)
    d = x_ref.shape[1]

    @pl.when(step == 0)
    def _():
        gvec[...] = gvec_in[...]

    @pl.when(step < steps)
    def _():
        dh = dh_ref[...]
        low = dh.astype(BF16)
        tok = pl.ds(pl.multiple_of(step * ROW, ROW), ROW)
        branch[tok, :] = low
        gvec[6:7, :] += col_sum(low.astype(F32))
        att_grad = mm_nt(low, wout_ref[...]).astype(BF16)
        blocked = jnp.where(segc_ref[0][:, 1:2] == segr_ref[0][0:1, :], 0.0, NEG_FILL)
        low_half = lax.broadcasted_iota(jnp.int32, (1, 2 * HD), 1) < HD
        keep = (low_half.astype(F32).astype(BF16), (1.0 - low_half.astype(F32)).astype(BF16))
        for p in range(d // (2 * HD)):
            lanes = slice(p * 2 * HD, (p + 1) * 2 * HD)
            k_lanes = slice(d + p * 2 * HD, d + (p + 1) * 2 * HD)
            v_lanes = slice(2 * d + p * 2 * HD, 2 * d + (p + 1) * 2 * HD)
            q2 = qkv_ref[:, lanes]
            k2 = qkv_ref[:, k_lanes]
            v2 = qkv_ref[:, v_lanes]
            g2 = att_grad[:, lanes]
            dq, dk, dv = [], [], []
            for h in range(2):
                scores = mm_nt(k2 * keep[h], q2) + blocked
                terms = jnp.exp(scores - jnp.max(scores, axis=0, keepdims=True))
                prob = terms / jnp.sum(terms, axis=0, keepdims=True)
                weighed = prob * mm_nt(v2 * keep[h], g2)
                sgrad = (weighed - prob * jnp.sum(weighed, axis=0, keepdims=True)).astype(BF16)
                dv.append(mm(prob.astype(BF16), g2))
                dk.append(mm(sgrad, q2))
                dq.append(mm_tn(sgrad, k2))
            proj[tok, lanes] = (jnp.where(low_half, dq[0], dq[1]) * (HD ** -0.5)).astype(BF16)
            proj[tok, k_lanes] = jnp.where(low_half, dk[0], dk[1]).astype(BF16)
            proj[tok, v_lanes] = jnp.where(low_half, dv[0], dv[1]).astype(BF16)
        gvec[4:5, :] += col_sum(proj[tok, :d].astype(F32))
        gvec[5:6, :] += col_sum(proj[tok, 2 * d :].astype(F32))
        gx_ref[...] = mm_nt(proj[tok, :], wqkv_ref[...]) + dh
        for s in range(steps):
            @pl.when(step == s)
            def _():
                x_t[:, s * ROW : (s + 1) * ROW] = x_ref[...].T
                att_t[:, s * ROW : (s + 1) * ROW] = att_ref[...].T

    @pl.when(step == steps)
    def _():
        wide = jnp.concatenate([mm(x_t[...], proj[:, g * d : (g + 1) * d]).astype(BF16) for g in range(3)], axis=1)
        out = mm(att_t[...], branch[...]).astype(BF16)
        for a in range(npa):
            block = jnp.concatenate([wide[:, a * wq : (a + 1) * wq], out[:, a * wo : (a + 1) * wo]], axis=1)
            for b in range(npb):
                dpack_ref[b, a, :r, :] = block[b * r : (b + 1) * r, :]
        c = wq + wo

        def widen(piece):
            if piece.shape[1] == c:
                return piece
            return jnp.concatenate([piece, jnp.zeros((piece.shape[0], c - piece.shape[1]), F32)], axis=1)

        for b in range(npb):
            for a in range(npa):
                rows = [widen(gvec[b * rows_per : (b + 1) * rows_per, a * w1 : (a + 1) * w1]),
                        widen(gbup_in[b : b + 1, a * w2 : (a + 1) * w2]),
                        jnp.zeros((EXTRA - 1 - rows_per, c), F32)]
                dpack_ref[b, a, r:, :] = jnp.concatenate(rows, axis=0).astype(BF16)


def attn_bwd(dims, dh, qkv, att, x, segc, segr, wqkv, wout, gvec, gbup):
    npb, npa, r, wq, wo, rows_per, w1, w2 = dims
    tokens, d = x.shape
    steps = tokens // ROW
    last = lambda i: jnp.minimum(i, steps - 1)
    row = lambda width: pl.BlockSpec((ROW, width), lambda i: (last(i), 0))
    return pl.pallas_call(
        functools.partial(attn_bwd_kernel, dims, steps),
        grid=(steps + 1,),
        in_specs=[row(d), row(3 * d), row(d), row(d), pl.BlockSpec((1, ROW, 2), lambda i: (last(i), 0, 0)),
                  pl.BlockSpec((1, 2, ROW), lambda i: (last(i), 0, 0)), whole(wqkv.shape), whole(wout.shape),
                  whole(gvec.shape), whole(gbup.shape)],
        out_specs=[row(d), whole((npb, npa, r + EXTRA, wq + wo))],
        out_shape=[
            jax.ShapeDtypeStruct((tokens, d), F32),
            jax.ShapeDtypeStruct((npb, npa, r + EXTRA, wq + wo), BF16),
        ],
        scratch_shapes=[pltpu.VMEM((d, tokens), BF16), pltpu.VMEM((d, tokens), BF16), pltpu.VMEM((tokens, 3 * d), BF16),
                        pltpu.VMEM((tokens, d), BF16), pltpu.VMEM(gvec.shape, F32)],
        compiler_params=pltpu.CompilerParams(vmem_limit_bytes=60 * MIB),
        cost_estimate=pl.CostEstimate(flops=4 * tokens * d * (4 * d + 10 * ROW), transcendentals=0,
                                      bytes_accessed=40 * MIB),
        name="attn_bwd",
    )(dh, qkv, att, x, segc, segr, wqkv, wout, gvec, gbup)


class Blocks:
    def __init__(self, npb, npa, d, ff):
        self.npb, self.npa, self.d, self.ff = npb, npa, d, ff
        self.r, self.wq, self.wo, self.c = d // npb, 3 * d // npa, d // npa, ff // npa
        self.dr, self.dc = d // npa, ff // npb
        self.rows_per, self.w1, self.w2 = 8 // npb, d // npa, ff // (npa * npb)
        self.direct = self.c % 128 == 0 and self.r % 16 == 0 and self.dr % 16 == 0
        if self.direct:
            self.dims = (npb, npa, self.r, self.wq, self.wo, self.rows_per, self.w1, self.w2)
        else:
            self.dims = (1, 1, d, 3 * d, d, 8, d, ff)

    def pack(self, w_qkv, w_out, w_up, w_down, norm_bias, bias_up):
        c = self.wq + self.wo
        vec = jnp.pad(norm_bias, ((0, 0), (0, 0), (0, c - self.w1)))
        bup = jnp.pad(bias_up[:, None, :], ((0, 0), (0, EXTRA - 1 - self.rows_per), (0, c - self.w2)))
        attn = jnp.concatenate([jnp.concatenate([w_qkv, w_out], axis=2), vec, bup], axis=1)
        down_t = jnp.swapaxes(w_down, 1, 2)
        down = jnp.concatenate([down_t[:, :, j : j + self.c] for j in range(0, self.dc, self.c)], axis=1)
        return attn, jnp.stack([w_up, down], axis=1)

    def from_blocks(self, attn, ffn):
        if self.direct:
            return attn, ffn
        d, ff, r = self.d, self.ff, self.r
        rows = lambda part, height: part.transpose(0, 2, 1, 3).reshape(height, -1)
        qkv = rows(attn[:, :, :r, : self.wq], d)
        out = rows(attn[:, :, :r, self.wq :], d)
        vec = rows(attn[:, :, r : r + self.rows_per, : self.w1], 8)
        bup = attn[:, :, r + self.rows_per, : self.w2].reshape(1, ff)
        vec = jnp.pad(vec, ((0, 0), (0, 3 * d)))
        bup = jnp.pad(bup, ((0, EXTRA - 9), (0, 4 * d - ff)))
        wide = jnp.concatenate([jnp.concatenate([qkv, out], axis=1), vec, bup], axis=0)
        up = rows(ffn[:, :, 0], d)
        pieces = self.dc // self.c
        down = ffn[:, :, 1].reshape(self.npb, self.npa, pieces, self.dr, self.c)
        down = down.transpose(1, 3, 0, 2, 4).reshape(d, ff)
        return wide[None, None], jnp.stack([up, down])[None, None]

    def to_blocks(self, attn, up, down):
        if self.direct:
            return attn, up, down
        d, ff, npb, npa = self.d, self.ff, self.npb, self.npa
        blocks = lambda part, height: part.reshape(npb, height, npa, -1).transpose(0, 2, 1, 3)
        wide = attn[0, 0]
        c = self.wq + self.wo
        main = jnp.concatenate([blocks(wide[:d, : 3 * d], self.r), blocks(wide[:d, 3 * d :], self.r)], axis=3)
        vec = blocks(wide[d : d + 8, :d], self.rows_per)
        vec = jnp.pad(vec, ((0, 0), (0, 0), (0, 0), (0, c - self.w1)))
        bup = wide[d + 8, :ff].reshape(npb, npa, 1, self.w2)
        bup = jnp.pad(bup, ((0, 0), (0, 0), (0, EXTRA - 1 - self.rows_per), (0, c - self.w2)))
        pieces = self.dc // self.c
        down = down[0, 0].reshape(npa, self.dr, npb, pieces, self.c).transpose(2, 0, 3, 1, 4)
        down = down.reshape(npb, npa, pieces * self.dr, self.c)
        return jnp.concatenate([main, vec, bup], axis=2), blocks(up[0, 0], self.r), down

    def unpack(self, attn, up, down):
        r = self.r
        down = jnp.concatenate([down[:, j * self.dr : (j + 1) * self.dr] for j in range(self.dc // self.c)], axis=2)
        return (attn[:, :r, : self.wq], attn[:, :r, self.wq :], up, jnp.swapaxes(down, 1, 2),
                attn[:, r : r + self.rows_per, : self.w1], attn[:, r + self.rows_per, : self.w2])


BOTH = ("pb", "pa")


def body(questions, passages, cot_questions, cot_passages, question_lengths, segment_lengths, positives, w_qkv, w_out, w_up,
         w_down, norm_bias, bias_up):
    q_count, q_len, d = questions.shape
    row_count, row_len, _ = passages.shape
    segs = segment_lengths.shape[1]
    npb, npa = lax.axis_size("pb"), lax.axis_size("pa")
    size = Blocks(npb, npa, d, bias_up.shape[1] * npb * npa)
    dims = size.dims
    device = lax.axis_index("pb") * npa + lax.axis_index("pa")

    attn_pack, ffn_pack = size.pack(w_qkv, w_out, w_up, w_down, norm_bias, bias_up)
    attn_all = lax.all_gather(attn_pack, BOTH, axis=0).reshape((npb, npa) + attn_pack.shape)
    ffn_all = lax.all_gather(ffn_pack, BOTH, axis=0).reshape((npb, npa) + ffn_pack.shape)
    attn_w, ffn_w = zip(*[size.from_blocks(attn_all[:, :, e], ffn_all[:, :, e]) for e in range(2)])

    per_row = ROW // q_len
    q_rows = q_count // per_row
    token = jnp.arange(ROW, dtype=jnp.int32)
    q_seg = jnp.broadcast_to(token // q_len, (q_rows, ROW))
    q_valid = (token % q_len)[None, :] < jnp.repeat(question_lengths.reshape(q_rows, per_row), q_len, axis=1)
    starts = jnp.cumsum(segment_lengths, axis=1) - segment_lengths
    p_seg = jnp.sum((token[None, None, :] >= starts[:, :, None]).astype(jnp.int32), axis=1)
    seg_pairs = (jnp.stack([q_seg, jnp.where(q_valid, q_seg, -1)], axis=1), jnp.stack([p_seg, p_seg], axis=1))
    segr = seg_pairs
    segc = tuple(jnp.swapaxes(pair, 1, 2) for pair in seg_pairs)
    spots = (jnp.broadcast_to(jnp.arange(per_row, dtype=jnp.int32) * q_len, (q_rows, per_row)), starts)
    xs = (questions.reshape(-1, d), passages.reshape(-1, d))
    cots = (cot_questions.reshape(-1, d), cot_passages.reshape(-1, d))

    half = [attn_fwd(dims, attn_w[e], xs[e], segc[e], segr[e]) for e in range(2)]
    done = [ffn_fwd(spots[e], ffn_w[e], half[e][2], half[e][6], half[e][7]) for e in range(2)]
    q_own = done[0][5].reshape(q_count, d).astype(BF16)
    p_own = done[1][5].reshape(row_count * segs, d).astype(BF16)

    heads = lax.all_gather(jnp.concatenate([q_own, p_own]), BOTH, axis=0)
    q_all = heads[:, :q_count].reshape(-1, d)
    p_all = heads[:, q_count:].reshape(-1, d)
    hit_all = lax.all_gather(positives, "pb", axis=0, tiled=True)[:, None]
    hit_own = lax.dynamic_slice_in_dim(hit_all, device * q_count, q_count)
    losses, gq, gp = loss_part(q_all, p_all, q_own, p_own, hit_all - device * (row_count * segs), hit_own)
    gcls = (gq.reshape(q_rows, per_row, d), gp.reshape(row_count, segs, d))

    grads = []
    for e in range(2):
        qkv, att, xhat, inv1, wqkv, wout, vec, bup = half[e]
        act, slope, norm2, inv2, _, _ = done[e]
        dh, dup, ddown, gvec, gbup = ffn_bwd(spots[e], ffn_w[e], cots[e], gcls[e], norm2, inv2, act, slope, xhat, inv1, vec,
                                             bup.shape)
        gx, dattn = attn_bwd(dims, dh, qkv, att, xs[e], segc[e], segr[e], wqkv, wout, gvec, gbup)
        grads.append((gx, size.to_blocks(dattn, dup, ddown)))

    def scatter(index):
        both = jnp.stack([grads[e][1][index] for e in range(2)], axis=2)
        flat = both.reshape((npb * npa,) + both.shape[2:])
        return lax.psum_scatter(flat, BOTH, scatter_dimension=0, tiled=False).astype(F32)

    outs = size.unpack(scatter(0), scatter(1), scatter(2))
    return (
        done[0][4].reshape(questions.shape),
        done[1][4].reshape(passages.shape),
        losses[:, 0],
        grads[0][0].reshape(questions.shape),
        grads[1][0].reshape(passages.shape),
    ) + outs


def solution(mesh):
    rows = P(BOTH, None, None)
    shard = P(None, "pb", "pa")
    vector = P(None, BOTH)
    in_specs = (rows, rows, rows, rows, P(BOTH), P(BOTH, None), P("pb"), shard, shard, shard, shard, shard, vector)
    out_specs = (rows, rows, P(BOTH), rows, rows, shard, shard, shard, shard, shard, vector)
    return jax.shard_map(body, mesh=mesh, in_specs=in_specs, out_specs=out_specs, check_vma=False)
```

time: 2540 us -> 847 us (0.33)
  local copies, waits for them, and re-layouts: 942 us -> 41.1 us
  waiting for transfers between devices: 964 us -> 540 us
  blocking collectives: 271 us -> 4.89 us
  matrix products: 252 us -> 0 us
  Pallas kernels: 0 us -> 197 us
  other arithmetic: 77.9 us -> 40.2 us
    unnamed x287 -> x15, local copies, waits for them, and re-layouts: 644 us -> 2.16 us
    unnamed x29 -> x6, waiting for transfers between devices: 506 us -> 0.1 us
    reduce_scatter x3, waiting for transfers between devices: 75.1 us -> 333 us  [scatter(): lax.psum_scatter(flat, BOTH, scatter_dimension=0, tiled=False).astype(F32)]
    dot_general x51 -> x0, matrix products: 252 us -> none  [the longest x4 39 us: forward_layer(): jnp.dot(gelu_low, w_down, preferred_element_type=jnp.float32) + vec_rows[7]]
    all_gather x14 -> x0, blocking collectives: 227 us -> none  [the longest x2 64.8 us: gather_weights(): lax.all_gather(by_rows[5], 'pa', axis=2, tiled=True)]
    pallas_call x0 -> x9, Pallas kernels: none -> 197 us  [the longest x2 64.1 us: attn_bwd(): pl.pallas_call(functools.partial(attn_bwd_kernel, dims, steps), grid=(ste...]
    all_gather x12 -> x3, waiting for transfers between devices: 382 us -> 206 us  [the longest x1 81.4 us: body(): lax.all_gather(attn_pack, BOTH, axis=0)]
    slice x16 -> x7, local copies, waits for them, and re-layouts: 133 us -> 5.94 us  [the longest x1 2.09 us: body(): p_all = heads[:, q_count:].reshape(-1, d)]
  transfers between devices with their start and end apart: 22 -> 6, of which waited for: 11 -> 6; matrix products, arithmetic and copies ran while one was open for 39% -> 5% of each run, Pallas kernels for 0% -> 12%
where the time goes in v1:
time: 847 us; the launch traced here: 839 us
  waiting for transfers between devices  540 us (64%)
  Pallas kernels  197 us (23%)
  local copies, waits for them, and re-layouts  41.1 us (5%)
  other arithmetic  40.2 us (5%)
  between operations  15.4 us (2%)
    reduce_scatter x3, waiting for transfers between devices, scatter(): lax.psum_scatter(flat, BOTH, scatter_dimension=0, tiled=False).astype(F32)  333 us
    all_gather x1, waiting for transfers between devices, body(): lax.all_gather(attn_pack, BOTH, axis=0)  81.4 us
    all_gather x1, waiting for transfers between devices, body(): lax.all_gather(ffn_pack, BOTH, axis=0).reshape((npb, npa) + ffn_pack.shape)  80.6 us
    pallas_call x2, Pallas kernels, attn_bwd(): pl.pallas_call(functools.partial(attn_bwd_kernel, dims, steps), grid=(ste...  64.1 us
    pallas_call x2, Pallas kernels, ffn_bwd(): pl.pallas_call(functools.partial(ffn_bwd_kernel, steps), grid=(steps + np...  57.5 us
    all_gather x1, waiting for transfers between devices, body(): heads = lax.all_gather(jnp.concatenate([q_own, p_own]), BOTH, axis=0)  44.5 us
    pallas_call x2, Pallas kernels, attn_fwd(): pl.pallas_call(functools.partial(attn_fwd_kernel, dims), grid=(steps,), i...  37.3 us
    pallas_call x2, Pallas kernels, ffn_fwd(): pl.pallas_call(ffn_fwd_kernel, grid=(steps,), in_specs=[pl.BlockSpec(memo...  34.5 us
  transfers between devices with their start and end apart: 6, of which 6 were waited for; matrix products, arithmetic and copies ran while one was open for 5% of the time, Pallas kernels for 12%

profile of v1, /device:TPU:0, one launch (start us, length us, event | category | flops | bytes accessed | tf_op | source)
XLA Modules:
  0.0 838.6 jit_solution(9318028891815348889)
XLA Ops:
  7.2 0.0 all-gather.9.cloned.1.call-start
  7.2 0.7 copy.116
  7.9 1.8 fusion.4
  9.8 0.0 all-gather.7.cloned.1.call-start
  9.8 1.0 fusion.10
  10.9 1.8 pad_maximum_fusion.3
  12.7 0.0 all-gather.11.cloned.1.call-start
  12.8 0.7 reshape.157
  13.5 0.9 reduce_window_sum.11
  14.4 0.7 sub.20.spot_ref
  15.1 0.1 broadcast_in_dim.22
  15.1 0.1 reshape.158
  15.2 0.1 convert_reduce_fusion
  15.4 0.6 pad_add_fusion.1
  16.0 0.9 copy.98.segc_ref
  16.8 0.6 pad_add_fusion
  17.4 1.0 copy.101.segc_ref
  18.5 81.4 %all-gather.9.cloned.1.call-done = bf16[64,208,384]{2,1,0:T(8,128)(2,1)} async-done(((bf16[2,208,384]{2,1,0:T(8,128)(2,1)}), bf16[64,208,384]{2,1,0:T(8,128)(2,1)}) %all-gather.9.cloned.1.call-update) | async-done | bytes 10223632 | tf_op jit(solution)/shard_map/all_gather | solution.py:529
  99.9 8.9 %slice_bitcast_fusion.2 = (bf16[4,8,208,384]{3,2,1,0:T(8,128)(2,1)}, bf16[4,8,208,384]{3,2,1,0:T(8,128)(2,1)}) fusion(bf16[4,8,2,208,384]{4,3,2,1,0:T(8,128)(2,1)} %bitcast.74), kind=kLoop, calls=%fused_computation.5 | loop fusion | bytes 20447232 | tf_op jit(solution)/shard_map/squeeze | solution.py:531
  108.8 15.2 %attn_fwd.2 = (bf16[512,2304]{1,0:T(8,128)(2,1)}, bf16[512,768]{1,0:T(8,128)(2,1)}, f32[512,768]{1,0:T(8,128)}, f32[512,1]{1,0:T(8,128)}, bf16[768,2304]{1,0:T(8...) custom-call(bf16[4,8,208,384]{3,2,1,0:T(8,128)(2,1)} %get-tuple-element.137.pack, ...), custom_call_target="tpu_custom_call" | custom-call | flops 4026531840 | bytes 41943040 | tf_op jit(solution)/shard_map/attn_fwd/pallas_call | solution.py:112
  124.0 22.1 %attn_fwd.3 = (bf16[1024,2304]{1,0:T(8,128)(2,1)}, bf16[1024,768]{1,0:T(8,128)(2,1)}, f32[1024,768]{1,0:T(8,128)}, f32[1024,1]{1,0:T(8,128)}, bf16[768,2304]{1,0...) custom-call(bf16[4,8,208,384]{3,2,1,0:T(8,128)(2,1)} %get-tuple-element.136.pack, ...), custom_call_target="tpu_custom_call" | custom-call | flops 8053063680 | bytes 41943040 | tf_op jit(solution)/shard_map/attn_fwd/pallas_call | solution.py:112
  146.1 80.6 %all-gather.7.cloned.1.call-done = bf16[64,2,192,384]{3,2,1,0:T(8,128)(2,1)} async-done(((bf16[2,2,192,384]{3,2,1,0:T(8,128)(2,1)}), bf16[64,2,192,384]{3,2,1,0:T(8,128)(2,1)}) %all-gather.7.cloned.1.call-update) | async-done | bytes 18874384 | tf_op jit(solution)/shard_map/all_gather | solution.py:530
  226.7 14.6 %slice_bitcast_fusion = (bf16[4,8,2,192,384]{4,3,2,1,0:T(8,128)(2,1)}, bf16[4,8,2,192,384]{4,3,2,1,0:T(8,128)(2,1)}) fusion(bf16[4,8,2,2,192,384]{5,4,3,2,1,0:T(8,128)(2,1)} %bitcast.73), kind=kLoop, calls=%fused_computation.1 | loop fusion | bytes 37748736 | tf_op jit(solution)/shard_map/squeeze | solution.py:531
  241.2 0.6 broadcast_in_dim.20.spot_ref
  241.8 13.7 %ffn_fwd.2 = (bf16[512,3072]{1,0:T(8,128)(2,1)}, bf16[512,3072]{1,0:T(8,128)(2,1)}, f32[512,768]{1,0:T(8,128)}, f32[512,1]{1,0:T(8,128)}, bf16[512,768]{1,0:T(8,128)(2,1)}, /*index=5*/f32[2,4,768]{2,1,0:T(4,128)}) custom-call(s32[2,4]{1,0:T(2,128)} %broadcast_in_dim.20.spot_ref, bf16[4,8,2,192,384]{4,3,2,1,0:T(8,128)(2,1)} %get-tuple-element.135.pack, ...), custom_call_target="tpu_custom_call" | custom-call | flops 4831838208 | bytes 41943040 | tf_op jit(solution)/shard_map/ffn_fwd/pallas_call | solution.py:192
  255.5 0.7 convert_element_type.36
  256.3 20.8 %ffn_fwd.3 = (bf16[1024,3072]{1,0:T(8,128)(2,1)}, bf16[1024,3072]{1,0:T(8,128)(2,1)}, f32[1024,768]{1,0:T(8,128)}, f32[1024,1]{1,0:T(8,128)}, bf16[1024,768]{1,0:T(8,128)(2,1)}, /*index=5*/f32[4,4,768]{2,1,0:T(4,128)}) custom-call(s32[4,4]{1,0:T(4,128)} %copy-done.2, bf16[4,8,2,192,384]{4,3,2,1,0:T(8,128)(2,1)} %get-tuple-element.134.pack, ...), custom_call_target="tpu_custom_call" | custom-call | flops 9663676416 | bytes 41943040 | tf_op jit(solution)/shard_map/ffn_fwd/pallas_call | solution.py:192
  277.1 0.8 convert_element_type.38
  278.0 0.6 pad_maximum_fusion.4
  278.6 0.0 reduce-scatter.8.cloned.1.call-start
  278.7 0.6 dynamic-slice.4
  279.9 0.2 dynamic-update-slice
  280.2 4.9 all-reduce.2
  285.1 0.1 dynamic-slice_bitcast_fusion
  285.1 0.7 copy.103.hit_own
  285.8 0.8 copy.102.hit_all
  286.6 44.5 %all-gather.11.cloned.1.call-done = bf16[768,768]{1,0:T(8,128)(2,1)} async-done(((bf16[24,768]{1,0:T(8,128)(2,1)}), bf16[768,768]{1,0:T(8,128)(2,1)}) %all-gather.11.cloned.1.call-update) | async-done | bytes 1179664 | tf_op jit(solution)/shard_map/all_gather | solution.py:552
  331.1 1.8 slice_bitcast_fusion.4.q_all
  332.9 2.1 slice.63
  335.0 3.5 loss_part.1
  338.5 1.3 reshape.165.gcls_ref
  339.8 1.4 reshape.168.gcls_ref
  341.3 22.5 %ffn_bwd.2 = (f32[512,768]{1,0:T(8,128)}, bf16[4,8,192,384]{3,2,1,0:T(8,128)(2,1)}, bf16[4,8,192,384]{3,2,1,0:T(8,128)(2,1)}, f32[8,768]{1,0:T(8,128)}, f32[4,768]{1,0:T(4,128)}) custom-call(s32[2,4]{1,0:T(2,128)} %broadcast_in_dim.20.spot_ref, bf16[4,8,2,192,384]{4,3,2,1,0:T(8,128)(2,1)} %get-tuple-element.135.pack, bf16[512,768]{1,0:T(8,128)(2,1)} %bitcast.91, ...), custom_call_target="tpu_custom_call" | custom-call | flops 9663676416 | bytes 62914560 | tf_op jit(solution)/shard_map/ffn_bwd/pallas_call | solution.py:328
  363.8 35.0 %ffn_bwd.3 = (f32[1024,768]{1,0:T(8,128)}, bf16[4,8,192,384]{3,2,1,0:T(8,128)(2,1)}, bf16[4,8,192,384]{3,2,1,0:T(8,128)(2,1)}, f32[8,768]{1,0:T(8,128)}, f32[4,768]{1,0:T(4,128)}) custom-call(s32[4,4]{1,0:T(4,128)} %copy-done.2, bf16[4,8,2,192,384]{4,3,2,1,0:T(8,128)(2,1)} %get-tuple-element.134.pack, bf16[1024,768]{1,0:T(8,128)(2,1)} %bitcast.88, ...), custom_call_target="tpu_custom_call" | custom-call | flops 19327352832 | bytes 62914560 | tf_op jit(solution)/shard_map/ffn_bwd/pallas_call | solution.py:328
  398.8 8.4 %pad_maximum_fusion.2 = bf16[32,2,192,384]{3,2,1,0:T(8,128)(2,1)} fusion(bf16[32,1,192,384]{3,2,1,0:T(8,128)(2,1)} %bitcast.80, bf16[32,1,192,384]{3,2,1,0:T(8,128)(2,1)} %bitcast.78), kind=kLoop, calls=%fused_computation.4 | loop fusion | flops 4718592 | bytes 18874368 | tf_op jit(solution)/shard_map/stack | solution.py:570
  407.2 0.0 reduce-scatter.6.cloned.1.call-start
  407.3 8.5 %pad_maximum_fusion.1 = bf16[32,2,192,384]{3,2,1,0:T(8,128)(2,1)} fusion(bf16[32,1,192,384]{3,2,1,0:T(8,128)(2,1)} %bitcast.79, bf16[32,1,192,384]{3,2,1,0:T(8,128)(2,1)} %bitcast.77), kind=kLoop, calls=%fused_computation.3 | loop fusion | flops 4718592 | bytes 18874368 | tf_op jit(solution)/shard_map/stack | solution.py:570
  415.8 0.0 reduce-scatter.4.cloned.1.call-start
  415.9 23.6 %attn_bwd.2 = (f32[512,768]{1,0:T(8,128)}, bf16[4,8,208,384]{3,2,1,0:T(8,128)(2,1)}) custom-call(f32[512,768]{1,0:T(8,128)} %get-tuple-element.73.dh_ref, bf16[512,2304]{1,0:T(8,128)(2,1)} %get-tuple-element.74.qkv_ref, bf16[512,768]{1,0:T(8,128)(2,1)} %get-tuple-element.75.att_ref, bf16[512,768]{1,0:T(8,128)(2,1)} %bitcast.93, s32[2,256,2]{2,1,0:T(8,128)} %copy.98.segc_ref, ...), custom_call_target="tpu_custom_call" | custom-call | flops 8858370048 | bytes 41943040 | tf_op jit(solution)/shard_map/attn_bwd/pallas_call | solution.py:432
  439.5 40.5 %attn_bwd.3 = (f32[1024,768]{1,0:T(8,128)}, bf16[4,8,208,384]{3,2,1,0:T(8,128)(2,1)}) custom-call(f32[1024,768]{1,0:T(8,128)} %get-tuple-element.87.dh_ref, bf16[1024,2304]{1,0:T(8,128)(2,1)} %get-tuple-element.88.qkv_ref, bf16[1024,768]{1,0:T(8,128)(2,1)} %get-tuple-element.89.att_ref, bf16[1024,768]{1,0:T(8,128)(2,1)} %bitcast.90, ...), custom_call_target="tpu_custom_call" | custom-call | flops 17716740096 | bytes 41943040 | tf_op jit(solution)/shard_map/attn_bwd/pallas_call | solution.py:432
  480.0 9.2 %pad_maximum_fusion = bf16[32,2,208,384]{3,2,1,0:T(8,128)(2,1)} fusion(bf16[32,1,208,384]{3,2,1,0:T(8,128)(2,1)} %bitcast.76, bf16[32,1,208,384]{3,2,1,0:T(8,128)(2,1)} %bitcast.75), kind=kLoop, calls=%fused_computation | loop fusion | flops 5111808 | bytes 20447232 | tf_op jit(solution)/shard_map/stack | solution.py:570
  489.2 0.6 copy-done.3
  489.8 0.6 reduce
  490.5 51.4 %reduce-scatter.8.cloned.1.call-done = bf16[1,2,192,384]{3,2,1,0:T(8,128)(2,1)} async-done(((bf16[32,2,192,384]{3,2,1,0:T(8,128)(2,1)}), bf16[1,2,192,384]{3,2,1,0:T(8,128)(2,1)}) %reduce-scatter.8.cloned.1.call-update) | async-done | bytes 294928 | tf_op jit(solution)/shard_map/reduce_scatter | solution.py:572
  541.9 1.0 bitcast_convert_fusion.2
  542.9 0.9 maximum_bitcast_fusion
  543.8 139.5 %reduce-scatter.6.cloned.1.call-done = bf16[1,2,192,384]{3,2,1,0:T(8,128)(2,1)} async-done(((bf16[32,2,192,384]{3,2,1,0:T(8,128)(2,1)}), bf16[1,2,192,384]{3,2,1,0:T(8,128)(2,1)}) %reduce-scatter.6.cloned.1.call-update) | async-done | bytes 294928 | tf_op jit(solution)/shard_map/reduce_scatter | solution.py:572
  683.3 1.8 bitcast_convert_fusion.1
  685.1 142.4 %reduce-scatter.4.cloned.1.call-done = bf16[1,2,208,384]{3,2,1,0:T(8,128)(2,1)} async-done(((bf16[32,2,208,384]{3,2,1,0:T(8,128)(2,1)}), bf16[1,2,208,384]{3,2,1,0:T(8,128)(2,1)}) %reduce-scatter.4.cloned.1.call-update) | async-done | bytes 319504 | tf_op jit(solution)/shard_map/reduce_scatter | solution.py:572
  827.5 1.0 bitcast_convert_fusion
  828.5 0.6 slice.69
  829.1 0.6 slice.68
  829.6 0.8 slice.65
  830.4 0.9 slice.64
  (28 shorter events, 0.3 us)
Async XLA Ops:
  7.2 92.7 %all-gather.9.cloned.1.call-start = ((), (), s32[]{:S(2)}) async-start(), calls=%async_computation.7 | async-start | bytes 10543104 | tf_op jit(solution)/shard_map/all_gather | solution.py:529
  9.8 216.9 %all-gather.7.cloned.1.call-start = ((), (), s32[]{:S(2)}) async-start(), calls=%async_computation.6 | async-start | bytes 19464192 | tf_op jit(solution)/shard_map/all_gather | solution.py:530
  12.7 318.3 %all-gather.11.cloned.1.call-start = ((), (), s32[]{:S(2)}) async-start(), calls=%async_computation.8 | async-start | bytes 1216512 | tf_op jit(solution)/shard_map/all_gather | solution.py:552
  15.1 93.8 %copy-start.2 = (s32[4,4]{1,0:T(4,128)}, s32[4,4]{1,0:T(4,128)S(1)}, u32[]{:S(2)}) copy-start(s32[4,4]{1,0:T(4,128)S(1)} %sub.20.spot_ref) | copy-start | bytes 196
  256.2 21.7 %copy-start.1 = (bf16[8,768]{1,0:T(8,128)(2,1)}, bf16[8,768]{1,0:T(8,128)(2,1)S(1)}, u32[]{:S(2)}) copy-start(bf16[8,768]{1,0:T(8,128)(2,1)S(1)} %convert_element_type.37.q_own) | copy-start | bytes 36868
  256.2 22.4 %copy-start.5 = (u32[32]{0:T(128)S(1)}, u32[32]{0:T(128)}, u32[]{:S(2)}) copy-start(u32[32]{0:T(128)} %constant.66) | copy-start | bytes 388
  256.2 23.7 %copy-start.4 = (s32[64]{0:T(128)S(1)}, s32[64]{0:T(128)}, u32[]{:S(2)}) copy-start(s32[64]{0:T(128)} %param.19) | copy-start | bytes 772
  277.9 57.0 %copy-start = (bf16[16,768]{1,0:T(8,128)(2,1)}, bf16[16,768]{1,0:T(8,128)(2,1)S(1)}, u32[]{:S(2)}) copy-start(bf16[16,768]{1,0:T(8,128)(2,1)S(1)} %convert_element_type.39.p_own) | copy-start | bytes 73732
  278.6 263.3 %reduce-scatter.8.cloned.1.call-start = ((), (), s32[]{:S(2)}) async-start(), calls=%async_computation.5 | async-start | bytes 9732096 | tf_op jit(solution)/shard_map/reduce_scatter | solution.py:572
  407.2 276.1 %reduce-scatter.6.cloned.1.call-start = ((), (), s32[]{:S(2)}) async-start(), calls=%async_computation.4 | async-start | bytes 9732096 | tf_op jit(solution)/shard_map/reduce_scatter | solution.py:572
  415.8 411.7 %reduce-scatter.4.cloned.1.call-start = ((), (), s32[]{:S(2)}) async-start(), calls=%async_computation.3 | async-start | bytes 10543104 | tf_op jit(solution)/shard_map/reduce_scatter | solution.py:572
  489.2 0.7 copy-start.3
Sparse Core Ops, SparseCore 0:
  11.6 88.2 all-gather.8
  103.4 123.1 all-gather.6
  278.7 52.3 all-gather.10
  407.3 134.5 reduce-scatter.7
  548.6 134.6 reduce-scatter.5
  689.2 138.2 reduce-scatter.3

commit v2 on v1

v2 whole, which is shorter than its diff:
```python
import functools
import math

import jax
import jax.numpy as jnp
from jax import lax
from jax.experimental import pallas as pl
from jax.experimental.pallas import tpu as pltpu
from jax.sharding import PartitionSpec as P

HD = 64
EXTRA = 16
ROW = 256
FFN_ROW = 256
NEG_FILL = -1000000000.0
EPSILON = 1e-06
ROOT_HALF = 0.7071067811865476
INV_ROOT_TWO_PI = 0.3989422804014327
F32 = jnp.float32
BF16 = jnp.bfloat16
MIB = 1 << 20
ANY = pl.BlockSpec(memory_space=pl.ANY)
SMEM = pl.BlockSpec(memory_space=pltpu.SMEM)


def mm(left, right):
    return lax.dot_general(left, right, (((1,), (0,)), ((), ())), preferred_element_type=F32)


def mm_nt(left, right):
    return lax.dot_general(left, right, (((1,), (1,)), ((), ())), preferred_element_type=F32)


def mm_tn(left, right):
    return lax.dot_general(left, right, (((0,), (0,)), ((), ())), preferred_element_type=F32)


def whole(shape):
    return pl.BlockSpec(shape, lambda i: (0,) * len(shape), pipeline_mode=pl.Buffered(1))


def norm_rows(summed):
    centred = summed - jnp.mean(summed, axis=-1, keepdims=True)
    inverse = lax.rsqrt(jnp.mean(centred * centred, axis=-1, keepdims=True) + EPSILON)
    return centred * inverse, inverse


def norm_back(grad_out, gain, normed, inverse):
    scaled = grad_out * gain
    inner = (
        scaled
        - jnp.mean(scaled, axis=-1, keepdims=True)
        - normed * jnp.mean(scaled * normed, axis=-1, keepdims=True)
    )
    return inverse * inner


def col_sum(block):
    return jnp.sum(block, axis=0, keepdims=True)


class Place:
    def __init__(self, npb, npa, first, into):
        self.npb, self.npa, self.first, self.into = npb, npa, first, into
        self.count = 1 if first is None else 8 if into else 2
        self.lead = (npb, npa) if first is None else (4,) if into else (2, 2, 4)

    def blocks(self, spot):
        if self.first is None:
            return [(0, (b, a), b, a) for b in range(self.npb) for a in range(self.npa)]
        y, core, z, x = (spot[k] for k in range(4))
        found = []
        for core_d in range(2):
            for second in range(2):
                for first in range(2):
                    for z_d in range(4):
                        y_d, x_d = (first, second) if self.first == "y" else (second, first)
                        index = core_d * 4 + second * 2 + first if self.into else core_d
                        lead = (z_d,) if self.into else (first, second, z_d)
                        b = lax.bitwise_xor(y, y_d) * 2 + lax.bitwise_xor(core, core_d)
                        a = lax.bitwise_xor(z, z_d) * 2 + lax.bitwise_xor(x, x_d)
                        found.append((index, lead, b, a))
        return found


def span(index, length):
    start = index * length
    if isinstance(start, int):
        return pl.ds(start, length)
    return pl.ds(pl.multiple_of(start, math.gcd(length, 1 << 20)), length)


def lane_span(index, stride, base, length):
    start = index * stride + base
    if isinstance(start, int):
        return pl.ds(start, length)
    return pl.ds(pl.multiple_of(start, 128), length)


def attn_fwd_kernel(dims, place, here_ref, *refs):
    packs, refs = refs[: place.count], refs[place.count :]
    (x_ref, segc_ref, segr_ref, qkv_ref, att_ref, xhat_ref, inv_ref, wqkv_ref, wout_ref, vec_ref, bup_ref, held, sem) = refs
    npb, npa, r, wq, wo, rows_per, w1, w2 = dims
    d = x_ref.shape[1]

    @pl.when(pl.program_id(0) == 0)
    def _():
        for index, lead, b, a in place.blocks(here_ref):
            pltpu.make_async_copy(packs[index].at[lead], held.at[b, a], sem).start()
        pltpu.make_async_copy(held, held, sem).wait()
        for b in range(npb):
            rows = pl.ds(b * r, r)
            wqkv_ref[rows, :] = jnp.concatenate([held[b, a, :r, :wq] for a in range(npa)], axis=1)
            wout_ref[rows, :] = jnp.concatenate([held[b, a, :r, wq:] for a in range(npa)], axis=1)
            extra = [held[b, a, r:, :].astype(F32) for a in range(npa)]
            vec_ref[pl.ds(b * rows_per, rows_per), :] = jnp.concatenate(
                [part[:rows_per, :w1] for part in extra], axis=1)
            bup_ref[b : b + 1, :] = jnp.concatenate(
                [part[rows_per : rows_per + 1, :w2] for part in extra], axis=1)

    flat = x_ref[...]
    qkv_ref[:, :d] = ((mm(flat, wqkv_ref[:, :d]) + vec_ref[4:5, :]).astype(BF16) * BF16(HD ** -0.5))
    qkv_ref[:, d : 2 * d] = mm(flat, wqkv_ref[:, d : 2 * d]).astype(BF16)
    qkv_ref[:, 2 * d :] = (mm(flat, wqkv_ref[:, 2 * d :]) + vec_ref[5:6, :]).astype(BF16)
    blocked = jnp.where(segc_ref[0][:, 0:1] == segr_ref[0][1:2, :], 0.0, NEG_FILL)
    low_half = lax.broadcasted_iota(jnp.int32, (1, 2 * HD), 1) < HD
    keep = (low_half.astype(F32).astype(BF16), (1.0 - low_half.astype(F32)).astype(BF16))
    for p in range(d // (2 * HD)):
        lanes = slice(p * 2 * HD, (p + 1) * 2 * HD)
        q2 = qkv_ref[:, lanes]
        k2 = qkv_ref[:, d + p * 2 * HD : d + (p + 1) * 2 * HD]
        v2 = qkv_ref[:, 2 * d + p * 2 * HD : 2 * d + (p + 1) * 2 * HD]
        parts = []
        for h in range(2):
            scores = mm_nt(q2 * keep[h], k2) + blocked
            terms = jnp.exp(scores - jnp.max(scores, axis=-1, keepdims=True))
            total = jnp.sum(terms, axis=-1, keepdims=True)
            prob = (terms * (1.0 / total)).astype(BF16)
            parts.append(mm(prob, v2))
        att_ref[:, lanes] = jnp.where(low_half, parts[0], parts[1]).astype(BF16)
    branch = mm(att_ref[...], wout_ref[...]) + vec_ref[6:7, :]
    normed, inverse = norm_rows(flat.astype(F32) + branch)
    xhat_ref[...] = normed
    inv_ref[...] = inverse


def attn_fwd(dims, place, here, packs, x, segc, segr):
    npb, npa, r, wq, wo, rows_per, w1, w2 = dims
    tokens, d = x.shape
    steps = tokens // ROW
    ff = w2 * npa * npb
    row = lambda width: pl.BlockSpec((ROW, width), lambda i: (i, 0))
    return pl.pallas_call(
        functools.partial(attn_fwd_kernel, dims, place),
        grid=(steps,),
        in_specs=[SMEM] + [ANY] * place.count + [row(d), pl.BlockSpec((1, ROW, 2), lambda i: (i, 0, 0)),
                  pl.BlockSpec((1, 2, ROW), lambda i: (i, 0, 0))],
        out_specs=[row(3 * d), row(d), row(d), row(1), whole((d, 3 * d)), whole((d, d)), whole((8, d)),
                   whole((npb, ff // npb))],
        out_shape=[
            jax.ShapeDtypeStruct((tokens, 3 * d), BF16),
            jax.ShapeDtypeStruct((tokens, d), BF16),
            jax.ShapeDtypeStruct((tokens, d), F32),
            jax.ShapeDtypeStruct((tokens, 1), F32),
            jax.ShapeDtypeStruct((d, 3 * d), BF16),
            jax.ShapeDtypeStruct((d, d), BF16),
            jax.ShapeDtypeStruct((8, d), F32),
            jax.ShapeDtypeStruct((npb, ff // npb), F32),
        ],
        scratch_shapes=[pltpu.VMEM((npb, npa, r + EXTRA, wq + wo), BF16), pltpu.SemaphoreType.DMA],
        compiler_params=pltpu.CompilerParams(vmem_limit_bytes=58 * MIB),
        cost_estimate=pl.CostEstimate(flops=2 * tokens * d * (4 * d + 8 * ROW), transcendentals=0,
                                      bytes_accessed=40 * MIB),
        name="attn_fwd",
    )(here, *packs, x, segc, segr)


class FfnPlace:
    def __init__(self, up, down=None, e=None):
        self.up, self.down, self.apart, self.e = up, down or up, down is not None, e
        self.npb, self.npa = up.npb, up.npa
        self.count = up.count + down.count if down else up.count

    def shapes(self, d, ff):
        block = (d // self.npb * (1 if self.apart else 2), ff // self.npa)
        places = [self.up, self.down] if self.apart else [self.up]
        return [jax.ShapeDtypeStruct(place.lead + block, BF16) for place in places for _ in range(place.count)]

    def pieces(self, arrays, which, rows, spot):
        place = self.down if which else self.up
        arrays = arrays[self.up.count :] if which and self.apart else arrays
        base = rows if which and not self.apart else 0
        extra = () if self.e is None else (self.e,)
        return [(arrays[index], lead + extra, base, b, a) for index, lead, b, a in place.blocks(spot)]


class FfnLoad:
    def __init__(self, place, spot, packs, up, down, sems):
        self.place, self.spot, self.packs, self.up, self.down, self.sems = place, spot, packs, up, down, sems

    def start(self):
        npb, npa = self.place.npb, self.place.npa
        d, ff = self.up.shape
        r, c, dr, dc = d // npb, ff // npa, d // npa, ff // npb
        ups = self.place.pieces(self.packs, 0, r, self.spot)
        downs = self.place.pieces(self.packs, 1, r, self.spot)
        if not self.place.apart:
            downs = sorted(downs, key=lambda piece: piece[3])
            ups = sorted(ups, key=lambda piece: piece[4])
        for k in range(len(ups)):
            array, lead, base, b, a = ups[k]
            pltpu.make_async_copy(array.at[lead + (pl.ds(base, r),)], self.up.at[span(b, r), lane_span(a, c, 0, c)],
                                  self.sems.at[0, a * npb // npa]).start()
            array, lead, base, b, a = downs[k]
            for j in range(dc // c):
                pltpu.make_async_copy(array.at[lead + (pl.ds(base + j * dr, dr),)],
                                      self.down.at[span(a, dr), lane_span(b, dc, j * c, c)], self.sems.at[1, b]).start()

    def wait(self, which, t):
        ref = self.down if which else self.up
        width = ref.shape[1] // self.place.npb
        part = ref.at[:, pl.ds(t * width, width)]
        pltpu.make_async_copy(part, part, self.sems.at[which, t]).wait()


def ffn_fwd_kernel(place, here_ref, spot_ref, *refs):
    packs, refs = refs[: place.count], refs[place.count :]
    (xhat_ref, vec_ref, bup_ref, act_ref, slope_ref, norm_ref, inv_ref, enc_ref, cls_ref, up, down, held, sems) = refs
    step = pl.program_id(0)

    load = FfnLoad(place, here_ref, packs, up, down, sems)

    @pl.when(step == 0)
    def _():
        load.start()

    ff = up.shape[1]
    tiles = bup_ref.shape[0]
    width = ff // tiles
    first_norm = xhat_ref[...] * vec_ref[0:1, :] + vec_ref[1:2, :]
    first_low = first_norm.astype(BF16)
    total = first_norm + vec_ref[7:8, :]
    for t in range(tiles):
        cols = slice(t * width, (t + 1) * width)

        @pl.when(step == 0)
        def _():
            load.wait(0, t)
            load.wait(1, t)

        hidden = mm(first_low, up[:, cols]) + bup_ref[t : t + 1, :]
        cdf = 0.5 + 0.5 * lax.erf(hidden * ROOT_HALF)
        act = (hidden * cdf).astype(BF16)
        act_ref[:, cols] = act
        slope_ref[:, cols] = (cdf + hidden * (jnp.exp(-0.5 * hidden * hidden) * INV_ROOT_TWO_PI)).astype(BF16)
        total = total + mm_nt(act, down[:, cols])
    normed, inverse = norm_rows(total)
    norm_ref[...] = normed
    inv_ref[...] = inverse
    enc = (normed * vec_ref[2:3, :] + vec_ref[3:4, :]).astype(BF16)
    enc_ref[...] = enc
    held[...] = enc.astype(F32)
    for j in range(cls_ref.shape[1]):
        cls_ref[0, j : j + 1, :] = held[pl.ds(spot_ref[step, j], 1), :]


def ffn_fwd(place, here, spots, packs, xhat, vec, bup):
    tokens, d = xhat.shape
    steps, per_row = spots.shape
    ff = bup.shape[0] * bup.shape[1]
    row = lambda width: pl.BlockSpec((FFN_ROW, width), lambda i: (i, 0))
    return pl.pallas_call(
        functools.partial(ffn_fwd_kernel, place),
        grid=(steps,),
        in_specs=[SMEM, SMEM] + [ANY] * place.count + [row(d), whole(vec.shape), whole(bup.shape)],
        out_specs=[row(ff), row(ff), row(d), row(1), row(d), pl.BlockSpec((1, per_row, d), lambda i: (i, 0, 0))],
        out_shape=[
            jax.ShapeDtypeStruct((tokens, ff), BF16),
            jax.ShapeDtypeStruct((tokens, ff), BF16),
            jax.ShapeDtypeStruct((tokens, d), F32),
            jax.ShapeDtypeStruct((tokens, 1), F32),
            jax.ShapeDtypeStruct((tokens, d), BF16),
            jax.ShapeDtypeStruct((steps, per_row, d), F32),
        ],
        scratch_shapes=[pltpu.VMEM((d, ff), BF16), pltpu.VMEM((d, ff), BF16), pltpu.VMEM((FFN_ROW, d), F32),
                        pltpu.SemaphoreType.DMA((2, place.npb))],
        compiler_params=pltpu.CompilerParams(vmem_limit_bytes=58 * MIB),
        cost_estimate=pl.CostEstimate(flops=4 * tokens * d * ff, transcendentals=0, bytes_accessed=40 * MIB),
        name="ffn_fwd",
    )(here, spots, *packs, xhat, vec, bup)


def loss_kernel(scale, q_count, p_count, ids_ref, own_ids_ref, heads_ref, own_ref, loss_ref, gq_ref, gp_ref):
    def split_mm(dot, left, right):
        high = left.astype(BF16)
        rest = left - high.astype(F32)
        mid = rest.astype(BF16)
        tail = (rest - mid.astype(F32)).astype(BF16)
        return dot(high, right) + dot(mid, right) + dot(tail, right)

    def log_norm(scores):
        peak = jnp.max(scores, axis=1, keepdims=True)
        return peak + jnp.log(jnp.sum(jnp.exp(scores - peak), axis=1, keepdims=True))

    def parts(block):
        wide = block.astype(F32)
        d = wide.shape[-1]
        p_rows = wide[:, :p_count].reshape(-1, d).astype(BF16)
        q_rows = wide[:, p_count : p_count + q_count].reshape(-1, d).astype(BF16)
        code = wide[:, p_count + q_count :, :128].reshape(-1, 128)
        return p_rows, q_rows, (code[:, 0:1] * 256.0 + code[:, 1:2]).astype(jnp.int32)

    p_all, q_all, hit_all = parts(heads_ref[...])
    p_own, q_own, hit_own = parts(own_ref[...])
    norm_all = log_norm(mm_nt(q_all, p_all) * scale)
    own_rows = mm_nt(q_own, p_all) * scale
    norm_own = log_norm(own_rows)
    hits = ids_ref[...] == hit_own
    loss_ref[...] = norm_own - jnp.sum(jnp.where(hits, own_rows, 0.0), axis=1, keepdims=True)
    tile = jnp.exp(own_rows - norm_own) - jnp.where(hits, 1.0, 0.0)
    gq_ref[...] = split_mm(mm, tile, p_all) * scale
    own_cols = mm_nt(q_all, p_own) * scale
    hits = own_ids_ref[...] == hit_all
    tile = jnp.exp(own_cols - norm_all) - jnp.where(hits, 1.0, 0.0)
    gp_ref[...] = split_mm(mm_tn, tile, q_all) * scale


def loss_part(ids, own_ids, heads, own, q_count, p_count):
    d = heads.shape[2]
    return pl.pallas_call(
        functools.partial(loss_kernel, 3.0 / math.sqrt(d), q_count, p_count),
        out_shape=[
            jax.ShapeDtypeStruct((q_count, 1), F32),
            jax.ShapeDtypeStruct((q_count, d), F32),
            jax.ShapeDtypeStruct((p_count, d), F32),
        ],
        compiler_params=pltpu.CompilerParams(vmem_limit_bytes=60 * MIB),
        name="loss_part",
    )(ids, own_ids, heads, own)


def ffn_bwd_kernel(place, goal, steps, here_ref, spot_ref, *refs):
    packs, refs = refs[: place.count], refs[place.count :]
    cot_ref, gcls_ref, norm_ref, inv2_ref, act_ref, slope_ref, xhat_ref, inv1_ref, vec_ref, dh_ref = refs[:10]
    grads, refs = refs[10 : 10 + goal.count], refs[10 + goal.count :]
    gvec_ref, gbup_ref, up, down, held, first_t, down_t, hidden_all, act_all, sems = refs
    step = pl.program_id(0)
    tiles = gbup_ref.shape[0]
    ff = up.shape[1]
    width = ff // tiles

    load = FfnLoad(place, here_ref, packs, up, down, sems)

    @pl.when(step == 0)
    def _():
        load.start()
        gvec_ref[...] = jnp.zeros_like(gvec_ref)
        gbup_ref[...] = jnp.zeros_like(gbup_ref)

    @pl.when(step < steps)
    def _():
        held[...] = cot_ref[...].astype(F32)
        for j in range(gcls_ref.shape[1]):
            spot = pl.ds(spot_ref[step, j], 1)
            held[spot, :] = held[spot, :] + gcls_ref[0, j : j + 1, :]
        grad_out = held[...]
        normed = norm_ref[...]
        gvec_ref[2:3, :] += col_sum(grad_out * normed)
        gvec_ref[3:4, :] += col_sum(grad_out)
        grad_two = norm_back(grad_out, vec_ref[2:3, :], normed, inv2_ref[...])
        down_low = grad_two.astype(BF16)
        gvec_ref[7:8, :] += col_sum(down_low.astype(F32))
        tok = pl.ds(pl.multiple_of(step * FFN_ROW, FFN_ROW), FFN_ROW)
        total = grad_two
        for t in range(tiles):
            cols = slice(t * width, (t + 1) * width)

            @pl.when(step == 0)
            def _():
                load.wait(1, t)
                load.wait(0, t)

            hidden = (mm(down_low, down[:, cols]) * slope_ref[:, cols].astype(F32)).astype(BF16)
            hidden_all[tok, cols] = hidden
            gbup_ref[t : t + 1, :] += col_sum(hidden.astype(F32))
            total = total + mm_nt(hidden, up[:, cols])
        act_all[tok, :] = act_ref[...]
        xhat = xhat_ref[...]
        gvec_ref[0:1, :] += col_sum(total * xhat)
        gvec_ref[1:2, :] += col_sum(total)
        dh_ref[...] = norm_back(total, vec_ref[0:1, :], xhat, inv1_ref[...])
        first_low = (xhat * vec_ref[0:1, :] + vec_ref[1:2, :]).astype(BF16)
        for s in range(steps):
            @pl.when(step == s)
            def _():
                first_t[:, s * FFN_ROW : (s + 1) * FFN_ROW] = first_low.T
                down_t[:, s * FFN_ROW : (s + 1) * FFN_ROW] = down_low.T

    npb, npa = goal.npb, goal.npa
    r, c, dr = up.shape[0] // npb, ff // npa, up.shape[0] // npa
    part = ff // npb

    for b in range(npb):
        @pl.when(step == steps + b)
        def _():
            cols = slice(b * part, (b + 1) * part)
            up[:, cols] = mm(first_t[...], hidden_all[:, cols]).astype(BF16)

    @pl.when(step == steps + npb - 1)
    def _():
        for array, lead, base, b, a in goal.pieces(grads, 0, r, here_ref):
            pltpu.make_async_copy(up.at[span(b, r), lane_span(a, c, 0, c)], array.at[lead + (pl.ds(base, r),)],
                                  sems.at[0, 0]).start()

    for b in range(npb):
        @pl.when(step == steps + npb + b)
        def _():
            cols = slice(b * part, (b + 1) * part)
            down[:, cols] = mm(down_t[...], act_all[:, cols]).astype(BF16)

    @pl.when(step == steps + 2 * npb - 1)
    def _():
        for array, lead, base, b, a in goal.pieces(grads, 1, r, here_ref):
            for j in range(part // c):
                pltpu.make_async_copy(down.at[span(a, dr), lane_span(b, part, j * c, c)],
                                      array.at[lead + (pl.ds(base + j * dr, dr),)], sems.at[1, 0]).start()
        pltpu.make_async_copy(up, up, sems.at[0, 0]).wait()
        pltpu.make_async_copy(down, down, sems.at[1, 0]).wait()


def ffn_bwd(place, goal, here, spots, packs, cot, gcls, norm2, inv2, act, slope, xhat, inv1, vec, bup_shape):
    tokens, d = xhat.shape
    steps, per_row = spots.shape
    goal_shapes = goal.shapes(d, act.shape[1])
    ff = act.shape[1]
    last = lambda i: jnp.minimum(i, steps - 1)
    row = lambda width: pl.BlockSpec((FFN_ROW, width), lambda i: (last(i), 0))
    return pl.pallas_call(
        functools.partial(ffn_bwd_kernel, place, goal, steps),
        grid=(steps + 2 * goal.npb,),
        in_specs=[SMEM, SMEM] + [ANY] * place.count + [
            row(d), pl.BlockSpec((1, per_row, d), lambda i: (last(i), 0, 0)), row(d), row(1), row(ff), row(ff), row(d), row(1),
            whole(vec.shape)],
        out_specs=[row(d)] + [ANY] * goal.count + [whole(vec.shape), whole(bup_shape)],
        out_shape=[
            jax.ShapeDtypeStruct((tokens, d), F32),
            *goal_shapes,
            jax.ShapeDtypeStruct(vec.shape, F32),
            jax.ShapeDtypeStruct(bup_shape, F32),
        ],
        scratch_shapes=[pltpu.VMEM((d, ff), BF16), pltpu.VMEM((d, ff), BF16), pltpu.VMEM((FFN_ROW, d), F32),
                        pltpu.VMEM((d, tokens), BF16), pltpu.VMEM((d, tokens), BF16), pltpu.VMEM((tokens, ff), BF16),
                        pltpu.VMEM((tokens, ff), BF16), pltpu.SemaphoreType.DMA((2, place.npb))],
        compiler_params=pltpu.CompilerParams(vmem_limit_bytes=60 * MIB),
        cost_estimate=pl.CostEstimate(flops=8 * tokens * d * ff, transcendentals=0, bytes_accessed=60 * MIB),
        name="ffn_bwd",
    )(here, spots, *packs, cot, gcls, norm2, inv2, act, slope, xhat, inv1, vec)


def attn_bwd_kernel(first, dh_ref, qkv_ref, att_w_ref, segc_ref, segr_ref, gvec_in, proj_in, branch_in, proj, branch, gvec):
    d = dh_ref.shape[1]

    @pl.when(pl.program_id(0) == 0)
    def _():
        gvec[...] = gvec_in[...]

    low = dh_ref[...].astype(BF16)
    branch[...] = low
    gvec[6:7, :] += col_sum(low.astype(F32))
    att_grad = mm_nt(low, att_w_ref[...]).astype(BF16)
    blocked = jnp.where(segc_ref[0][:, 1:2] == segr_ref[0][0:1, :], 0.0, NEG_FILL)
    low_half = lax.broadcasted_iota(jnp.int32, (1, 2 * HD), 1) < HD
    keep = (low_half.astype(F32).astype(BF16), (1.0 - low_half.astype(F32)).astype(BF16))
    for p in range(d // (2 * HD)):
        lanes = slice(p * 2 * HD, (p + 1) * 2 * HD)
        k_lanes = slice(d + p * 2 * HD, d + (p + 1) * 2 * HD)
        v_lanes = slice(2 * d + p * 2 * HD, 2 * d + (p + 1) * 2 * HD)
        q2 = qkv_ref[:, lanes]
        k2 = qkv_ref[:, k_lanes]
        v2 = qkv_ref[:, v_lanes]
        g2 = att_grad[:, lanes]
        dq, dk, dv = [], [], []
        for h in range(2):
            scores = mm_nt(k2 * keep[h], q2) + blocked
            terms = jnp.exp(scores - jnp.max(scores, axis=0, keepdims=True))
            prob = terms * (1.0 / jnp.sum(terms, axis=0, keepdims=True))
            weighed = prob * mm_nt(v2 * keep[h], g2)
            sgrad = (weighed - prob * jnp.sum(weighed, axis=0, keepdims=True)).astype(BF16)
            dv.append(mm(prob.astype(BF16), g2))
            dk.append(mm(sgrad, q2))
            dq.append(mm_tn(sgrad, k2))
        proj[:, lanes] = (jnp.where(low_half, dq[0], dq[1]) * (HD ** -0.5)).astype(BF16)
        proj[:, k_lanes] = jnp.where(low_half, dk[0], dk[1]).astype(BF16)
        proj[:, v_lanes] = jnp.where(low_half, dv[0], dv[1]).astype(BF16)
    gvec[4:5, :] += col_sum(proj[:, :d].astype(F32))
    gvec[5:6, :] += col_sum(proj[:, 2 * d :].astype(F32))


def attn_bwd(first, last, dh, qkv, segc, segr, wout, gvec, before):
    tokens, d = dh.shape
    row = lambda width: pl.BlockSpec((ROW, width), lambda i: (i + first, 0))
    shapes = [jax.ShapeDtypeStruct((tokens, 3 * d), BF16), jax.ShapeDtypeStruct((tokens, d), BF16)]
    if before is None:
        kernel = lambda *refs: attn_bwd_kernel(first, *refs[:6], None, None, *refs[6:])
    else:
        kernel = lambda *refs: attn_bwd_kernel(first, *refs)
    return pl.pallas_call(
        kernel,
        grid=(last - first,),
        in_specs=[row(d), row(3 * d), whole(wout.shape), pl.BlockSpec((1, ROW, 2), lambda i: (i + first, 0, 0)),
                  pl.BlockSpec((1, 2, ROW), lambda i: (i + first, 0, 0)), whole(gvec.shape)]
        + ([] if before is None else [ANY, ANY]),
        out_specs=[row(3 * d), row(d), whole(gvec.shape)],
        out_shape=shapes + [jax.ShapeDtypeStruct(gvec.shape, F32)],
        input_output_aliases={} if before is None else {6: 0, 7: 1},
        compiler_params=pltpu.CompilerParams(vmem_limit_bytes=60 * MIB),
        cost_estimate=pl.CostEstimate(flops=(last - first) * ROW * d * (2 * d + 40 * ROW), transcendentals=0,
                                      bytes_accessed=8 * MIB),
        name="attn_bwd",
    )(dh, qkv, wout, segc, segr, gvec, *(before or ()))


def attn_grad_kernel(dims, goals, here_ref, x_ref, att_ref, proj_ref, branch_ref, gvec, gbup, *refs):
    total = sum(goal.count for goal, _, _ in goals)
    grads, (x_t, wide, out, main, extra, sems) = refs[:total], refs[total:]
    npb, npa, r, wq, wo, rows_per, w1, w2 = dims
    step = pl.program_id(0)
    d = x_ref.shape[1]
    c = wq + wo

    def widen(piece):
        if piece.shape[1] == c:
            return piece
        return jnp.concatenate([piece, jnp.zeros((piece.shape[0], c - piece.shape[1]), F32)], axis=1)

    def multiply(g):
        wide[:, g * d : (g + 1) * d] = mm(x_t[...], proj_ref[...]).astype(BF16)

    def fill(g):
        for a in range(npa):
            if -(-(a + 1) * wq // d) == g:
                main[a] = jnp.concatenate([wide[:, a * wq : (a + 1) * wq], out[:, a * wo : (a + 1) * wo]], axis=1)

    @pl.when(step == 0)
    def _():
        x_t[...] = x_ref[...].T
        multiply(0)
        out[...] = mm(att_ref[...].T, branch_ref[...]).astype(BF16)

    for g in range(1, 3):
        @pl.when(step == g)
        def _():
            multiply(g)
            fill(g)

    @pl.when(step == 3)
    def _():
        fill(3)
        for b in range(npb):
            for a in range(npa):
                rows = [widen(gvec[b * rows_per : (b + 1) * rows_per, a * w1 : (a + 1) * w1]),
                        widen(gbup[b : b + 1, a * w2 : (a + 1) * w2]),
                        jnp.zeros((EXTRA - 1 - rows_per, c), F32)]
                extra[b * npa + a] = jnp.concatenate(rows, axis=0).astype(BF16)
        base = 0
        for goal, low, high in goals:
            top = min(high, r)
            for index, lead, b, a in goal.blocks(here_ref):
                target = grads[base + index]
                start = b * r + low
                if not isinstance(start, int):
                    start = pl.multiple_of(start, 16)
                pltpu.make_async_copy(main.at[a, pl.ds(start, top - low)], target.at[lead + (pl.ds(0, top - low),)],
                                      sems.at[0]).start()
                if high > r:
                    pltpu.make_async_copy(extra.at[b * npa + a], target.at[lead + (pl.ds(r - low, EXTRA),)],
                                          sems.at[1]).start()
            base += goal.count
        pltpu.make_async_copy(main, main, sems.at[0]).wait()
        pltpu.make_async_copy(extra, extra, sems.at[1]).wait()


def attn_grad(dims, goals, here, x, att, proj, branch, gvec, gbup):
    npb, npa, r, wq, wo, rows_per, w1, w2 = dims
    tokens, d = x.shape
    c = wq + wo
    return pl.pallas_call(
        functools.partial(attn_grad_kernel, dims, goals),
        grid=(4,),
        in_specs=[SMEM, whole(x.shape), whole(att.shape), pl.BlockSpec((tokens, d), lambda i: (0, jnp.minimum(i, 2))),
                  whole(branch.shape), whole(gvec.shape), whole(gbup.shape)],
        out_specs=[ANY] * sum(goal.count for goal, _, _ in goals),
        out_shape=[jax.ShapeDtypeStruct(goal.lead + (high - low, c), BF16)
                   for goal, low, high in goals for _ in range(goal.count)],
        scratch_shapes=[pltpu.VMEM((d, tokens), BF16), pltpu.VMEM((d, 3 * d), BF16), pltpu.VMEM((d, d), BF16),
                        pltpu.VMEM((npa, d, c), BF16),
                        pltpu.VMEM((npb * npa, EXTRA, c), BF16), pltpu.SemaphoreType.DMA((2,))],
        compiler_params=pltpu.CompilerParams(vmem_limit_bytes=60 * MIB),
        cost_estimate=pl.CostEstimate(flops=8 * tokens * d * d, transcendentals=0, bytes_accessed=16 * MIB),
        name="attn_grad",
    )(here, x, att, proj, branch, gvec, gbup)


def input_grad_kernel(proj_ref, weight_ref, dh_ref, out_ref):
    out_ref[...] = mm_nt(proj_ref[...], weight_ref[...]) + dh_ref[...]


def input_grad(proj, wqkv, dh):
    tokens, d = dh.shape
    row = lambda width: pl.BlockSpec((ROW, width), lambda i: (i, 0))
    return pl.pallas_call(
        input_grad_kernel,
        grid=(tokens // ROW,),
        in_specs=[row(3 * d), whole(wqkv.shape), row(d)],
        out_specs=row(d),
        out_shape=jax.ShapeDtypeStruct((tokens, d), F32),
        compiler_params=pltpu.CompilerParams(vmem_limit_bytes=60 * MIB),
        cost_estimate=pl.CostEstimate(flops=6 * tokens * d * d, transcendentals=0, bytes_accessed=16 * MIB),
        name="input_grad",
    )(proj, wqkv, dh)


class Blocks:
    def __init__(self, npb, npa, d, ff):
        self.npb, self.npa, self.d, self.ff = npb, npa, d, ff
        self.r, self.wq, self.wo, self.c = d // npb, 3 * d // npa, d // npa, ff // npa
        self.dr, self.dc = d // npa, ff // npb
        self.rows_per, self.w1, self.w2 = 8 // npb, d // npa, ff // (npa * npb)
        self.direct = self.c % 128 == 0 and self.r % 16 == 0 and self.dr % 16 == 0
        if self.direct:
            self.dims = (npb, npa, self.r, self.wq, self.wo, self.rows_per, self.w1, self.w2)
        else:
            self.dims = (1, 1, d, 3 * d, d, 8, d, ff)

    def pack(self, w_qkv, w_out, w_up, w_down, norm_bias, bias_up):
        c = self.wq + self.wo
        vec = jnp.pad(norm_bias, ((0, 0), (0, 0), (0, c - self.w1)))
        bup = jnp.pad(bias_up[:, None, :], ((0, 0), (0, EXTRA - 1 - self.rows_per), (0, c - self.w2)))
        attn = jnp.concatenate([jnp.concatenate([w_qkv, w_out], axis=2), vec, bup], axis=1)
        down_t = jnp.swapaxes(w_down, 1, 2)
        down = jnp.concatenate([down_t[:, :, j : j + self.c] for j in range(0, self.dc, self.c)], axis=1)
        return attn, jnp.concatenate([w_up, down], axis=1)

    def from_blocks(self, attn, ffn):
        if self.direct:
            return attn, ffn
        d, ff, r = self.d, self.ff, self.r
        rows = lambda part, height: part.transpose(0, 2, 1, 3).reshape(height, -1)
        qkv = rows(attn[:, :, :r, : self.wq], d)
        out = rows(attn[:, :, :r, self.wq :], d)
        vec = rows(attn[:, :, r : r + self.rows_per, : self.w1], 8)
        bup = attn[:, :, r + self.rows_per, : self.w2].reshape(1, ff)
        vec = jnp.pad(vec, ((0, 0), (0, 3 * d)))
        bup = jnp.pad(bup, ((0, EXTRA - 9), (0, 4 * d - ff)))
        wide = jnp.concatenate([jnp.concatenate([qkv, out], axis=1), vec, bup], axis=0)
        up = rows(ffn[:, :, :r], d)
        pieces = self.dc // self.c
        down = ffn[:, :, r:].reshape(self.npb, self.npa, pieces, self.dr, self.c)
        down = down.transpose(1, 3, 0, 2, 4).reshape(d, ff)
        return wide[None, None], jnp.concatenate([up, down])[None, None]

    def to_blocks(self, attn, ffn):
        if self.direct:
            return attn, ffn
        d, ff, npb, npa = self.d, self.ff, self.npb, self.npa
        blocks = lambda part, height: part.reshape(npb, height, npa, -1).transpose(0, 2, 1, 3)
        wide = attn[0, 0]
        c = self.wq + self.wo
        main = jnp.concatenate([blocks(wide[:d, : 3 * d], self.r), blocks(wide[:d, 3 * d :], self.r)], axis=3)
        vec = blocks(wide[d : d + 8, :d], self.rows_per)
        vec = jnp.pad(vec, ((0, 0), (0, 0), (0, 0), (0, c - self.w1)))
        bup = wide[d + 8, :ff].reshape(npb, npa, 1, self.w2)
        bup = jnp.pad(bup, ((0, 0), (0, 0), (0, EXTRA - 1 - self.rows_per), (0, c - self.w2)))
        pieces = self.dc // self.c
        down = ffn[0, 0, d:].reshape(npa, self.dr, npb, pieces, self.c).transpose(2, 0, 3, 1, 4)
        down = down.reshape(npb, npa, pieces * self.dr, self.c)
        return jnp.concatenate([main, vec, bup], axis=2), jnp.concatenate([blocks(ffn[0, 0, :d], self.r), down], axis=2)

    def unpack(self, attn, ffn):
        r = self.r
        attn, ffn = jnp.stack(attn), jnp.stack(ffn)
        down = ffn[:, r:]
        down = jnp.concatenate([down[:, j * self.dr : (j + 1) * self.dr] for j in range(self.dc // self.c)], axis=2)
        return (attn[:, :r, : self.wq], attn[:, :r, self.wq :], ffn[:, :r], jnp.swapaxes(down, 1, 2),
                attn[:, r : r + self.rows_per, : self.w1], attn[:, r + self.rows_per, : self.w2])


BOTH = ("pb", "pa")
BITS = {"core": 8, "y": 16, "z1": 2, "z2": 4, "z3": 6, "x": 1, "xy": 17}


def swap(block, way):
    return lax.ppermute(block, BOTH, [(i, i ^ BITS[way]) for i in range(32)])


class Gather:
    def __init__(self, block, ways):
        self.held, self.ways = [block], ways

    def after(self, *others):
        late = [held for other in others for held in other.held]
        self.held = list(lax.optimization_barrier((tuple(self.held), tuple(late)))[0])

    def step(self, stage):
        if stage == 0:
            block = self.held[0]
            self.held = [jnp.stack([block] + [swap(block, way) for way in ("z1", "z2", "z3")])]
        else:
            way = self.ways[stage - 1] if stage < 3 else "core"
            self.held = self.held + [swap(part, way) for part in self.held]


def gather_heads(block):
    near = jnp.stack([block] + [swap(block, way) for way in ("z1", "z2", "z3")])
    wide = jnp.stack([near] + [swap(near, way) for way in ("x", "y", "xy")])
    return jnp.stack([wide, swap(wide, "core")]).reshape((-1,) + block.shape)


HEAD_ORDER = [c ^ s ^ z for c in (0, 8) for s in (0, 1, 16, 17) for z in (0, 2, 4, 6)]


class Scatter:
    def __init__(self, keep, send, ways):
        self.terms, self.ways = [(keep, ()), (send, ())], ways

    def newest(self, line, count):
        arrays, spots = zip(*self.terms)
        fresh = line.wait(arrays[-count:])
        self.terms = list(zip(arrays[:-count] + tuple(fresh), spots))

    def sum(self, *pick):
        return sum(array[spot + pick].astype(F32) for array, spot in self.terms)

    def step(self, stage, line):
        if stage == 0:
            self.terms = [self.terms[0], (swap(self.terms[1][0], "core"), ())]
            return
        self.newest(line, 1)
        ways = (self.ways[stage - 1],) if stage < 3 else ("z1", "z2", "z3")
        parts = [self.sum(j).astype(BF16) for j in range(1, len(ways) + 1)]
        line.mark(parts)
        self.terms = [(array, spot + (0,)) for array, spot in self.terms] + [
            (swap(part, way), ()) for part, way in zip(parts, ways)]

    def total(self, line):
        self.newest(line, 3)
        return line.mark(self.sum())


class Line:
    def __init__(self):
        self.last = None

    def wait(self, operands):
        if self.last is None:
            return operands
        return lax.optimization_barrier((operands, self.last))[0]

    def mark(self, result):
        self.last = jax.tree.leaves(result)[0]
        return result

    def run(self, step, *operands):
        return self.mark(step(*self.wait(operands)))


def body(questions, passages, cot_questions, cot_passages, question_lengths, segment_lengths, positives, w_qkv, w_out, w_up,
         w_down, norm_bias, bias_up):
    q_count, q_len, d = questions.shape
    row_count, row_len, _ = passages.shape
    segs = segment_lengths.shape[1]
    npb, npa = lax.axis_size("pb"), lax.axis_size("pa")
    size = Blocks(npb, npa, d, bias_up.shape[1] * npb * npa)
    dims = size.dims
    near = size.direct and (npb, npa) == (4, 8)
    pb, pa = lax.axis_index("pb"), lax.axis_index("pa")
    device = pb * npa + pa
    here = jnp.stack([pb // 2, pb % 2, pa // 2, pa % 2]).astype(jnp.int32)
    order = (("y", "x"), ("x", "y"))

    attn_pack, ffn_pack = size.pack(w_qkv, w_out, w_up, w_down, norm_bias, bias_up)
    mesh_order = Place(dims[0], dims[1], None, False)
    one_array = FfnPlace(mesh_order)
    if near:
        ffn_all = lax.all_gather(ffn_pack, BOTH, axis=0).reshape((npb, npa) + ffn_pack.shape)
        parts = [Gather(attn_pack[e], order[e]) for e in range(2)]
        for stage in range(4):
            for each in parts:
                each.step(stage)
        attn_w = [each.held for each in parts]
        attn_into = [Place(npb, npa, order[e][0], True) for e in range(2)]
        ffn_w = [[ffn_all]] * 2
        ffn_into = [FfnPlace(mesh_order, e=e) for e in range(2)]
    else:
        attn_all = lax.all_gather(attn_pack, BOTH, axis=0).reshape((npb, npa) + attn_pack.shape)
        ffn_all = lax.all_gather(ffn_pack, BOTH, axis=0).reshape((npb, npa) + ffn_pack.shape)
        attn_w, ffn_w = zip(*[size.from_blocks(attn_all[:, :, e], ffn_all[:, :, e]) for e in range(2)])
        attn_w = [[blocks] for blocks in attn_w]
        ffn_w = [[blocks] for blocks in ffn_w]
        attn_into = [mesh_order] * 2
        ffn_into = [one_array] * 2

    per_row = ROW // q_len
    q_rows = q_count // per_row
    token = jnp.arange(ROW, dtype=jnp.int32)
    q_seg = jnp.broadcast_to(token // q_len, (q_rows, ROW))
    q_valid = (token % q_len)[None, :] < jnp.repeat(question_lengths.reshape(q_rows, per_row), q_len, axis=1)
    starts = jnp.cumsum(segment_lengths, axis=1) - segment_lengths
    p_seg = jnp.sum((token[None, None, :] >= starts[:, :, None]).astype(jnp.int32), axis=1)
    segr = (jnp.stack([q_seg, jnp.where(q_valid, q_seg, -1)], axis=1), jnp.stack([p_seg, p_seg], axis=1))
    segc = tuple(jnp.swapaxes(pair, 1, 2) for pair in segr)
    spots = (jnp.broadcast_to(jnp.arange(per_row, dtype=jnp.int32) * q_len, (q_rows, per_row)), starts)
    xs = (questions.reshape(-1, d), passages.reshape(-1, d))
    cots = [cot_questions.reshape(-1, d), cot_passages.reshape(-1, d)]
    p_count = row_count * segs

    def by_step(spots):
        rows = FFN_ROW // ROW
        base = jnp.arange(spots.shape[0], dtype=jnp.int32) % rows * ROW
        return (spots + base[:, None]).reshape(-1, rows * spots.shape[1])

    spots = tuple(by_step(each) for each in spots)
    own_hits = lax.dynamic_slice_in_dim(positives, pa * q_count, q_count)
    code = jnp.pad(jnp.stack([own_hits // 256, own_hits % 256], axis=1).astype(BF16), ((0, 0), (0, d - 2)))
    listed = device ^ jnp.array(HEAD_ORDER, jnp.int32) if near else jnp.arange(npb * npa, dtype=jnp.int32)
    ids = (listed[:, None] * p_count + jnp.arange(p_count, dtype=jnp.int32)[None, :]).reshape(1, -1)
    own_ids = device * p_count + jnp.arange(p_count, dtype=jnp.int32)[None, :]

    line = Line()
    half = [
        line.run(lambda x, *packs, e=e: attn_fwd(dims, attn_into[e], here, packs, x, segc[e], segr[e]), xs[e], *attn_w[e])
        for e in range(2)
    ]
    done = [None, None]
    for e in (0, 1):
        done[e] = line.run(
            lambda *packs, e=e: ffn_fwd(ffn_into[e], here, spots[e], packs, half[e][2], half[e][6], half[e][7]), *ffn_w[e])
    own = jnp.concatenate([done[1][5].reshape(p_count, d).astype(BF16), done[0][5].reshape(q_count, d).astype(BF16), code])
    heads = gather_heads(own) if near else lax.all_gather(own, BOTH, axis=0)
    losses, gq, gp = loss_part(ids, own_ids, heads, own[None], q_count, p_count)
    gcls = tuple(grad.reshape(each.shape + (d,)) for grad, each in zip((gq, gp), spots))

    def ffn_step(e, goal, cot):
        _, _, xhat, inv1, _, _, vec, bup = half[e]
        act, slope, norm2, inv2, _, _ = done[e]
        dh, *blocks, gvec, gbup = ffn_bwd(ffn_into[e], goal, here, spots[e], ffn_w[e], cot, gcls[e], norm2,
                                          inv2, act, slope, xhat, inv1, vec, bup.shape)
        return dh, blocks, gvec, gbup

    def attn_rows(e, first, last, dh, gvec, before):
        return attn_bwd(first, last, dh, half[e][0], segc[e], segr[e], half[e][5], gvec, before)

    def attn_weights(e, goals, rows, gbup):
        return attn_grad(dims, goals, here, xs[e], half[e][1], rows[0], rows[1], rows[2], gbup)

    def scatter(blocks):
        flat = blocks.reshape((npb * npa,) + blocks.shape[2:])
        return lax.psum_scatter(flat, BOTH, scatter_dimension=0, tiled=False).astype(F32)

    counts = (q_rows, row_count)
    if near:
        whole_block = attn_pack.shape[1]
        cut = whole_block // 32 * 16 + 16
        out_place = {way[0]: Place(npb, npa, way[0], False) for way in order}
        line = Line()
        dh_q, blocks_q, gvec_q, gbup_q = line.run(lambda cot: ffn_step(0, one_array, cot), cots[0])
        sum_q = scatter(blocks_q[0])
        dh_p, blocks_p, gvec_p, gbup_p = line.run(lambda cot: ffn_step(1, FfnPlace(out_place["y"]), cot), cots[1])
        ffn_p = Scatter(*blocks_p, order[0])
        ffn_p.step(0, line)

        rows_q = line.run(lambda dh: attn_rows(0, 0, q_rows, dh, gvec_q, None), dh_q)
        ffn_p.step(1, line)
        got = line.run(lambda *rows: attn_weights(0, [(out_place["x"], 0, whole_block)], rows, gbup_q), *rows_q)
        attn_q = Scatter(*got, order[1])
        attn_q.step(0, line)
        middle = row_count // 2
        rows_p = line.run(lambda dh: attn_rows(1, 0, middle, dh, gvec_p, None), dh_p)
        attn_q.step(1, line)
        rows_p = line.run(lambda *rows: attn_rows(1, middle, row_count, dh_p, rows[2], rows[:2]), *rows_p)
        goals = [(out_place["y"], 0, cut), (out_place["x"], cut, whole_block)]
        got = line.run(lambda *rows: attn_weights(1, goals, rows, gbup_p), *rows_p)
        attn_p = [Scatter(*got[:2], order[0]), Scatter(*got[2:], order[1])]
        for each in attn_p:
            each.step(0, line)
        ffn_p.step(2, line)
        attn_q.step(2, line)
        gx_q = line.run(lambda proj: input_grad(proj, half[0][4], dh_q), rows_q[0])
        for each in attn_p:
            each.step(1, line)
        gx_p = line.run(lambda proj: input_grad(proj, half[1][4], dh_p), rows_p[0])
        gx = (gx_q, gx_p)
        ffn_p.step(3, line)
        attn_q.step(3, line)
        for stage in (2, 3):
            for each in attn_p:
                each.step(stage, line)
        sums = [each.total(line) for each in [ffn_p, attn_q] + attn_p]
        ffn_sum = [sum_q, sums[0]]
        attn_sum = [sums[1], jnp.concatenate(sums[2:])]
    else:
        pairs, gx = [], []
        for e in range(2):
            dh, blocks, gvec, gbup = ffn_step(e, one_array, cots[e])
            rows = attn_rows(e, 0, counts[e], dh, gvec, None)
            got = attn_weights(e, [(mesh_order, 0, dims[2] + EXTRA)], rows, gbup)
            pairs.append(size.to_blocks(got[0], blocks[0]))
            gx.append(input_grad(rows[0], half[e][4], dh))
        attn_sum = [scatter(pair[0]) for pair in pairs]
        ffn_sum = [scatter(pair[1]) for pair in pairs]
    outs = size.unpack(attn_sum, ffn_sum)
    return (
        done[0][4].reshape(questions.shape),
        done[1][4].reshape(passages.shape),
        losses[:, 0],
        gx[0].reshape(questions.shape),
        gx[1].reshape(passages.shape),
    ) + outs


def solution(mesh):
    rows = P(BOTH, None, None)
    shard = P(None, "pb", "pa")
    vector = P(None, BOTH)
    in_specs = (rows, rows, rows, rows, P(BOTH), P(BOTH, None), P("pb"), shard, shard, shard, shard, shard, vector)
    out_specs = (rows, rows, P(BOTH), rows, rows, shard, shard, shard, shard, shard, vector)
    return jax.shard_map(body, mesh=mesh, in_specs=in_specs, out_specs=out_specs, check_vma=False)
```

time: 847 us -> 526 us (0.62)
  waiting for transfers between devices: 540 us -> 165 us
  starting transfers between devices: 0.25 us -> 64.6 us
  local copies, waits for them, and re-layouts: 41.1 us -> 7.5 us
  Pallas kernels: 197 us -> 215 us
  other arithmetic: 40.2 us -> 49.3 us
    reduce_scatter x3 -> x1, waiting for transfers between devices: 333 us -> 0.01 us  [scatter(): lax.psum_scatter(flat, BOTH, scatter_dimension=0, tiled=False).astype(F32)]
    ppermute x0 -> x51, waiting for transfers between devices: none -> 146 us  [swap(): return lax.ppermute(block, BOTH, [(i, i ^ BITS[way]) for i in range(32)])]
    all_gather x2 -> x0, waiting for transfers between devices: 126 us -> none  [the longest x1 81.4 us: body(): lax.all_gather(attn_pack, BOTH, axis=0)]
    ppermute x0 -> x51, starting transfers between devices: none -> 64.6 us  [swap(): return lax.ppermute(block, BOTH, [(i, i ^ BITS[way]) for i in range(32)])]
    all_gather x1, waiting for transfers between devices: 80.6 us -> 18.6 us  [body(): lax.all_gather(ffn_pack, BOTH, axis=0).reshape((npb, npa) + ffn_pack.shape)]
    convert_element_type x2 -> x14, other arithmetic: 1.56 us -> 31.8 us  [the longest x12 30.3 us: step(): parts = [self.sum(j).astype(BF16) for j in range(1, len(ways) + 1)]]
    squeeze x2 -> x0, local copies, waits for them, and re-layouts: 23.5 us -> none  [the longest x1 14.6 us: body(): ffn_all[:, :, e]]
    another operation x5 -> x17, other arithmetic: 28 us -> 6.12 us  [the longest x7 3.75 us: unpack(): attn, ffn = (jnp.stack(attn), jnp.stack(ffn))]
  transfers between devices with their start and end apart: 6 -> 53, of which waited for: 6 -> 26; matrix products, arithmetic and copies ran while one was open for 5% -> 9% of each run, Pallas kernels for 12% -> 22%
where the time goes in v2:
time: 526 us; the launch traced here: 516 us
  Pallas kernels  215 us (41%)
  waiting for transfers between devices  165 us (31%)
  starting transfers between devices  64.6 us (12%)
  other arithmetic  49.3 us (9%)
  between operations  15.1 us (3%)
  local copies, waits for them, and re-layouts  7.5 us (1%)
    ppermute x51, waiting for transfers between devices, swap(): return lax.ppermute(block, BOTH, [(i, i ^ BITS[way]) for i in range(32)])  146 us
    ppermute x51, starting transfers between devices, swap(): return lax.ppermute(block, BOTH, [(i, i ^ BITS[way]) for i in range(32)])  64.6 us
    pallas_call x2, Pallas kernels, ffn_bwd(): pl.pallas_call(functools.partial(ffn_bwd_kernel, place, goal, steps), gri...  62.3 us
    pallas_call x3, Pallas kernels, attn_bwd(): pl.pallas_call(kernel, grid=(last - first,), in_specs=[row(d), row(3 * d)...  42.3 us
    pallas_call x2, Pallas kernels, attn_fwd(): pl.pallas_call(functools.partial(attn_fwd_kernel, dims, place), grid=(ste...  35.9 us
    pallas_call x2, Pallas kernels, ffn_fwd(): pl.pallas_call(functools.partial(ffn_fwd_kernel, place), grid=(steps,), i...  35.3 us
    convert_element_type x12, other arithmetic, step(): parts = [self.sum(j).astype(BF16) for j in range(1, len(ways) + 1)]  30.3 us
    pallas_call x2, Pallas kernels, attn_grad(): pl.pallas_call(functools.partial(attn_grad_kernel, dims, goals), grid=(4,...  20.2 us
  transfers between devices with their start and end apart: 53, of which 26 were waited for; matrix products, arithmetic and copies ran while one was open for 9% of the time, Pallas kernels for 22%

profile of v2, /device:TPU:0, one launch (start us, length us, event | category | flops | bytes accessed | tf_op | source)
XLA Modules:
  0.0 516.1 jit_solution(17490273213116982011)
XLA Ops:
  8.3 1.8 pad_maximum_fusion.5
  10.5 5.1 collective-permute-start.12
  16.3 4.4 collective-permute-done.12
  20.7 16.0 %collective-permute-done.11 = bf16[208,384]{1,0:T(8,128)(2,1)S(1)} collective-permute-done((bf16[208,384]{1,0:T(8,128)(2,1)S(1)}, bf16[208,384]{1,0:T(8,128)(2,1)S(1)}, u32[]{:S(2)}, u32[]{:S(2)}) %collective-permute-start.11) | collective-permute-done | bytes 159776 | tf_op jit(solution)/shard_map/ppermute | solution.py:693
  36.8 2.4 collective-permute-start.13
  39.2 8.1 %collective-permute-start.2 = (bf16[208,384]{1,0:T(8,128)(2,1)S(1)}, bf16[208,384]{1,0:T(8,128)(2,1)S(1)}, u32[]{:S(2)}, u32[]{:S(2)}) collective-permute-start(bf16[208,384]{1,0:T(8,128)(2,1)S(1)} %get-tuple-element.236), channel_id=1, source_target_pairs={{0,6},{1,7},{2,4},{3,5},{4,2},{5,3},{6,0},{7,1},{8,14},{9,15},{10,... | collective-permute-start | bytes 479240 | tf_op jit(solution)/shard_map/ppermute | solution.py:693
  47.8 2.8 collective-permute-done.2
  51.9 3.6 collective-permute-done.1
  55.7 1.6 collective-permute-start.3
  58.2 1.5 collective-permute-start.4
  59.7 17.6 %collective-permute-done.14.refs_2_ = bf16[4,208,384]{2,1,0:T(8,128)(2,1)} collective-permute-done((bf16[4,208,384]{2,1,0:T(8,128)(2,1)S(1)}, bf16[4,208,384]{2,1,0:T(8,128)(2,1)}, u32[]{:S(2)}, u32[]{:S(2)}) %collective-permute-start.14) | collective-permute-done | bytes 639008 | tf_op jit(solution)/shard_map/ppermute | solution.py:693
  77.3 21.2 %collective-permute-done.3.refs_1_ = bf16[4,208,384]{2,1,0:T(8,128)(2,1)S(1)} collective-permute-done((bf16[4,208,384]{2,1,0:T(8,128)(2,1)S(1)}, bf16[4,208,384]{2,1,0:T(8,128)(2,1)S(1)}, u32[]{:S(2)}, u32[]{:S(2)}) %collective-permute-start.3) | collective-permute-done | bytes 639008 | tf_op jit(solution)/shard_map/ppermute | solution.py:693
  100.3 8.6 %collective-permute-done.15.refs_3_ = bf16[4,208,384]{2,1,0:T(8,128)(2,1)} collective-permute-done((bf16[4,208,384]{2,1,0:T(8,128)(2,1)S(1)}, bf16[4,208,384]{2,1,0:T(8,128)(2,1)}, u32[]{:S(2)}, u32[]{:S(2)}) %collective-permute-start.15) | collective-permute-done | bytes 639008 | tf_op jit(solution)/shard_map/ppermute | solution.py:693
  113.1 14.3 %attn_fwd.2 = (bf16[512,2304]{1,0:T(8,128)(2,1)}, bf16[512,768]{1,0:T(8,128)(2,1)}, f32[512,768]{1,0:T(8,128)}, f32[512,1]{1,0:T(8,128)}, bf16[768,2304]{1,0:T(8...) custom-call(s32[4]{0:T(128)} %pad_add_fusion.2.here_ref, ...), custom_call_target="tpu_custom_call" | custom-call | flops 4026531840 | bytes 41943040 | tf_op jit(solution)/shard_map/attn_fwd/pallas_call | solution.py:153
  127.5 21.6 %attn_fwd.3 = (bf16[1024,2304]{1,0:T(8,128)(2,1)}, bf16[1024,768]{1,0:T(8,128)(2,1)}, f32[1024,768]{1,0:T(8,128)}, f32[1024,1]{1,0:T(8,128)}, bf16[768,2304]{1,0...) custom-call(s32[4]{0:T(128)} %pad_add_fusion.2.here_ref, ...), custom_call_target="tpu_custom_call" | custom-call | flops 8053063680 | bytes 41943040 | tf_op jit(solution)/shard_map/attn_fwd/pallas_call | solution.py:153
  149.1 18.6 %all-gather.3.cloned.1.call-done = bf16[64,384,384]{2,1,0:T(8,128)(2,1)} async-done(((bf16[2,384,384]{2,1,0:T(8,128)(2,1)}), bf16[64,384,384]{2,1,0:T(8,128)(2,1)}) %all-gather.3.cloned.1.call-update) | async-done | bytes 18874384 | tf_op jit(solution)/shard_map/all_gather | solution.py:785
  168.3 13.2 %ffn_fwd.2 = (bf16[512,3072]{1,0:T(8,128)(2,1)}, bf16[512,3072]{1,0:T(8,128)(2,1)}, f32[512,768]{1,0:T(8,128)}, f32[512,1]{1,0:T(8,128)}, bf16[512,768]{1,0:T(8,128)(2,1)}, /*index=5*/f32[2,4,768]{2,1,0:T(4,128)}) custom-call(s32[4]{0:T(128)} %pad_add_fusion.2.here_ref, s32[2,4]{1,0:T(2,128)} %broadcast_in_dim.12.spot_ref, ...), custom_call_target="tpu_custom_call" | custom-call | flops 4831838208 | bytes 41943040 | tf_op jit(solution)/shard_map/ffn_fwd/pallas_call | solution.py:272
  182.3 22.1 %ffn_fwd.3 = (bf16[1024,3072]{1,0:T(8,128)(2,1)}, bf16[1024,3072]{1,0:T(8,128)(2,1)}, f32[1024,768]{1,0:T(8,128)}, f32[1024,1]{1,0:T(8,128)}, bf16[1024,768]{1,0:T(8,128)(2,1)}, /*index=5*/f32[4,4,768]{2,1,0:T(4,128)}) custom-call(s32[4]{0:T(128)} %pad_add_fusion.2.here_ref, s32[4,4]{1,0:T(4,128)} %copy-done.9, bf16[4,8,2,384,384]{4,3,2,1,0:T(8,128)(2,1)} %bitcast.212, ...), custom_call_target="tpu_custom_call" | custom-call | flops 9663676416 | bytes 41943040 | tf_op jit(solution)/shard_map/ffn_fwd/pallas_call | solution.py:272
  205.3 1.6 collective-permute-start.21
  207.3 2.4 collective-permute-start.22
  211.3 1.9 collective-permute-done.22
  213.3 1.7 collective-permute-start.24
  214.9 1.6 collective-permute-start.23
  216.8 3.4 collective-permute-done.24
  220.3 2.3 collective-permute-done.23
  222.6 2.0 collective-permute-done.25
  228.3 3.7 loss_part.1
  234.8 23.9 %ffn_bwd.2 = (f32[512,768]{1,0:T(8,128)}, bf16[4,8,384,384]{3,2,1,0:T(8,128)(2,1)}, f32[8,768]{1,0:T(8,128)}, f32[4,768]{1,0:T(4,128)}) custom-call(s32[4]{0:T(128)} %pad_add_fusion.2.here_ref, s32[2,4]{1,0:T(2,128)} %broadcast_in_dim.12.spot_ref, bf16[4,8,2,384,384]{4,3,2,1,0:T(8,128)(2,1)} %bitcast.213, bf16[512,768]{1,0:T(8,128)(2,1)} %bitcast.244, ...), custom_call_target="tpu_custom_call" | custom-call | flops 9663676416 | bytes 62914560 | tf_op jit(solution)/shard_map/ffn_bwd/pallas_call | solution.py:438
  258.7 38.4 %ffn_bwd.3 = (f32[1024,768]{1,0:T(8,128)}, bf16[2,2,4,384,384]{4,3,2,1,0:T(8,128)(2,1)}, bf16[2,2,4,384,384]{4,3,2,1,0:T(8,128)(2,1)}, f32[8,768]{1,0:T(8,128)}, f32[4,768]{1,0:T(4,128)}) custom-call(s32[4]{0:T(128)} %pad_add_fusion.2.here_ref, s32[4,4]{1,0:T(4,128)} %copy-done.9, bf16[4,8,2,384,384]{4,3,2,1,0:T(8,128)(2,1)} %bitcast.214, ...), custom_call_target="tpu_custom_call" | custom-call | flops 19327352832 | bytes 62914560 | tf_op jit(solution)/shard_map/ffn_bwd/pallas_call | solution.py:438
  297.4 14.0 %attn_bwd.3 = (bf16[512,2304]{1,0:T(8,128)(2,1)}, bf16[512,768]{1,0:T(8,128)(2,1)}, f32[8,768]{1,0:T(8,128)}) custom-call(f32[512,768]{1,0:T(8,128)} %get-tuple-element.154.refs_0_.dh_ref, bf16[512,2304]{1,0:T(8,128)(2,1)} %get-tuple-element.115.refs_1_, bf16[768,768]{1,0:T(8,128)(2,1)} %get-tuple-element.155.refs_2_, s32[2,256,2]{2,1,0:T(8,128)} %copy.50.refs_9_.refs_3_, ...), custom_call_target="tpu_custom_call" | custom-call | flops 4630511616 | bytes 8388608 | tf_op jit(solution)/shard_map/attn_bwd/pallas_call | solution.py:507
  311.3 4.6 fusion
  315.9 8.5 %attn_grad.2 = (bf16[2,2,4,208,384]{4,3,2,1,0:T(8,128)(2,1)}, bf16[2,2,4,208,384]{4,3,2,1,0:T(8,128)(2,1)}) custom-call(s32[4]{0:T(128)} %pad_add_fusion.2.here_ref, bf16[512,768]{1,0:T(8,128)(2,1)} %bitcast.246, bf16[512,768]{1,0:T(8,128)(2,1)} %get-tuple-element.158.att_ref, bf16[512,2304]{1,0:T(8,128)(2,1)} %get-tuple-element.191.proj_ref, ...), custom_call_target="tpu_custom_call" | custom-call | flops 2415919104 | bytes 16777216 | tf_op jit(solution)/shard_map/attn_grad/pallas_call | solution.py:587
  324.9 1.6 collective-permute-start.30
  326.5 14.4 %attn_bwd.4 = (bf16[1024,2304]{1,0:T(8,128)(2,1)}, bf16[1024,768]{1,0:T(8,128)(2,1)}, f32[8,768]{1,0:T(8,128)}) custom-call(f32[1024,768]{1,0:T(8,128)} %get-tuple-element.170.refs_0_.dh_ref, bf16[1024,2304]{1,0:T(8,128)(2,1)} %get-tuple-element.125.refs_1_, bf16[768,768]{1,0:T(8,128)(2,1)} %get-tuple-element.171.refs_2_, ...), custom_call_target="tpu_custom_call" | custom-call | flops 4630511616 | bytes 8388608 | tf_op jit(solution)/shard_map/attn_bwd/pallas_call | solution.py:507
  340.9 2.7 fusion.2
  344.9 14.0 %attn_bwd.5 = (bf16[1024,2304]{1,0:T(8,128)(2,1)}, bf16[1024,768]{1,0:T(8,128)(2,1)}, f32[8,768]{1,0:T(8,128)}) custom-call(f32[1024,768]{1,0:T(8,128)} %get-tuple-element.170.refs_0_.dh_ref, bf16[1024,2304]{1,0:T(8,128)(2,1)} %get-tuple-element.125.refs_1_, ...), custom_call_target="tpu_custom_call", output_to_operand_aliasing={{0}: (6, {}), {1}: (7, {})} | custom-call | flops 4630511616 | bytes 8388608 | tf_op jit(solution)/shard_map/attn_bwd/pallas_call | solution.py:507
  358.9 11.7 %attn_grad.3 = (bf16[2,2,4,112,384]{4,3,2,1,0:T(8,128)(2,1)}, bf16[2,2,4,112,384]{4,3,2,1,0:T(8,128)(2,1)}, bf16[2,2,4,96,384]{4,3,2,1,0:T(8,128)(2,1)}, bf16[2,2,4,96,384]{4,3,2,1,0:T(8,128)(2,1)}) custom-call(s32[4]{0:T(128)} %pad_add_fusion.2.here_ref, bf16[1024,768]{1,0:T(8,128)(2,1)} %bitcast.243, bf16[1024,768]{1,0:T(8,128)(2,1)} %get-tuple-element.175.att_ref, ...), custom_call_target="tpu_custom_call" | custom-call | flops 4831838208 | bytes 16777216 | tf_op jit(solution)/shard_map/attn_grad/pallas_call | solution.py:587
  371.2 20.7 %collective-permute-done.30 = bf16[2,4,384,384]{3,2,1,0:T(8,128)(2,1)} collective-permute-done((bf16[2,4,384,384]{3,2,1,0:T(8,128)(2,1)}, bf16[2,4,384,384]{3,2,1,0:T(8,128)(2,1)}, u32[]{:S(2)}, u32[]{:S(2)}) %collective-permute-start.30) | collective-permute-done | bytes 2359328 | tf_op jit(solution)/shard_map/ppermute | solution.py:693
  391.9 3.4 fusion.1
  395.4 2.2 collective-permute-start.34
  397.6 2.4 fusion.3
  401.3 5.7 %input_grad.2 = f32[512,768]{1,0:T(8,128)} custom-call(bf16[512,2304]{1,0:T(8,128)(2,1)} %get-tuple-element.191.proj_ref, bf16[768,2304]{1,0:T(8,128)(2,1)} %get-tuple-element.192.weight_ref, f32[512,768]{1,0:T(8,128)} %get-tuple-element.154.refs_0_.dh_ref), custom_call_target="tpu_custom_call" | custom-call | flops 1811939328 | bytes 16777216 | tf_op jit(solution)/shard_map/input_grad/pallas_call | solution.py:611
  407.1 2.5 fusion.4
  409.6 2.0 fusion.10
  412.6 9.4 %input_grad.3 = f32[1024,768]{1,0:T(8,128)} custom-call(bf16[1024,2304]{1,0:T(8,128)(2,1)} %get-tuple-element.198.proj_ref, bf16[768,2304]{1,0:T(8,128)(2,1)} %get-tuple-element.199.weight_ref, f32[1024,768]{1,0:T(8,128)} %get-tuple-element.170.refs_0_.dh_ref), custom_call_target="tpu_custom_call" | custom-call | flops 3623878656 | bytes 16777216 | tf_op jit(solution)/shard_map/input_grad/pallas_call | solution.py:611
  422.1 7.0 %collective-permute-done.34 = bf16[4,384,384]{2,1,0:T(8,128)(2,1)} collective-permute-done((bf16[4,384,384]{2,1,0:T(8,128)(2,1)}, bf16[4,384,384]{2,1,0:T(8,128)(2,1)}, u32[]{:S(2)}, u32[]{:S(2)}) %collective-permute-start.34) | collective-permute-done | bytes 1179680 | tf_op jit(solution)/shard_map/ppermute | solution.py:693
  429.0 3.3 fusion.15
  432.3 2.4 fusion.23
  434.7 2.3 collective-permute-done.42
  437.0 2.2 fusion.5
  439.7 2.0 fusion.14
  441.6 1.7 collective-permute-start.43
  444.0 1.8 collective-permute-start.40
  445.8 1.7 collective-permute-start.39
  450.3 2.6 collective-permute-start.37
  454.3 10.3 %collective-permute-done.40 = bf16[384,384]{1,0:T(8,128)(2,1)S(1)} collective-permute-done((bf16[384,384]{1,0:T(8,128)(2,1)}, bf16[384,384]{1,0:T(8,128)(2,1)S(1)}, u32[]{:S(2)}, u32[]{:S(2)}) %collective-permute-start.40) | collective-permute-done | bytes 294944 | tf_op jit(solution)/shard_map/ppermute | solution.py:693
  464.5 9.6 %collective-permute-start.36 = (bf16[208,384]{1,0:T(8,128)(2,1)S(1)}, bf16[208,384]{1,0:T(8,128)(2,1)S(1)}, u32[]{:S(2)}, u32[]{:S(2)}) collective-permute-start(bf16[208,384]{1,0:T(8,128)(2,1)S(1)} %copy-done.7), channel_id=1, source_target_pairs={{0,4},{1,5},{2,6},{3,7},{4,0},{5,1},{6,2},{7,3},{8,12},{9,13},{10,... | collective-permute-start | bytes 479240 | tf_op jit(solution)/shard_map/ppermute | solution.py:693
  474.1 11.0 %collective-permute-done.39 = bf16[384,384]{1,0:T(8,128)(2,1)S(1)} collective-permute-done((bf16[384,384]{1,0:T(8,128)(2,1)}, bf16[384,384]{1,0:T(8,128)(2,1)S(1)}, u32[]{:S(2)}, u32[]{:S(2)}) %collective-permute-start.39) | collective-permute-done | bytes 294944 | tf_op jit(solution)/shard_map/ppermute | solution.py:693
  485.1 2.0 collective-permute-start.48
  487.1 1.5 fusion.19
  488.6 1.4 collective-permute-start.47
  490.1 3.9 collective-permute-done.36
  495.9 2.3 collective-permute-start.49
  498.2 2.3 collective-permute-done.46
  (164 shorter events, 42.4 us)
Async XLA Ops:
  7.2 160.6 %all-gather.3.cloned.1.call-start = ((), (), s32[]{:S(2)}) async-start(), calls=%async_computation.2 | async-start | bytes 19464192 | tf_op jit(solution)/shard_map/all_gather | solution.py:785
  10.2 495.7 %reduce-scatter.2.cloned.1.call-start = ((), (), s32[]{:S(2)}) async-start(), calls=%async_computation.1 | async-start | bytes 9732096 | tf_op jit(solution)/shard_map/reduce_scatter | solution.py:858
  10.4 46.8 %copy-start.17 = (s32[8]{0:T(128)S(1)}, s32[8]{0:T(128)}, u32[]{:S(2)}) copy-start(s32[8]{0:T(128)} %param.18) | copy-start | bytes 100
  10.4 46.9 %copy-start.10 = (s32[4,4]{1,0:T(4,128)S(1)}, s32[4,4]{1,0:T(4,128)}, u32[]{:S(2)}) copy-start(s32[4,4]{1,0:T(4,128)} %param.19) | copy-start | bytes 196
  10.5 98.5 %copy-start.13 = (s32[64]{0:T(128)S(1)}, s32[64]{0:T(128)}, u32[]{:S(2)}) copy-start(s32[64]{0:T(128)} %param.20) | copy-start | bytes 772
  10.5 10.2 %collective-permute-start.12 = (bf16[208,384]{1,0:T(8,128)(2,1)S(1)}, bf16[208,384]{1,0:T(8,128)(2,1)S(1)}, u32[]{:S(2)}, u32[]{:S(2)}) collective-permute-start(bf16[208,384]{1,0:T(8,128)(2,1)S(1)} %get-tuple-element.237), channel_id=1, source_target_pairs={{0,6},{1,7},{2,4},{3,5},{4,2},{5,3},{6,0},{7,1},{8,14},{9,15},{10,... | collective-permute-start | bytes 479240 | tf_op jit(solution)/shard_map/ppermute | solution.py:693
  15.6 21.0 %collective-permute-start.11 = (bf16[208,384]{1,0:T(8,128)(2,1)S(1)}, bf16[208,384]{1,0:T(8,128)(2,1)S(1)}, u32[]{:S(2)}, u32[]{:S(2)}) collective-permute-start(bf16[208,384]{1,0:T(8,128)(2,1)S(1)} %get-tuple-element.237), channel_id=1, source_target_pairs={{0,4},{1,5},{2,6},{3,7},{4,0},{5,1},{6,2},{7,3},{8,12},{9,13},{10,... | collective-permute-start | bytes 479240 | tf_op jit(solution)/shard_map/ppermute | solution.py:693
  15.6 21.0 %collective-permute-start.10 = (bf16[208,384]{1,0:T(8,128)(2,1)S(1)}, bf16[208,384]{1,0:T(8,128)(2,1)S(1)}, u32[]{:S(2)}, u32[]{:S(2)}) collective-permute-start(bf16[208,384]{1,0:T(8,128)(2,1)S(1)} %get-tuple-element.237), channel_id=1, source_target_pairs={{0,2},{1,3},{2,0},{3,1},{4,6},{5,7},{6,4},{7,5},{8,10},{9,11},{10,... | collective-permute-start | bytes 479240 | tf_op jit(solution)/shard_map/ppermute | solution.py:693
  36.8 76.3 %copy-start.3 = (bf16[4,208,384]{2,1,0:T(8,128)(2,1)}, bf16[4,208,384]{2,1,0:T(8,128)(2,1)S(1)}, u32[]{:S(2)}) copy-start(bf16[4,208,384]{2,1,0:T(8,128)(2,1)S(1)} %pad_maximum_fusion.3.refs_0_) | copy-start | bytes 1916932
  36.8 20.9 %collective-permute-start.13 = (bf16[4,208,384]{2,1,0:T(8,128)(2,1)S(1)}, bf16[4,208,384]{2,1,0:T(8,128)(2,1)S(1)}, u32[]{:S(2)}, u32[]{:S(2)}) collective-permute-start(bf16[4,208,384]{2,1,0:T(8,128)(2,1)S(1)} %pad_maximum_fusion.3.refs_0_), channel_id=1, source_target_pairs={{0,16},{1,17},{2,18},{3,19},{4,20},{5,21},{6,22},{7,23},{8,24},{9,... | collective-permute-start | bytes 1916936 | tf_op jit(solution)/shard_map/ppermute | solution.py:693
  39.2 11.4 %collective-permute-start.2 = (bf16[208,384]{1,0:T(8,128)(2,1)S(1)}, bf16[208,384]{1,0:T(8,128)(2,1)S(1)}, u32[]{:S(2)}, u32[]{:S(2)}) collective-permute-start(bf16[208,384]{1,0:T(8,128)(2,1)S(1)} %get-tuple-element.236), channel_id=1, source_target_pairs={{0,6},{1,7},{2,4},{3,5},{4,2},{5,3},{6,0},{7,1},{8,14},{9,15},{10,... | collective-permute-start | bytes 479240 | tf_op jit(solution)/shard_map/ppermute | solution.py:693
  47.2 8.3 %collective-permute-start.1 = (bf16[208,384]{1,0:T(8,128)(2,1)S(1)}, bf16[208,384]{1,0:T(8,128)(2,1)S(1)}, u32[]{:S(2)}, u32[]{:S(2)}) collective-permute-start(bf16[208,384]{1,0:T(8,128)(2,1)S(1)} %get-tuple-element.236), channel_id=1, source_target_pairs={{0,4},{1,5},{2,6},{3,7},{4,0},{5,1},{6,2},{7,3},{8,12},{9,13},{10,... | collective-permute-start | bytes 479240 | tf_op jit(solution)/shard_map/ppermute | solution.py:693
  47.3 8.3 %collective-permute-start = (bf16[208,384]{1,0:T(8,128)(2,1)S(1)}, bf16[208,384]{1,0:T(8,128)(2,1)S(1)}, u32[]{:S(2)}, u32[]{:S(2)}) collective-permute-start(bf16[208,384]{1,0:T(8,128)(2,1)S(1)} %get-tuple-element.236), channel_id=1, source_target_pairs={{0,2},{1,3},{2,0},{3,1},{4,6},{5,7},{6,4},{7,5},{8,10},{9,11},{10,... | collective-permute-start | bytes 479240 | tf_op jit(solution)/shard_map/ppermute | solution.py:693
  47.8 11.9 %collective-permute-start.16 = (bf16[4,208,384]{2,1,0:T(8,128)(2,1)S(1)}, bf16[4,208,384]{2,1,0:T(8,128)(2,1)}, u32[]{:S(2)}, u32[]{:S(2)}) collective-permute-start(bf16[4,208,384]{2,1,0:T(8,128)(2,1)S(1)} %pad_maximum_fusion.3.refs_0_), channel_id=1, source_target_pairs={{0,8},{1,9},{2,10},{3,11},{4,12},{5,13},{6,14},{7,15},{8,0},{9,1},... | collective-permute-start | bytes 1916936 | tf_op jit(solution)/shard_map/ppermute | solution.py:693
  50.6 26.7 %collective-permute-start.14 = (bf16[4,208,384]{2,1,0:T(8,128)(2,1)S(1)}, bf16[4,208,384]{2,1,0:T(8,128)(2,1)}, u32[]{:S(2)}, u32[]{:S(2)}) collective-permute-start(bf16[4,208,384]{2,1,0:T(8,128)(2,1)S(1)} %pad_maximum_fusion.3.refs_0_), channel_id=1, source_target_pairs={{0,1},{1,0},{2,3},{3,2},{4,5},{5,4},{6,7},{7,6},{8,9},{9,8},{10,11... | collective-permute-start | bytes 1916936 | tf_op jit(solution)/shard_map/ppermute | solution.py:693
  55.7 71.8 %copy-start.4 = (bf16[4,208,384]{2,1,0:T(8,128)(2,1)}, bf16[4,208,384]{2,1,0:T(8,128)(2,1)S(1)}, u32[]{:S(2)}) copy-start(bf16[4,208,384]{2,1,0:T(8,128)(2,1)S(1)} %pad_maximum_fusion.2.refs_0_) | copy-start | bytes 1916932
  55.7 42.8 %collective-permute-start.3 = (bf16[4,208,384]{2,1,0:T(8,128)(2,1)S(1)}, bf16[4,208,384]{2,1,0:T(8,128)(2,1)S(1)}, u32[]{:S(2)}, u32[]{:S(2)}) collective-permute-start(bf16[4,208,384]{2,1,0:T(8,128)(2,1)S(1)} %pad_maximum_fusion.2.refs_0_), channel_id=1, source_target_pairs={{0,1},{1,0},{2,3},{3,2},{4,5},{5,4},{6,7},{7,6},{8,9},{9,8},{10,11... | collective-permute-start | bytes 1916936 | tf_op jit(solution)/shard_map/ppermute | solution.py:693
  57.5 69.9 %copy-start.9 = (s32[4,4]{1,0:T(4,128)}, s32[4,4]{1,0:T(4,128)S(1)}, u32[]{:S(2)}) copy-start(s32[4,4]{1,0:T(4,128)S(1)} %sub.25.spot_ref) | copy-start | bytes 196
  57.7 55.5 %copy-start.14 = (bf16[4,208,384]{2,1,0:T(8,128)(2,1)}, bf16[4,208,384]{2,1,0:T(8,128)(2,1)S(1)}, u32[]{:S(2)}) copy-start(bf16[4,208,384]{2,1,0:T(8,128)(2,1)S(1)} %collective-permute-done.13.refs_1_) | copy-start | bytes 1916932
  57.7 51.3 %collective-permute-start.15 = (bf16[4,208,384]{2,1,0:T(8,128)(2,1)S(1)}, bf16[4,208,384]{2,1,0:T(8,128)(2,1)}, u32[]{:S(2)}, u32[]{:S(2)}) collective-permute-start(bf16[4,208,384]{2,1,0:T(8,128)(2,1)S(1)} %collective-permute-done.13.refs_1_), channel_id=1, source_target_pairs={{0,1},{1,0},{2,3},{3,2},{4,5},{5,4},{6,7},{7,6},{8,9},{9,8},{10,11... | collective-permute-start | bytes 1916936 | tf_op jit(solution)/shard_map/ppermute | solution.py:693
  58.2 50.8 %collective-permute-start.4 = (bf16[4,208,384]{2,1,0:T(8,128)(2,1)S(1)}, bf16[4,208,384]{2,1,0:T(8,128)(2,1)}, u32[]{:S(2)}, u32[]{:S(2)}) collective-permute-start(bf16[4,208,384]{2,1,0:T(8,128)(2,1)S(1)} %pad_maximum_fusion.2.refs_0_), channel_id=1, source_target_pairs={{0,16},{1,17},{2,18},{3,19},{4,20},{5,21},{6,22},{7,23},{8,24},{9,... | collective-permute-start | bytes 1916936 | tf_op jit(solution)/shard_map/ppermute | solution.py:693
  59.7 50.0 %collective-permute-start.17 = (bf16[4,208,384]{2,1,0:T(8,128)(2,1)S(1)}, bf16[4,208,384]{2,1,0:T(8,128)(2,1)}, u32[]{:S(2)}, u32[]{:S(2)}) collective-permute-start(bf16[4,208,384]{2,1,0:T(8,128)(2,1)S(1)} %collective-permute-done.13.refs_1_), channel_id=1, source_target_pairs={{0,8},{1,9},{2,10},{3,11},{4,12},{5,13},{6,14},{7,15},{8,0},{9,1},... | collective-permute-start | bytes 1916936 | tf_op jit(solution)/shard_map/ppermute | solution.py:693
  77.3 32.3 %collective-permute-start.18 = (bf16[4,208,384]{2,1,0:T(8,128)(2,1)}, bf16[4,208,384]{2,1,0:T(8,128)(2,1)}, u32[]{:S(2)}, u32[]{:S(2)}) collective-permute-start(bf16[4,208,384]{2,1,0:T(8,128)(2,1)} %collective-permute-done.14.refs_2_), channel_id=1, source_target_pairs={{0,8},{1,9},{2,10},{3,11},{4,12},{5,13},{6,14},{7,15},{8,0},{9,1},... | collective-permute-start | bytes 1916936 | tf_op jit(solution)/shard_map/ppermute | solution.py:693
  98.5 29.0 %copy-start.15 = (bf16[4,208,384]{2,1,0:T(8,128)(2,1)}, bf16[4,208,384]{2,1,0:T(8,128)(2,1)S(1)}, u32[]{:S(2)}) copy-start(bf16[4,208,384]{2,1,0:T(8,128)(2,1)S(1)} %collective-permute-done.3.refs_1_) | copy-start | bytes 1916932
  98.5 11.7 %collective-permute-start.5 = (bf16[4,208,384]{2,1,0:T(8,128)(2,1)S(1)}, bf16[4,208,384]{2,1,0:T(8,128)(2,1)}, u32[]{:S(2)}, u32[]{:S(2)}) collective-permute-start(bf16[4,208,384]{2,1,0:T(8,128)(2,1)S(1)} %collective-permute-done.3.refs_1_), channel_id=1, source_target_pairs={{0,16},{1,17},{2,18},{3,19},{4,20},{5,21},{6,22},{7,23},{8,24},{9,... | collective-permute-start | bytes 1916936 | tf_op jit(solution)/shard_map/ppermute | solution.py:693
  109.0 4.2 collective-permute-start.19
  109.1 18.4 %collective-permute-start.6 = (bf16[4,208,384]{2,1,0:T(8,128)(2,1)S(1)}, bf16[4,208,384]{2,1,0:T(8,128)(2,1)}, u32[]{:S(2)}, u32[]{:S(2)}) collective-permute-start(bf16[4,208,384]{2,1,0:T(8,128)(2,1)S(1)} %pad_maximum_fusion.2.refs_0_), channel_id=1, source_target_pairs={{0,8},{1,9},{2,10},{3,11},{4,12},{5,13},{6,14},{7,15},{8,0},{9,1},... | collective-permute-start | bytes 1916936 | tf_op jit(solution)/shard_map/ppermute | solution.py:693
  109.6 17.8 %collective-permute-start.7 = (bf16[4,208,384]{2,1,0:T(8,128)(2,1)S(1)}, bf16[4,208,384]{2,1,0:T(8,128)(2,1)}, u32[]{:S(2)}, u32[]{:S(2)}) collective-permute-start(bf16[4,208,384]{2,1,0:T(8,128)(2,1)S(1)} %collective-permute-done.3.refs_1_), channel_id=1, source_target_pairs={{0,8},{1,9},{2,10},{3,11},{4,12},{5,13},{6,14},{7,15},{8,0},{9,1},... | collective-permute-start | bytes 1916936 | tf_op jit(solution)/shard_map/ppermute | solution.py:693
  109.7 17.7 %collective-permute-start.8 = (bf16[4,208,384]{2,1,0:T(8,128)(2,1)}, bf16[4,208,384]{2,1,0:T(8,128)(2,1)}, u32[]{:S(2)}, u32[]{:S(2)}) collective-permute-start(bf16[4,208,384]{2,1,0:T(8,128)(2,1)} %collective-permute-done.4.refs_2_), channel_id=1, source_target_pairs={{0,8},{1,9},{2,10},{3,11},{4,12},{5,13},{6,14},{7,15},{8,0},{9,1},... | collective-permute-start | bytes 1916936 | tf_op jit(solution)/shard_map/ppermute | solution.py:693
  110.2 17.3 %collective-permute-start.9 = (bf16[4,208,384]{2,1,0:T(8,128)(2,1)}, bf16[4,208,384]{2,1,0:T(8,128)(2,1)}, u32[]{:S(2)}, u32[]{:S(2)}) collective-permute-start(bf16[4,208,384]{2,1,0:T(8,128)(2,1)} %collective-permute-done.5.refs_3_), channel_id=1, source_target_pairs={{0,8},{1,9},{2,10},{3,11},{4,12},{5,13},{6,14},{7,15},{8,0},{9,1},... | collective-permute-start | bytes 1916936 | tf_op jit(solution)/shard_map/ppermute | solution.py:693
  205.2 19.6 %copy-start.18 = (s32[32]{0:T(128)S(1)}, s32[32]{0:T(128)}, u32[]{:S(2)}) copy-start(s32[32]{0:T(128)} %constant.136.clone) | copy-start | bytes 388
  205.3 23.1 %copy-start.5 = (bf16[1,32,768]{2,1,0:T(8,128)(2,1)}, bf16[1,32,768]{2,1,0:T(8,128)(2,1)S(1)}, u32[]{:S(2)}) copy-start(bf16[1,32,768]{2,1,0:T(8,128)(2,1)S(1)} %get-tuple-element.243.own_ref) | copy-start | bytes 147460
  205.3 5.7 %collective-permute-start.21 = (bf16[32,768]{1,0:T(8,128)(2,1)S(1)}, bf16[32,768]{1,0:T(8,128)(2,1)S(1)}, u32[]{:S(2)}, u32[]{:S(2)}) collective-permute-start(bf16[32,768]{1,0:T(8,128)(2,1)S(1)} %get-tuple-element.244), channel_id=1, source_target_pairs={{0,4},{1,5},{2,6},{3,7},{4,0},{5,1},{6,2},{7,3},{8,12},{9,13},{10,... | collective-permute-start | bytes 147464 | tf_op jit(solution)/shard_map/ppermute | solution.py:693
  206.8 4.5 collective-permute-start.20
  207.3 5.9 %collective-permute-start.22 = (bf16[32,768]{1,0:T(8,128)(2,1)S(1)}, bf16[32,768]{1,0:T(8,128)(2,1)S(1)}, u32[]{:S(2)}, u32[]{:S(2)}) collective-permute-start(bf16[32,768]{1,0:T(8,128)(2,1)S(1)} %get-tuple-element.244), channel_id=1, source_target_pairs={{0,6},{1,7},{2,4},{3,5},{4,2},{5,3},{6,0},{7,1},{8,14},{9,15},{10,... | collective-permute-start | bytes 147464 | tf_op jit(solution)/shard_map/ppermute | solution.py:693
  213.3 7.0 %collective-permute-start.24 = (bf16[4,32,768]{2,1,0:T(8,128)(2,1)S(1)}, bf16[4,32,768]{2,1,0:T(8,128)(2,1)S(1)}, u32[]{:S(2)}, u32[]{:S(2)}) collective-permute-start(bf16[4,32,768]{2,1,0:T(8,128)(2,1)S(1)} %get-tuple-element.242), channel_id=1, source_target_pairs={{0,16},{1,17},{2,18},{3,19},{4,20},{5,21},{6,22},{7,23},{8,24},{9,... | collective-permute-start | bytes 589832 | tf_op jit(solution)/shard_map/ppermute | solution.py:693
  214.9 7.6 %collective-permute-start.23 = (bf16[4,32,768]{2,1,0:T(8,128)(2,1)S(1)}, bf16[4,32,768]{2,1,0:T(8,128)(2,1)S(1)}, u32[]{:S(2)}, u32[]{:S(2)}) collective-permute-start(bf16[4,32,768]{2,1,0:T(8,128)(2,1)S(1)} %get-tuple-element.242), channel_id=1, source_target_pairs={{0,1},{1,0},{2,3},{3,2},{4,5},{5,4},{6,7},{7,6},{8,9},{9,8},{10,11... | collective-permute-start | bytes 589832 | tf_op jit(solution)/shard_map/ppermute | solution.py:693
  216.5 8.0 %collective-permute-start.25 = (bf16[4,32,768]{2,1,0:T(8,128)(2,1)S(1)}, bf16[4,32,768]{2,1,0:T(8,128)(2,1)S(1)}, u32[]{:S(2)}, u32[]{:S(2)}) collective-permute-start(bf16[4,32,768]{2,1,0:T(8,128)(2,1)S(1)} %get-tuple-element.242), channel_id=1, source_target_pairs={{0,17},{1,16},{2,19},{3,18},{4,21},{5,20},{6,23},{7,22},{8,25},{9,... | collective-permute-start | bytes 589832 | tf_op jit(solution)/shard_map/ppermute | solution.py:693
  224.7 2.4 collective-permute-start.26
  297.1 14.2 %collective-permute-start.27 = (bf16[2,2,4,384,384]{4,3,2,1,0:T(8,128)(2,1)}, bf16[2,2,4,384,384]{4,3,2,1,0:T(8,128)(2,1)}, u32[]{:S(2)}, u32[]{:S(2)}) collective-permute-start(bf16[2,2,4,384,384]{4,3,2,1,0:T(8,128)(2,1)} %get-tuple-element.162), channel_id=1, source_target_pairs={{0,8},{1,9},{2,10},{3,11},{4,12},{5,13},{6,14},{7,15},{8,0},{9,1},... | collective-permute-start | bytes 14155784 | tf_op jit(solution)/shard_map/ppermute | solution.py:693
  324.5 16.4 %collective-permute-start.28 = (bf16[2,2,4,208,384]{4,3,2,1,0:T(8,128)(2,1)}, bf16[2,2,4,208,384]{4,3,2,1,0:T(8,128)(2,1)}, u32[]{:S(2)}, u32[]{:S(2)}) collective-permute-start(bf16[2,2,4,208,384]{4,3,2,1,0:T(8,128)(2,1)} %get-tuple-element.169), channel_id=1, source_target_pairs={{0,8},{1,9},{2,10},{3,11},{4,12},{5,13},{6,14},{7,15},{8,0},{9,1},... | collective-permute-start | bytes 7667720 | tf_op jit(solution)/shard_map/ppermute | solution.py:693
  324.9 67.0 %collective-permute-start.30 = (bf16[2,4,384,384]{3,2,1,0:T(8,128)(2,1)}, bf16[2,4,384,384]{3,2,1,0:T(8,128)(2,1)}, u32[]{:S(2)}, u32[]{:S(2)}) collective-permute-start(bf16[2,4,384,384]{3,2,1,0:T(8,128)(2,1)} %fusion), channel_id=1, source_target_pairs={{0,16},{1,17},{2,18},{3,19},{4,20},{5,21},{6,22},{7,23},{8,24},{9,... | collective-permute-start | bytes 7077896 | tf_op jit(solution)/shard_map/ppermute | solution.py:693
  343.6 54.0 %collective-permute-start.29 = (bf16[2,4,208,384]{3,2,1,0:T(8,128)(2,1)}, bf16[2,4,208,384]{3,2,1,0:T(8,128)(2,1)}, u32[]{:S(2)}, u32[]{:S(2)}) collective-permute-start(bf16[2,4,208,384]{3,2,1,0:T(8,128)(2,1)} %fusion.2), channel_id=1, source_target_pairs={{0,1},{1,0},{2,3},{3,2},{4,5},{5,4},{6,7},{7,6},{8,9},{9,8},{10,11... | collective-permute-start | bytes 3833864 | tf_op jit(solution)/shard_map/ppermute | solution.py:693
  370.6 36.5 %collective-permute-start.32 = (bf16[2,2,4,112,384]{4,3,2,1,0:T(8,128)(2,1)}, bf16[2,2,4,112,384]{4,3,2,1,0:T(8,128)(2,1)}, u32[]{:S(2)}, u32[]{:S(2)}) collective-permute-start(bf16[2,2,4,112,384]{4,3,2,1,0:T(8,128)(2,1)} %get-tuple-element.195), channel_id=1, source_target_pairs={{0,8},{1,9},{2,10},{3,11},{4,12},{5,13},{6,14},{7,15},{8,0},{9,1},... | collective-permute-start | bytes 4128776 | tf_op jit(solution)/shard_map/ppermute | solution.py:693
  370.7 38.9 %collective-permute-start.31 = (bf16[2,2,4,96,384]{4,3,2,1,0:T(8,128)(2,1)}, bf16[2,2,4,96,384]{4,3,2,1,0:T(8,128)(2,1)}, u32[]{:S(2)}, u32[]{:S(2)}) collective-permute-start(bf16[2,2,4,96,384]{4,3,2,1,0:T(8,128)(2,1)} %get-tuple-element.194), channel_id=1, source_target_pairs={{0,8},{1,9},{2,10},{3,11},{4,12},{5,13},{6,14},{7,15},{8,0},{9,1},... | collective-permute-start | bytes 3538952 | tf_op jit(solution)/shard_map/ppermute | solution.py:693
  395.4 33.7 %collective-permute-start.34 = (bf16[4,384,384]{2,1,0:T(8,128)(2,1)}, bf16[4,384,384]{2,1,0:T(8,128)(2,1)}, u32[]{:S(2)}, u32[]{:S(2)}) collective-permute-start(bf16[4,384,384]{2,1,0:T(8,128)(2,1)} %fusion.1), channel_id=1, source_target_pairs={{0,1},{1,0},{2,3},{3,2},{4,5},{5,4},{6,7},{7,6},{8,9},{9,8},{10,11... | collective-permute-start | bytes 3538952 | tf_op jit(solution)/shard_map/ppermute | solution.py:693
  400.0 32.3 %collective-permute-start.33 = (bf16[4,208,384]{2,1,0:T(8,128)(2,1)}, bf16[4,208,384]{2,1,0:T(8,128)(2,1)}, u32[]{:S(2)}, u32[]{:S(2)}) collective-permute-start(bf16[4,208,384]{2,1,0:T(8,128)(2,1)} %fusion.3), channel_id=1, source_target_pairs={{0,16},{1,17},{2,18},{3,19},{4,20},{5,21},{6,22},{7,23},{8,24},{9,... | collective-permute-start | bytes 1916936 | tf_op jit(solution)/shard_map/ppermute | solution.py:693
  411.6 28.0 %collective-permute-start.41 = (bf16[2,4,96,384]{3,2,1,0:T(8,128)(2,1)}, bf16[2,4,96,384]{3,2,1,0:T(8,128)(2,1)}, u32[]{:S(2)}, u32[]{:S(2)}) collective-permute-start(bf16[2,4,96,384]{3,2,1,0:T(8,128)(2,1)} %fusion.10), channel_id=1, source_target_pairs={{0,1},{1,0},{2,3},{3,2},{4,5},{5,4},{6,7},{7,6},{8,9},{9,8},{10,11... | collective-permute-start | bytes 1769480 | tf_op jit(solution)/shard_map/ppermute | solution.py:693
  412.6 24.4 %collective-permute-start.42 = (bf16[2,4,112,384]{3,2,1,0:T(8,128)(2,1)}, bf16[2,4,112,384]{3,2,1,0:T(8,128)(2,1)S(1)}, u32[]{:S(2)}, u32[]{:S(2)}) collective-permute-start(bf16[2,4,112,384]{3,2,1,0:T(8,128)(2,1)} %fusion.4), channel_id=1, source_target_pairs={{0,16},{1,17},{2,18},{3,19},{4,20},{5,21},{6,22},{7,23},{8,24},{9,... | collective-permute-start | bytes 2064392 | tf_op jit(solution)/shard_map/ppermute | solution.py:693
  439.2 9.5 %collective-permute-start.44 = (bf16[4,112,384]{2,1,0:T(8,128)(2,1)}, bf16[4,112,384]{2,1,0:T(8,128)(2,1)}, u32[]{:S(2)}, u32[]{:S(2)}) collective-permute-start(bf16[4,112,384]{2,1,0:T(8,128)(2,1)} %fusion.5), channel_id=1, source_target_pairs={{0,1},{1,0},{2,3},{3,2},{4,5},{5,4},{6,7},{7,6},{8,9},{9,8},{10,11... | collective-permute-start | bytes 1032200 | tf_op jit(solution)/shard_map/ppermute | solution.py:693
  441.6 8.6 %collective-permute-start.43 = (bf16[4,96,384]{2,1,0:T(8,128)(2,1)}, bf16[4,96,384]{2,1,0:T(8,128)(2,1)}, u32[]{:S(2)}, u32[]{:S(2)}) collective-permute-start(bf16[4,96,384]{2,1,0:T(8,128)(2,1)} %fusion.14), channel_id=1, source_target_pairs={{0,16},{1,17},{2,18},{3,19},{4,20},{5,21},{6,22},{7,23},{8,24},{9,... | collective-permute-start | bytes 884744 | tf_op jit(solution)/shard_map/ppermute | solution.py:693
  444.0 20.5 %copy-start.7 = (bf16[208,384]{1,0:T(8,128)(2,1)S(1)}, bf16[208,384]{1,0:T(8,128)(2,1)}, u32[]{:S(2)}) copy-start(bf16[208,384]{1,0:T(8,128)(2,1)} %get-tuple-element.225) | copy-start | bytes 479236
  444.0 41.1 %collective-permute-start.38 = (bf16[384,384]{1,0:T(8,128)(2,1)S(1)}, bf16[384,384]{1,0:T(8,128)(2,1)S(1)}, u32[]{:S(2)}, u32[]{:S(2)}) collective-permute-start(bf16[384,384]{1,0:T(8,128)(2,1)S(1)} %get-tuple-element.223), channel_id=1, source_target_pairs={{0,2},{1,3},{2,0},{3,1},{4,6},{5,7},{6,4},{7,5},{8,10},{9,11},{10,... | collective-permute-start | bytes 884744 | tf_op jit(solution)/shard_map/ppermute | solution.py:693
  444.0 20.5 %collective-permute-start.40 = (bf16[384,384]{1,0:T(8,128)(2,1)}, bf16[384,384]{1,0:T(8,128)(2,1)S(1)}, u32[]{:S(2)}, u32[]{:S(2)}) collective-permute-start(bf16[384,384]{1,0:T(8,128)(2,1)} %get-tuple-element.221), channel_id=1, source_target_pairs={{0,6},{1,7},{2,4},{3,5},{4,2},{5,3},{6,0},{7,1},{8,14},{9,15},{10,... | collective-permute-start | bytes 884744 | tf_op jit(solution)/shard_map/ppermute | solution.py:693
  445.8 39.3 %collective-permute-start.39 = (bf16[384,384]{1,0:T(8,128)(2,1)}, bf16[384,384]{1,0:T(8,128)(2,1)S(1)}, u32[]{:S(2)}, u32[]{:S(2)}) collective-permute-start(bf16[384,384]{1,0:T(8,128)(2,1)} %get-tuple-element.222), channel_id=1, source_target_pairs={{0,4},{1,5},{2,6},{3,7},{4,0},{5,1},{6,2},{7,3},{8,12},{9,13},{10,... | collective-permute-start | bytes 884744 | tf_op jit(solution)/shard_map/ppermute | solution.py:693
  448.7 45.3 %collective-permute-start.35 = (bf16[208,384]{1,0:T(8,128)(2,1)}, bf16[208,384]{1,0:T(8,128)(2,1)S(1)}, u32[]{:S(2)}, u32[]{:S(2)}) collective-permute-start(bf16[208,384]{1,0:T(8,128)(2,1)} %get-tuple-element.226), channel_id=1, source_target_pairs={{0,2},{1,3},{2,0},{3,1},{4,6},{5,7},{6,4},{7,5},{8,10},{9,11},{10,... | collective-permute-start | bytes 479240 | tf_op jit(solution)/shard_map/ppermute | solution.py:693
  450.3 38.4 %collective-permute-start.37 = (bf16[208,384]{1,0:T(8,128)(2,1)}, bf16[208,384]{1,0:T(8,128)(2,1)S(1)}, u32[]{:S(2)}, u32[]{:S(2)}) collective-permute-start(bf16[208,384]{1,0:T(8,128)(2,1)} %get-tuple-element.224), channel_id=1, source_target_pairs={{0,6},{1,7},{2,4},{3,5},{4,2},{5,3},{6,0},{7,1},{8,14},{9,15},{10,... | collective-permute-start | bytes 479240 | tf_op jit(solution)/shard_map/ppermute | solution.py:693
  464.5 29.5 %collective-permute-start.36 = (bf16[208,384]{1,0:T(8,128)(2,1)S(1)}, bf16[208,384]{1,0:T(8,128)(2,1)S(1)}, u32[]{:S(2)}, u32[]{:S(2)}) collective-permute-start(bf16[208,384]{1,0:T(8,128)(2,1)S(1)} %copy-done.7), channel_id=1, source_target_pairs={{0,4},{1,5},{2,6},{3,7},{4,0},{5,1},{6,2},{7,3},{8,12},{9,13},{10,... | collective-permute-start | bytes 479240 | tf_op jit(solution)/shard_map/ppermute | solution.py:693
  485.1 15.3 %collective-permute-start.45 = (bf16[112,384]{1,0:T(8,128)(2,1)S(1)}, bf16[112,384]{1,0:T(8,128)(2,1)S(1)}, u32[]{:S(2)}, u32[]{:S(2)}) collective-permute-start(bf16[112,384]{1,0:T(8,128)(2,1)S(1)} %get-tuple-element.229), channel_id=1, source_target_pairs={{0,2},{1,3},{2,0},{3,1},{4,6},{5,7},{6,4},{7,5},{8,10},{9,11},{10,... | collective-permute-start | bytes 258056 | tf_op jit(solution)/shard_map/ppermute | solution.py:693
  485.1 16.9 %collective-permute-start.48 = (bf16[96,384]{1,0:T(8,128)(2,1)S(1)}, bf16[96,384]{1,0:T(8,128)(2,1)S(1)}, u32[]{:S(2)}, u32[]{:S(2)}) collective-permute-start(bf16[96,384]{1,0:T(8,128)(2,1)S(1)} %get-tuple-element.232), channel_id=1, source_target_pairs={{0,2},{1,3},{2,0},{3,1},{4,6},{5,7},{6,4},{7,5},{8,10},{9,11},{10,... | collective-permute-start | bytes 221192 | tf_op jit(solution)/shard_map/ppermute | solution.py:693
  488.6 7.2 %collective-permute-start.47 = (bf16[112,384]{1,0:T(8,128)(2,1)S(1)}, bf16[112,384]{1,0:T(8,128)(2,1)S(1)}, u32[]{:S(2)}, u32[]{:S(2)}) collective-permute-start(bf16[112,384]{1,0:T(8,128)(2,1)S(1)} %get-tuple-element.227), channel_id=1, source_target_pairs={{0,6},{1,7},{2,4},{3,5},{4,2},{5,3},{6,0},{7,1},{8,14},{9,15},{10,... | collective-permute-start | bytes 258056 | tf_op jit(solution)/shard_map/ppermute | solution.py:693
  494.0 6.5 %collective-permute-start.46 = (bf16[112,384]{1,0:T(8,128)(2,1)S(1)}, bf16[112,384]{1,0:T(8,128)(2,1)S(1)}, u32[]{:S(2)}, u32[]{:S(2)}) collective-permute-start(bf16[112,384]{1,0:T(8,128)(2,1)S(1)} %get-tuple-element.228), channel_id=1, source_target_pairs={{0,4},{1,5},{2,6},{3,7},{4,0},{5,1},{6,2},{7,3},{8,12},{9,13},{10,... | collective-permute-start | bytes 258056 | tf_op jit(solution)/shard_map/ppermute | solution.py:693
  494.0 7.6 %collective-permute-start.50 = (bf16[96,384]{1,0:T(8,128)(2,1)S(1)}, bf16[96,384]{1,0:T(8,128)(2,1)S(1)}, u32[]{:S(2)}, u32[]{:S(2)}) collective-permute-start(bf16[96,384]{1,0:T(8,128)(2,1)S(1)} %get-tuple-element.230), channel_id=1, source_target_pairs={{0,6},{1,7},{2,4},{3,5},{4,2},{5,3},{6,0},{7,1},{8,14},{9,15},{10,... | collective-permute-start | bytes 221192 | tf_op jit(solution)/shard_map/ppermute | solution.py:693
  495.9 6.2 %collective-permute-start.49 = (bf16[96,384]{1,0:T(8,128)(2,1)S(1)}, bf16[96,384]{1,0:T(8,128)(2,1)S(1)}, u32[]{:S(2)}, u32[]{:S(2)}) collective-permute-start(bf16[96,384]{1,0:T(8,128)(2,1)S(1)} %get-tuple-element.231), channel_id=1, source_target_pairs={{0,4},{1,5},{2,6},{3,7},{4,0},{5,1},{6,2},{7,3},{8,12},{9,13},{10,... | collective-permute-start | bytes 221192 | tf_op jit(solution)/shard_map/ppermute | solution.py:693
  (8 other events, 51.2 us)
Sparse Core Ops, SparseCore 0:
  11.6 156.1 all-gather.2
  297.5 160.0 reduce-scatter.1

commit v3 on v2

--- a/solution.py
+++ b/solution.py
@@ -21,6 +21,7 @@
 MIB = 1 << 20
 ANY = pl.BlockSpec(memory_space=pl.ANY)
 SMEM = pl.BlockSpec(memory_space=pltpu.SMEM)
+BRIEF = pl.CostEstimate(flops=1, transcendentals=0, bytes_accessed=1)
 
 
 def mm(left, right):
@@ -169,29 +170,24 @@
         ],
         scratch_shapes=[pltpu.VMEM((npb, npa, r + EXTRA, wq + wo), BF16), pltpu.SemaphoreType.DMA],
         compiler_params=pltpu.CompilerParams(vmem_limit_bytes=58 * MIB),
-        cost_estimate=pl.CostEstimate(flops=2 * tokens * d * (4 * d + 8 * ROW), transcendentals=0,
-                                      bytes_accessed=40 * MIB),
+        cost_estimate=BRIEF,
         name="attn_fwd",
     )(here, *packs, x, segc, segr)
 
 
 class FfnPlace:
     def __init__(self, up, down=None, e=None):
-        self.up, self.down, self.apart, self.e = up, down or up, down is not None, e
-        self.npb, self.npa = up.npb, up.npa
-        self.count = up.count + down.count if down else up.count
+        self.up, self.down, self.e = up, down or up, e
+        self.npb, self.npa, self.count = up.npb, up.npa, up.count
 
     def shapes(self, d, ff):
-        block = (d // self.npb * (1 if self.apart else 2), ff // self.npa)
-        places = [self.up, self.down] if self.apart else [self.up]
-        return [jax.ShapeDtypeStruct(place.lead + block, BF16) for place in places for _ in range(place.count)]
+        block = (d // self.npb * 2, ff // self.npa)
+        return [jax.ShapeDtypeStruct(self.up.lead + block, BF16)] * self.count
 
     def pieces(self, arrays, which, rows, spot):
         place = self.down if which else self.up
-        arrays = arrays[self.up.count :] if which and self.apart else arrays
-        base = rows if which and not self.apart else 0
         extra = () if self.e is None else (self.e,)
-        return [(arrays[index], lead + extra, base, b, a) for index, lead, b, a in place.blocks(spot)]
+        return [(arrays[index], lead + extra, rows if which else 0, b, a) for index, lead, b, a in place.blocks(spot)]
 
 
 class FfnLoad:
@@ -204,7 +200,7 @@
         r, c, dr, dc = d // npb, ff // npa, d // npa, ff // npb
         ups = self.place.pieces(self.packs, 0, r, self.spot)
         downs = self.place.pieces(self.packs, 1, r, self.spot)
-        if not self.place.apart:
+        if self.place.up.first is None:
             downs = sorted(downs, key=lambda piece: piece[3])
             ups = sorted(ups, key=lambda piece: piece[4])
         for k in range(len(ups)):
@@ -285,7 +281,7 @@
         scratch_shapes=[pltpu.VMEM((d, ff), BF16), pltpu.VMEM((d, ff), BF16), pltpu.VMEM((FFN_ROW, d), F32),
                         pltpu.SemaphoreType.DMA((2, place.npb))],
         compiler_params=pltpu.CompilerParams(vmem_limit_bytes=58 * MIB),
-        cost_estimate=pl.CostEstimate(flops=4 * tokens * d * ff, transcendentals=0, bytes_accessed=40 * MIB),
+        cost_estimate=BRIEF,
         name="ffn_fwd",
     )(here, spots, *packs, xhat, vec, bup)
 
@@ -297,6 +293,11 @@
         mid = rest.astype(BF16)
         tail = (rest - mid.astype(F32)).astype(BF16)
         return dot(high, right) + dot(mid, right) + dot(tail, right)
+
+    def put(ref, rows):
+        count = ref.shape[1]
+        for k in range(ref.shape[0]):
+            ref[k] = rows[k * count : (k + 1) * count]
 
     def log_norm(scores):
         peak = jnp.max(scores, axis=1, keepdims=True)
@@ -318,21 +319,22 @@
     hits = ids_ref[...] == hit_own
     loss_ref[...] = norm_own - jnp.sum(jnp.where(hits, own_rows, 0.0), axis=1, keepdims=True)
     tile = jnp.exp(own_rows - norm_own) - jnp.where(hits, 1.0, 0.0)
-    gq_ref[...] = split_mm(mm, tile, p_all) * scale
+    put(gq_ref, split_mm(mm, tile, p_all) * scale)
     own_cols = mm_nt(q_all, p_own) * scale
     hits = own_ids_ref[...] == hit_all
     tile = jnp.exp(own_cols - norm_all) - jnp.where(hits, 1.0, 0.0)
-    gp_ref[...] = split_mm(mm_tn, tile, q_all) * scale
-
-
-def loss_part(ids, own_ids, heads, own, q_count, p_count):
+    put(gp_ref, split_mm(mm_tn, tile, q_all) * scale)
+
+
+def loss_part(ids, own_ids, heads, own, q_spots, p_spots):
     d = heads.shape[2]
+    q_count, p_count = math.prod(q_spots), math.prod(p_spots)
     return pl.pallas_call(
         functools.partial(loss_kernel, 3.0 / math.sqrt(d), q_count, p_count),
         out_shape=[
             jax.ShapeDtypeStruct((q_count, 1), F32),
-            jax.ShapeDtypeStruct((q_count, d), F32),
-            jax.ShapeDtypeStruct((p_count, d), F32),
+            jax.ShapeDtypeStruct(q_spots + (d,), F32),
+            jax.ShapeDtypeStruct(p_spots + (d,), F32),
         ],
         compiler_params=pltpu.CompilerParams(vmem_limit_bytes=60 * MIB),
         name="loss_part",
@@ -452,7 +454,7 @@
                         pltpu.VMEM((d, tokens), BF16), pltpu.VMEM((d, tokens), BF16), pltpu.VMEM((tokens, ff), BF16),
                         pltpu.VMEM((tokens, ff), BF16), pltpu.SemaphoreType.DMA((2, place.npb))],
         compiler_params=pltpu.CompilerParams(vmem_limit_bytes=60 * MIB),
-        cost_estimate=pl.CostEstimate(flops=8 * tokens * d * ff, transcendentals=0, bytes_accessed=60 * MIB),
+        cost_estimate=BRIEF,
         name="ffn_bwd",
     )(here, spots, *packs, cot, gcls, norm2, inv2, act, slope, xhat, inv1, vec)
 
@@ -514,14 +516,13 @@
         out_shape=shapes + [jax.ShapeDtypeStruct(gvec.shape, F32)],
         input_output_aliases={} if before is None else {6: 0, 7: 1},
         compiler_params=pltpu.CompilerParams(vmem_limit_bytes=60 * MIB),
-        cost_estimate=pl.CostEstimate(flops=(last - first) * ROW * d * (2 * d + 40 * ROW), transcendentals=0,
-                                      bytes_accessed=8 * MIB),
+        cost_estimate=BRIEF,
         name="attn_bwd",
     )(dh, qkv, wout, segc, segr, gvec, *(before or ()))
 
 
 def attn_grad_kernel(dims, goals, here_ref, x_ref, att_ref, proj_ref, branch_ref, gvec, gbup, *refs):
-    total = sum(goal.count for goal, _, _ in goals)
+    total = goals[0][0].count
     grads, (x_t, wide, out, main, extra, sems) = refs[:total], refs[total:]
     npb, npa, r, wq, wo, rows_per, w1, w2 = dims
     step = pl.program_id(0)
@@ -562,20 +563,17 @@
                         widen(gbup[b : b + 1, a * w2 : (a + 1) * w2]),
                         jnp.zeros((EXTRA - 1 - rows_per, c), F32)]
                 extra[b * npa + a] = jnp.concatenate(rows, axis=0).astype(BF16)
-        base = 0
         for goal, low, high in goals:
             top = min(high, r)
             for index, lead, b, a in goal.blocks(here_ref):
-                target = grads[base + index]
+                target = grads[index]
                 start = b * r + low
                 if not isinstance(start, int):
                     start = pl.multiple_of(start, 16)
-                pltpu.make_async_copy(main.at[a, pl.ds(start, top - low)], target.at[lead + (pl.ds(0, top - low),)],
+                pltpu.make_async_copy(main.at[a, pl.ds(start, top - low)], target.at[lead + (pl.ds(low, top - low),)],
                                       sems.at[0]).start()
                 if high > r:
-                    pltpu.make_async_copy(extra.at[b * npa + a], target.at[lead + (pl.ds(r - low, EXTRA),)],
-                                          sems.at[1]).start()
-            base += goal.count
+                    pltpu.make_async_copy(extra.at[b * npa + a], target.at[lead + (pl.ds(r, EXTRA),)], sems.at[1]).start()
         pltpu.make_async_copy(main, main, sems.at[0]).wait()
         pltpu.make_async_copy(extra, extra, sems.at[1]).wait()
 
@@ -589,14 +587,13 @@
         grid=(4,),
         in_specs=[SMEM, whole(x.shape), whole(att.shape), pl.BlockSpec((tokens, d), lambda i: (0, jnp.minimum(i, 2))),
                   whole(branch.shape), whole(gvec.shape), whole(gbup.shape)],
-        out_specs=[ANY] * sum(goal.count for goal, _, _ in goals),
-        out_shape=[jax.ShapeDtypeStruct(goal.lead + (high - low, c), BF16)
-                   for goal, low, high in goals for _ in range(goal.count)],
+        out_specs=[ANY] * goals[0][0].count,
+        out_shape=[jax.ShapeDtypeStruct(goals[0][0].lead + (goals[-1][2], c), BF16)] * goals[0][0].count,
         scratch_shapes=[pltpu.VMEM((d, tokens), BF16), pltpu.VMEM((d, 3 * d), BF16), pltpu.VMEM((d, d), BF16),
                         pltpu.VMEM((npa, d, c), BF16),
                         pltpu.VMEM((npb * npa, EXTRA, c), BF16), pltpu.SemaphoreType.DMA((2,))],
         compiler_params=pltpu.CompilerParams(vmem_limit_bytes=60 * MIB),
-        cost_estimate=pl.CostEstimate(flops=8 * tokens * d * d, transcendentals=0, bytes_accessed=16 * MIB),
+        cost_estimate=BRIEF,
         name="attn_grad",
     )(here, x, att, proj, branch, gvec, gbup)
 
@@ -615,7 +612,7 @@
         out_specs=row(d),
         out_shape=jax.ShapeDtypeStruct((tokens, d), F32),
         compiler_params=pltpu.CompilerParams(vmem_limit_bytes=60 * MIB),
-        cost_estimate=pl.CostEstimate(flops=6 * tokens * d * d, transcendentals=0, bytes_accessed=16 * MIB),
+        cost_estimate=BRIEF,
         name="input_grad",
     )(proj, wqkv, dh)
 
@@ -719,32 +716,57 @@
 HEAD_ORDER = [c ^ s ^ z for c in (0, 8) for s in (0, 1, 16, 17) for z in (0, 2, 4, 6)]
 
 
+def cut_out(array, pick, rows):
+    depth = len(pick)
+    low = list(pick) + [0] * (array.ndim - depth)
+    high = [index + 1 for index in pick] + list(array.shape[depth:])
+    low[-2], high[-2] = rows.start, rows.stop
+    return lax.slice(array, low, high).reshape([h - l for l, h in zip(low, high)][depth:])
+
+
 class Scatter:
-    def __init__(self, keep, send, ways):
-        self.terms, self.ways = [(keep, ()), (send, ())], ways
-
-    def newest(self, line, count):
-        arrays, spots = zip(*self.terms)
-        fresh = line.wait(arrays[-count:])
-        self.terms = list(zip(arrays[:-count] + tuple(fresh), spots))
-
-    def sum(self, *pick):
-        return sum(array[spot + pick].astype(F32) for array, spot in self.terms)
+    def __init__(self, keep, send, cut):
+        self.shared = [keep, send]
+        self.own = [[], []]
+        self.rows = [slice(0, cut), slice(cut, keep.shape[-2])]
+        self.spot = ()
+
+    def sum(self, part, j=None):
+        pick = self.spot if j is None else self.spot + (j,)
+        terms = [cut_out(array, pick, self.rows[part]) for array in self.shared]
+        for age, array in self.own[part]:
+            terms.append(cut_out(array, pick[age:], slice(0, array.shape[-2])))
+        return sum(term.astype(F32) for term in terms)
 
     def step(self, stage, line):
         if stage == 0:
-            self.terms = [self.terms[0], (swap(self.terms[1][0], "core"), ())]
+            self.shared = [self.shared[0], swap(line.wait((self.shared[1],))[0], "core")]
             return
-        self.newest(line, 1)
-        ways = (self.ways[stage - 1],) if stage < 3 else ("z1", "z2", "z3")
-        parts = [self.sum(j).astype(BF16) for j in range(1, len(ways) + 1)]
+        self.fresh(line)
+        if stage < 3:
+            parts = [self.sum(part, 1).astype(BF16) for part in range(2)]
+            line.mark(parts)
+            self.spot += (0,)
+            for part, ways in enumerate((("y", "x"), ("x", "y"))):
+                self.own[part].append((len(self.spot), swap(parts[part], ways[stage - 1])))
+            return
+        parts = [jnp.concatenate([self.sum(part, j) for part in range(2)]).astype(BF16) for j in range(1, 4)]
         line.mark(parts)
-        self.terms = [(array, spot + (0,)) for array, spot in self.terms] + [
-            (swap(part, way), ()) for part, way in zip(parts, ways)]
+        self.spot += (0,)
+        self.last = [swap(part, f"z{j + 1}") for j, part in enumerate(parts)]
+
+    def fresh(self, line):
+        if self.spot:
+            arrays = line.wait(tuple(own[-1][1] for own in self.own))
+            for own, array in zip(self.own, arrays):
+                own[-1] = (own[-1][0], array)
+        else:
+            self.shared[1] = line.wait((self.shared[1],))[0]
 
     def total(self, line):
-        self.newest(line, 3)
-        return line.mark(self.sum())
+        last = line.wait(tuple(self.last))
+        kept = jnp.concatenate([self.sum(part) for part in range(2)])
+        return line.mark(kept + sum(term.astype(F32) for term in last))
 
 
 class Line:
@@ -837,8 +859,7 @@
             lambda *packs, e=e: ffn_fwd(ffn_into[e], here, spots[e], packs, half[e][2], half[e][6], half[e][7]), *ffn_w[e])
     own = jnp.concatenate([done[1][5].reshape(p_count, d).astype(BF16), done[0][5].reshape(q_count, d).astype(BF16), code])
     heads = gather_heads(own) if near else lax.all_gather(own, BOTH, axis=0)
-    losses, gq, gp = loss_part(ids, own_ids, heads, own[None], q_count, p_count)
-    gcls = tuple(grad.reshape(each.shape + (d,)) for grad, each in zip((gq, gp), spots))
+    losses, *gcls = loss_part(ids, own_ids, heads, own[None], spots[0].shape, spots[1].shape)
 
     def ffn_step(e, goal, cot):
         _, _, xhat, inv1, _, _, vec, bup = half[e]
@@ -853,51 +874,47 @@
     def attn_weights(e, goals, rows, gbup):
         return attn_grad(dims, goals, here, xs[e], half[e][1], rows[0], rows[1], rows[2], gbup)
 
-    def scatter(blocks):
+    def scatter(blocks, dtype=F32):
         flat = blocks.reshape((npb * npa,) + blocks.shape[2:])
-        return lax.psum_scatter(flat, BOTH, scatter_dimension=0, tiled=False).astype(F32)
+        return lax.psum_scatter(flat, BOTH, scatter_dimension=0, tiled=False).astype(dtype)
 
     counts = (q_rows, row_count)
     if near:
         whole_block = attn_pack.shape[1]
         cut = whole_block // 32 * 16 + 16
-        out_place = {way[0]: Place(npb, npa, way[0], False) for way in order}
+        y_first, x_first = (Place(npb, npa, way[0], False) for way in order)
+        goals = [(y_first, 0, cut), (x_first, cut, whole_block)]
         line = Line()
         dh_q, blocks_q, gvec_q, gbup_q = line.run(lambda cot: ffn_step(0, one_array, cot), cots[0])
-        sum_q = scatter(blocks_q[0])
-        dh_p, blocks_p, gvec_p, gbup_p = line.run(lambda cot: ffn_step(1, FfnPlace(out_place["y"]), cot), cots[1])
-        ffn_p = Scatter(*blocks_p, order[0])
+        sum_q = scatter(blocks_q[0], BF16)
+        dh_p, blocks_p, gvec_p, gbup_p = line.run(lambda cot: ffn_step(1, FfnPlace(y_first, x_first), cot), cots[1])
+        ffn_p = Scatter(*blocks_p, size.r)
         ffn_p.step(0, line)
-
         rows_q = line.run(lambda dh: attn_rows(0, 0, q_rows, dh, gvec_q, None), dh_q)
         ffn_p.step(1, line)
-        got = line.run(lambda *rows: attn_weights(0, [(out_place["x"], 0, whole_block)], rows, gbup_q), *rows_q)
-        attn_q = Scatter(*got, order[1])
-        attn_q.step(0, line)
+        attn_q = Scatter(*line.run(lambda *rows: attn_weights(0, goals, rows, gbup_q), *rows_q), cut)
         middle = row_count // 2
         rows_p = line.run(lambda dh: attn_rows(1, 0, middle, dh, gvec_p, None), dh_p)
+        ffn_p.step(2, line)
+        attn_q.step(0, line)
+        rows_p = line.run(lambda *rows: attn_rows(1, middle, row_count, dh_p, rows[2], rows[:2]), *rows_p)
+        ffn_p.step(3, line)
         attn_q.step(1, line)
-        rows_p = line.run(lambda *rows: attn_rows(1, middle, row_count, dh_p, rows[2], rows[:2]), *rows_p)
-        goals = [(out_place["y"], 0, cut), (out_place["x"], cut, whole_block)]
-        got = line.run(lambda *rows: attn_weights(1, goals, rows, gbup_p), *rows_p)
-        attn_p = [Scatter(*got[:2], order[0]), Scatter(*got[2:], order[1])]
-        for each in attn_p:
-            each.step(0, line)
-        ffn_p.step(2, line)
+        attn_p = Scatter(*line.run(lambda *rows: attn_weights(1, goals, rows, gbup_p), *rows_p), cut)
         attn_q.step(2, line)
+        attn_p.step(0, line)
         gx_q = line.run(lambda proj: input_grad(proj, half[0][4], dh_q), rows_q[0])
-        for each in attn_p:
-            each.step(1, line)
+        attn_p.step(1, line)
+        attn_q.step(3, line)
         gx_p = line.run(lambda proj: input_grad(proj, half[1][4], dh_p), rows_p[0])
         gx = (gx_q, gx_p)
-        ffn_p.step(3, line)
-        attn_q.step(3, line)
-        for stage in (2, 3):
-            for each in attn_p:
-                each.step(stage, line)
-        sums = [each.total(line) for each in [ffn_p, attn_q] + attn_p]
-        ffn_sum = [sum_q, sums[0]]
-        attn_sum = [sums[1], jnp.concatenate(sums[2:])]
+        attn_p.step(2, line)
+        attn_p.step(3, line)
+        sums = [ffn_p.total(line), attn_q.total(line)]
+        sum_q = line.wait((sum_q,))[0]
+        sums.append(attn_p.total(line))
+        ffn_sum = [sum_q.astype(F32), sums[0]]
+        attn_sum = sums[1:]
     else:
         pairs, gx = [], []
         for e in range(2):

time: 526 us -> 508 us (0.966)
  waiting for transfers between devices: 165 us -> 146 us
    ppermute x51, waiting for transfers between devices: 146 us -> 124 us  [swap(): return lax.ppermute(block, BOTH, [(i, i ^ BITS[way]) for i in range(32)])]
    another operation x0 -> x6, other arithmetic: none -> 11.6 us
    convert_element_type x13 -> x10, other arithmetic: 31.3 us -> 21.8 us  [step(): parts = [self.sum(part, 1).astype(BF16) for part in range(2)]]
  transfers between devices with their start and end apart: 53 -> 53, of which waited for: 26 -> 26; matrix products, arithmetic and copies ran while one was open for 9% -> 9% of each run, Pallas kernels for 22% -> 23%
where the time goes in v3:
time: 508 us; the launch traced here: 499 us
  Pallas kernels  215 us (42%)
  waiting for transfers between devices  146 us (29%)
  starting transfers between devices  65.8 us (13%)
  other arithmetic  51.2 us (10%)
  between operations  15.1 us (3%)
    ppermute x51, waiting for transfers between devices, swap(): return lax.ppermute(block, BOTH, [(i, i ^ BITS[way]) for i in range(32)])  124 us
    ppermute x51, starting transfers between devices, swap(): return lax.ppermute(block, BOTH, [(i, i ^ BITS[way]) for i in range(32)])  65.7 us
    pallas_call x2, Pallas kernels, ffn_bwd(): pl.pallas_call(functools.partial(ffn_bwd_kernel, place, goal, steps), gri...  62.3 us
    pallas_call x3, Pallas kernels, attn_bwd(): pl.pallas_call(kernel, grid=(last - first,), in_specs=[row(d), row(3 * d)...  42.4 us
    pallas_call x2, Pallas kernels, attn_fwd(): pl.pallas_call(functools.partial(attn_fwd_kernel, dims, place), grid=(ste...  36.3 us
    pallas_call x2, Pallas kernels, ffn_fwd(): pl.pallas_call(functools.partial(ffn_fwd_kernel, place), grid=(steps,), i...  35.3 us
    all_gather x1, waiting for transfers between devices, body(): lax.all_gather(ffn_pack, BOTH, axis=0).reshape((npb, npa) + ffn_pack.shape)  22 us
    convert_element_type x10, other arithmetic, step(): parts = [self.sum(part, 1).astype(BF16) for part in range(2)]  21.8 us
  transfers between devices with their start and end apart: 53, of which 26 were waited for; matrix products, arithmetic and copies ran while one was open for 9% of the time, Pallas kernels for 23%

profile of v3, /device:TPU:0, one launch (start us, length us, event | category | flops | bytes accessed | tf_op | source)
XLA Modules:
  0.0 498.6 jit_solution(14713348016245021391)
XLA Ops:
  8.3 1.8 pad_maximum_fusion.5
  10.5 5.1 %collective-permute-start.12 = (bf16[208,384]{1,0:T(8,128)(2,1)S(1)}, bf16[208,384]{1,0:T(8,128)(2,1)S(1)}, u32[]{:S(2)}, u32[]{:S(2)}) collective-permute-start(bf16[208,384]{1,0:T(8,128)(2,1)S(1)} %get-tuple-element.257), channel_id=1, source_target_pairs={{0,6},{1,7},{2,4},{3,5},{4,2},{5,3},{6,0},{7,1},{8,14},{9,15},{10,... | collective-permute-start | bytes 479240 | tf_op jit(solution)/shard_map/ppermute | solution.py:690
  16.2 3.7 collective-permute-start.2
  20.6 9.3 %collective-permute-start = (bf16[208,384]{1,0:T(8,128)(2,1)S(1)}, bf16[208,384]{1,0:T(8,128)(2,1)S(1)}, u32[]{:S(2)}, u32[]{:S(2)}) collective-permute-start(bf16[208,384]{1,0:T(8,128)(2,1)S(1)} %get-tuple-element.256), channel_id=1, source_target_pairs={{0,2},{1,3},{2,0},{3,1},{4,6},{5,7},{6,4},{7,5},{8,10},{9,11},{10,... | collective-permute-start | bytes 479240 | tf_op jit(solution)/shard_map/ppermute | solution.py:690
  30.0 14.7 %collective-permute-done.11 = bf16[208,384]{1,0:T(8,128)(2,1)S(1)} collective-permute-done((bf16[208,384]{1,0:T(8,128)(2,1)S(1)}, bf16[208,384]{1,0:T(8,128)(2,1)S(1)}, u32[]{:S(2)}, u32[]{:S(2)}) %collective-permute-start.11) | collective-permute-done | bytes 159776 | tf_op jit(solution)/shard_map/ppermute | solution.py:690
  44.9 2.0 collective-permute-start.14
  46.9 1.6 collective-permute-start.13
  48.5 7.0 %collective-permute-done.1 = bf16[208,384]{1,0:T(8,128)(2,1)S(1)} collective-permute-done((bf16[208,384]{1,0:T(8,128)(2,1)S(1)}, bf16[208,384]{1,0:T(8,128)(2,1)S(1)}, u32[]{:S(2)}, u32[]{:S(2)}) %collective-permute-start.1) | collective-permute-done | bytes 159776 | tf_op jit(solution)/shard_map/ppermute | solution.py:690
  55.6 1.6 collective-permute-start.3
  57.2 1.5 collective-permute-start.4
  58.8 9.7 %collective-permute-done.13.refs_1_ = bf16[4,208,384]{2,1,0:T(8,128)(2,1)} collective-permute-done((bf16[4,208,384]{2,1,0:T(8,128)(2,1)S(1)}, bf16[4,208,384]{2,1,0:T(8,128)(2,1)}, u32[]{:S(2)}, u32[]{:S(2)}) %collective-permute-start.13) | collective-permute-done | bytes 639008 | tf_op jit(solution)/shard_map/ppermute | solution.py:690
  69.3 22.8 %collective-permute-done.3.refs_1_ = bf16[4,208,384]{2,1,0:T(8,128)(2,1)S(1)} collective-permute-done((bf16[4,208,384]{2,1,0:T(8,128)(2,1)S(1)}, bf16[4,208,384]{2,1,0:T(8,128)(2,1)S(1)}, u32[]{:S(2)}, u32[]{:S(2)}) %collective-permute-start.3) | collective-permute-done | bytes 639008 | tf_op jit(solution)/shard_map/ppermute | solution.py:690
  92.1 1.9 collective-permute-start.5
  95.3 10.8 %collective-permute-done.15.refs_3_ = bf16[4,208,384]{2,1,0:T(8,128)(2,1)} collective-permute-done((bf16[4,208,384]{2,1,0:T(8,128)(2,1)}, bf16[4,208,384]{2,1,0:T(8,128)(2,1)}, u32[]{:S(2)}, u32[]{:S(2)}) %collective-permute-start.15) | collective-permute-done | bytes 639008 | tf_op jit(solution)/shard_map/ppermute | solution.py:690
  110.9 14.7 %attn_fwd.2 = (bf16[512,2304]{1,0:T(8,128)(2,1)}, bf16[512,768]{1,0:T(8,128)(2,1)}, f32[512,768]{1,0:T(8,128)}, f32[512,1]{1,0:T(8,128)}, bf16[768,2304]{1,0:T(8...) custom-call(s32[4]{0:T(128)} %pad_add_fusion.2.here_ref, ...), custom_call_target="tpu_custom_call" | custom-call | flops 1 | bytes 1 | tf_op jit(solution)/shard_map/attn_fwd/pallas_call | solution.py:154
  125.7 21.6 %attn_fwd.3 = (bf16[1024,2304]{1,0:T(8,128)(2,1)}, bf16[1024,768]{1,0:T(8,128)(2,1)}, f32[1024,768]{1,0:T(8,128)}, f32[1024,1]{1,0:T(8,128)}, bf16[768,2304]{1,0...) custom-call(s32[4]{0:T(128)} %pad_add_fusion.2.here_ref, ...), custom_call_target="tpu_custom_call" | custom-call | flops 1 | bytes 1 | tf_op jit(solution)/shard_map/attn_fwd/pallas_call | solution.py:154
  147.3 22.0 %all-gather.3.cloned.1.call-done = bf16[64,384,384]{2,1,0:T(8,128)(2,1)} async-done(((bf16[2,384,384]{2,1,0:T(8,128)(2,1)}), bf16[64,384,384]{2,1,0:T(8,128)(2,1)}) %all-gather.3.cloned.1.call-update) | async-done | bytes 18874384 | tf_op jit(solution)/shard_map/all_gather | solution.py:807
  169.9 13.2 %ffn_fwd.2 = (bf16[512,3072]{1,0:T(8,128)(2,1)}, bf16[512,3072]{1,0:T(8,128)(2,1)}, f32[512,768]{1,0:T(8,128)}, f32[512,1]{1,0:T(8,128)}, bf16[512,768]{1,0:T(8,128)(2,1)}, /*index=5*/f32[2,4,768]{2,1,0:T(4,128)}) custom-call(s32[4]{0:T(128)} %pad_add_fusion.2.here_ref, s32[2,4]{1,0:T(2,128)} %broadcast_in_dim.12.spot_ref, ...), custom_call_target="tpu_custom_call" | custom-call | flops 1 | bytes 1 | tf_op jit(solution)/shard_map/ffn_fwd/pallas_call | solution.py:268
  183.9 22.1 %ffn_fwd.3 = (bf16[1024,3072]{1,0:T(8,128)(2,1)}, bf16[1024,3072]{1,0:T(8,128)(2,1)}, f32[1024,768]{1,0:T(8,128)}, f32[1024,1]{1,0:T(8,128)}, bf16[1024,768]{1,0:T(8,128)(2,1)}, /*index=5*/f32[4,4,768]{2,1,0:T(4,128)}) custom-call(s32[4]{0:T(128)} %pad_add_fusion.2.here_ref, s32[4,4]{1,0:T(4,128)} %copy-done.20, bf16[4,8,2,384,384]{4,3,2,1,0:T(8,128)(2,1)} %bitcast.294, ...), custom_call_target="tpu_custom_call" | custom-call | flops 1 | bytes 1 | tf_op jit(solution)/shard_map/ffn_fwd/pallas_call | solution.py:268
  206.8 1.6 collective-permute-start.21
  208.9 2.4 collective-permute-start.22
  212.9 1.9 collective-permute-done.22
  214.8 1.5 collective-permute-start.24
  216.9 1.5 collective-permute-start.25
  218.3 3.4 collective-permute-done.24
  221.8 2.2 collective-permute-done.23
  224.0 2.1 collective-permute-done.25
  229.8 3.7 loss_part.1
  233.5 24.0 %ffn_bwd.2 = (f32[512,768]{1,0:T(8,128)}, bf16[4,8,384,384]{3,2,1,0:T(8,128)(2,1)}, f32[8,768]{1,0:T(8,128)}, f32[4,768]{1,0:T(4,128)}) custom-call(s32[4]{0:T(128)} %pad_add_fusion.2.here_ref, s32[2,4]{1,0:T(2,128)} %broadcast_in_dim.12.spot_ref, bf16[4,8,2,384,384]{4,3,2,1,0:T(8,128)(2,1)} %bitcast.295, bf16[512,768]{1,0:T(8,128)(2,1)} %bitcast.314, ...), custom_call_target="tpu_custom_call" | custom-call | flops 1 | bytes 1 | tf_op jit(solution)/shard_map/ffn_bwd/pallas_call | solution.py:440
  257.5 38.3 %ffn_bwd.3 = (f32[1024,768]{1,0:T(8,128)}, bf16[2,2,4,384,384]{4,3,2,1,0:T(8,128)(2,1)}, bf16[2,2,4,384,384]{4,3,2,1,0:T(8,128)(2,1)}, f32[8,768]{1,0:T(8,128)}, f32[4,768]{1,0:T(4,128)}) custom-call(s32[4]{0:T(128)} %pad_add_fusion.2.here_ref, s32[4,4]{1,0:T(4,128)} %copy-done.20, bf16[4,8,2,384,384]{4,3,2,1,0:T(8,128)(2,1)} %bitcast.296, ...), custom_call_target="tpu_custom_call" | custom-call | flops 1 | bytes 1 | tf_op jit(solution)/shard_map/ffn_bwd/pallas_call | solution.py:440
  296.1 14.0 %attn_bwd.3 = (bf16[512,2304]{1,0:T(8,128)(2,1)}, bf16[512,768]{1,0:T(8,128)(2,1)}, f32[8,768]{1,0:T(8,128)}) custom-call(f32[512,768]{1,0:T(8,128)} %get-tuple-element.156.refs_0_.dh_ref, bf16[512,2304]{1,0:T(8,128)(2,1)} %get-tuple-element.117.refs_1_, bf16[768,768]{1,0:T(8,128)(2,1)} %get-tuple-element.157.refs_2_, s32[2,256,2]{2,1,0:T(8,128)} %copy.50.refs_9_.refs_3_, ...), custom_call_target="tpu_custom_call" | custom-call | flops 1 | bytes 1 | tf_op jit(solution)/shard_map/attn_bwd/pallas_call | solution.py:509
  310.1 4.3 fusion.1
  316.4 8.5 %attn_grad.2 = (bf16[2,2,4,208,384]{4,3,2,1,0:T(8,128)(2,1)}, bf16[2,2,4,208,384]{4,3,2,1,0:T(8,128)(2,1)}) custom-call(s32[4]{0:T(128)} %pad_add_fusion.2.here_ref, bf16[512,768]{1,0:T(8,128)(2,1)} %bitcast.310, bf16[512,768]{1,0:T(8,128)(2,1)} %get-tuple-element.160.att_ref, bf16[512,2304]{1,0:T(8,128)(2,1)} %get-tuple-element.198.proj_ref, ...), custom_call_target="tpu_custom_call" | custom-call | flops 1 | bytes 1 | tf_op jit(solution)/shard_map/attn_grad/pallas_call | solution.py:585
  324.9 14.4 %attn_bwd.4 = (bf16[1024,2304]{1,0:T(8,128)(2,1)}, bf16[1024,768]{1,0:T(8,128)(2,1)}, f32[8,768]{1,0:T(8,128)}) custom-call(f32[1024,768]{1,0:T(8,128)} %get-tuple-element.173.refs_0_.dh_ref, bf16[1024,2304]{1,0:T(8,128)(2,1)} %get-tuple-element.127.refs_1_, bf16[768,768]{1,0:T(8,128)(2,1)} %get-tuple-element.174.refs_2_, ...), custom_call_target="tpu_custom_call" | custom-call | flops 1 | bytes 1 | tf_op jit(solution)/shard_map/attn_bwd/pallas_call | solution.py:509
  339.3 3.5 collective-permute-done.29
  343.7 2.5 fusion.2
  347.0 1.5 collective-permute-start.31
  348.5 14.0 %attn_bwd.5 = (bf16[1024,2304]{1,0:T(8,128)(2,1)}, bf16[1024,768]{1,0:T(8,128)(2,1)}, f32[8,768]{1,0:T(8,128)}) custom-call(f32[1024,768]{1,0:T(8,128)} %get-tuple-element.173.refs_0_.dh_ref, bf16[1024,2304]{1,0:T(8,128)(2,1)} %get-tuple-element.127.refs_1_, ...), custom_call_target="tpu_custom_call", output_to_operand_aliasing={{0}: (6, {}), {1}: (7, {})} | custom-call | flops 1 | bytes 1 | tf_op jit(solution)/shard_map/attn_bwd/pallas_call | solution.py:509
  362.5 8.0 %collective-permute-done.32 = bf16[4,192,384]{2,1,0:T(8,128)(2,1)S(1)} collective-permute-done((bf16[4,192,384]{2,1,0:T(8,128)(2,1)S(1)}, bf16[4,192,384]{2,1,0:T(8,128)(2,1)S(1)}, u32[]{:S(2)}, u32[]{:S(2)}) %collective-permute-start.32) | collective-permute-done | bytes 589856 | tf_op jit(solution)/shard_map/ppermute | solution.py:690
  370.9 2.3 fusion.23
  373.2 2.6 fusion.24
  376.6 2.1 fusion.4
  380.1 2.0 fusion.12
  382.8 11.7 %attn_grad.3 = (bf16[2,2,4,208,384]{4,3,2,1,0:T(8,128)(2,1)}, bf16[2,2,4,208,384]{4,3,2,1,0:T(8,128)(2,1)}) custom-call(s32[4]{0:T(128)} %pad_add_fusion.2.here_ref, bf16[1024,768]{1,0:T(8,128)(2,1)} %bitcast.307, bf16[1024,768]{1,0:T(8,128)(2,1)} %get-tuple-element.189.att_ref, bf16[1024,2304]{1,0:T(8,128)(2,1)} %get-tuple-element.206.proj_ref, ...), custom_call_target="tpu_custom_call" | custom-call | flops 1 | bytes 1 | tf_op jit(solution)/shard_map/attn_grad/pallas_call | solution.py:585
  394.5 5.1 %collective-permute-done.34 = bf16[2,4,96,384]{3,2,1,0:T(8,128)(2,1)} collective-permute-done((bf16[2,4,96,384]{3,2,1,0:T(8,128)(2,1)}, bf16[2,4,96,384]{3,2,1,0:T(8,128)(2,1)}, u32[]{:S(2)}, u32[]{:S(2)}) %collective-permute-start.34) | collective-permute-done | bytes 589856 | tf_op jit(solution)/shard_map/ppermute | solution.py:690
  399.6 2.2 collective-permute-done.33
  401.8 1.9 fusion.7
  405.4 1.9 collective-permute-start.42
  407.9 1.9 fusion.18
  411.3 5.7 %input_grad.2 = f32[512,768]{1,0:T(8,128)} custom-call(bf16[512,2304]{1,0:T(8,128)(2,1)} %get-tuple-element.198.proj_ref, bf16[768,2304]{1,0:T(8,128)(2,1)} %get-tuple-element.199.weight_ref, f32[512,768]{1,0:T(8,128)} %get-tuple-element.156.refs_0_.dh_ref), custom_call_target="tpu_custom_call" | custom-call | flops 1 | bytes 1 | tf_op jit(solution)/shard_map/input_grad/pallas_call | solution.py:608
  417.0 2.3 fusion.5
  419.9 2.2 fusion.13
  422.7 1.5 collective-permute-start.45
  424.2 2.1 fusion.39
  426.2 2.0 fusion.33
  428.9 9.4 %input_grad.3 = f32[1024,768]{1,0:T(8,128)} custom-call(bf16[1024,2304]{1,0:T(8,128)(2,1)} %get-tuple-element.206.proj_ref, bf16[768,2304]{1,0:T(8,128)(2,1)} %get-tuple-element.207.weight_ref, f32[1024,768]{1,0:T(8,128)} %get-tuple-element.173.refs_0_.dh_ref), custom_call_target="tpu_custom_call" | custom-call | flops 1 | bytes 1 | tf_op jit(solution)/shard_map/input_grad/pallas_call | solution.py:608
  442.5 3.3 collective-permute-start.43
  445.8 3.9 collective-permute-done.47
  451.3 2.4 collective-permute-start.39
  456.4 1.5 collective-permute-start.40
  459.3 13.7 %collective-permute-done.39 = bf16[208,384]{1,0:T(8,128)(2,1)S(1)} collective-permute-done((bf16[208,384]{1,0:T(8,128)(2,1)S(1)}, bf16[208,384]{1,0:T(8,128)(2,1)S(1)}, u32[]{:S(2)}, u32[]{:S(2)}) %collective-permute-start.39) | collective-permute-done | bytes 159776 | tf_op jit(solution)/shard_map/ppermute | solution.py:690
  473.1 3.7 collective-permute-start.49
  476.9 2.0 collective-permute-start.50
  481.6 6.7 %collective-permute-done.49 = bf16[208,384]{1,0:T(8,128)(2,1)S(1)} collective-permute-done((bf16[208,384]{1,0:T(8,128)(2,1)S(1)}, bf16[208,384]{1,0:T(8,128)(2,1)S(1)}, u32[]{:S(2)}, u32[]{:S(2)}) %collective-permute-start.49) | collective-permute-done | bytes 159776 | tf_op jit(solution)/shard_map/ppermute | solution.py:690
  (191 shorter events, 46.7 us)
Async XLA Ops:
  7.2 162.1 %all-gather.3.cloned.1.call-start = ((), (), s32[]{:S(2)}) async-start(), calls=%async_computation.2 | async-start | bytes 19464192 | tf_op jit(solution)/shard_map/all_gather | solution.py:807
  10.2 47.0 %copy-start.26 = (s32[8]{0:T(128)S(1)}, s32[8]{0:T(128)}, u32[]{:S(2)}) copy-start(s32[8]{0:T(128)} %param.18) | copy-start | bytes 100
  10.2 83.8 %copy-start.24 = (s32[64]{0:T(128)S(1)}, s32[64]{0:T(128)}, u32[]{:S(2)}) copy-start(s32[64]{0:T(128)} %param.20) | copy-start | bytes 772
  10.2 84.0 %copy-start.21 = (s32[4,4]{1,0:T(4,128)S(1)}, s32[4,4]{1,0:T(4,128)}, u32[]{:S(2)}) copy-start(s32[4,4]{1,0:T(4,128)} %param.19) | copy-start | bytes 196
  10.2 462.9 %reduce-scatter.2.cloned.1.call-start = ((), (), s32[]{:S(2)}) async-start(), calls=%async_computation.1 | async-start | bytes 9732096 | tf_op jit(solution)/shard_map/reduce_scatter | solution.py:879
  10.5 10.2 %collective-permute-start.12 = (bf16[208,384]{1,0:T(8,128)(2,1)S(1)}, bf16[208,384]{1,0:T(8,128)(2,1)S(1)}, u32[]{:S(2)}, u32[]{:S(2)}) collective-permute-start(bf16[208,384]{1,0:T(8,128)(2,1)S(1)} %get-tuple-element.257), channel_id=1, source_target_pairs={{0,6},{1,7},{2,4},{3,5},{4,2},{5,3},{6,0},{7,1},{8,14},{9,15},{10,... | collective-permute-start | bytes 479240 | tf_op jit(solution)/shard_map/ppermute | solution.py:690
  15.6 29.1 %collective-permute-start.11 = (bf16[208,384]{1,0:T(8,128)(2,1)S(1)}, bf16[208,384]{1,0:T(8,128)(2,1)S(1)}, u32[]{:S(2)}, u32[]{:S(2)}) collective-permute-start(bf16[208,384]{1,0:T(8,128)(2,1)S(1)} %get-tuple-element.257), channel_id=1, source_target_pairs={{0,4},{1,5},{2,6},{3,7},{4,0},{5,1},{6,2},{7,3},{8,12},{9,13},{10,... | collective-permute-start | bytes 479240 | tf_op jit(solution)/shard_map/ppermute | solution.py:690
  15.6 29.1 %collective-permute-start.10 = (bf16[208,384]{1,0:T(8,128)(2,1)S(1)}, bf16[208,384]{1,0:T(8,128)(2,1)S(1)}, u32[]{:S(2)}, u32[]{:S(2)}) collective-permute-start(bf16[208,384]{1,0:T(8,128)(2,1)S(1)} %get-tuple-element.257), channel_id=1, source_target_pairs={{0,2},{1,3},{2,0},{3,1},{4,6},{5,7},{6,4},{7,5},{8,10},{9,11},{10,... | collective-permute-start | bytes 479240 | tf_op jit(solution)/shard_map/ppermute | solution.py:690
  16.2 30.6 %collective-permute-start.2 = (bf16[208,384]{1,0:T(8,128)(2,1)S(1)}, bf16[208,384]{1,0:T(8,128)(2,1)S(1)}, u32[]{:S(2)}, u32[]{:S(2)}) collective-permute-start(bf16[208,384]{1,0:T(8,128)(2,1)S(1)} %get-tuple-element.256), channel_id=1, source_target_pairs={{0,6},{1,7},{2,4},{3,5},{4,2},{5,3},{6,0},{7,1},{8,14},{9,15},{10,... | collective-permute-start | bytes 479240 | tf_op jit(solution)/shard_map/ppermute | solution.py:690
  20.0 35.5 %collective-permute-start.1 = (bf16[208,384]{1,0:T(8,128)(2,1)S(1)}, bf16[208,384]{1,0:T(8,128)(2,1)S(1)}, u32[]{:S(2)}, u32[]{:S(2)}) collective-permute-start(bf16[208,384]{1,0:T(8,128)(2,1)S(1)} %get-tuple-element.256), channel_id=1, source_target_pairs={{0,4},{1,5},{2,6},{3,7},{4,0},{5,1},{6,2},{7,3},{8,12},{9,13},{10,... | collective-permute-start | bytes 479240 | tf_op jit(solution)/shard_map/ppermute | solution.py:690
  20.6 34.8 %collective-permute-start = (bf16[208,384]{1,0:T(8,128)(2,1)S(1)}, bf16[208,384]{1,0:T(8,128)(2,1)S(1)}, u32[]{:S(2)}, u32[]{:S(2)}) collective-permute-start(bf16[208,384]{1,0:T(8,128)(2,1)S(1)} %get-tuple-element.256), channel_id=1, source_target_pairs={{0,2},{1,3},{2,0},{3,1},{4,6},{5,7},{6,4},{7,5},{8,10},{9,11},{10,... | collective-permute-start | bytes 479240 | tf_op jit(solution)/shard_map/ppermute | solution.py:690
  44.8 66.1 %copy-start.3 = (bf16[4,208,384]{2,1,0:T(8,128)(2,1)}, bf16[4,208,384]{2,1,0:T(8,128)(2,1)S(1)}, u32[]{:S(2)}) copy-start(bf16[4,208,384]{2,1,0:T(8,128)(2,1)S(1)} %pad_maximum_fusion.3.refs_0_) | copy-start | bytes 1916932
  44.8 23.7 %collective-permute-start.16 = (bf16[4,208,384]{2,1,0:T(8,128)(2,1)S(1)}, bf16[4,208,384]{2,1,0:T(8,128)(2,1)S(1)}, u32[]{:S(2)}, u32[]{:S(2)}) collective-permute-start(bf16[4,208,384]{2,1,0:T(8,128)(2,1)S(1)} %pad_maximum_fusion.3.refs_0_), channel_id=1, source_target_pairs={{0,8},{1,9},{2,10},{3,11},{4,12},{5,13},{6,14},{7,15},{8,0},{9,1},... | collective-permute-start | bytes 1916936 | tf_op jit(solution)/shard_map/ppermute | solution.py:690
  44.9 23.7 %collective-permute-start.14 = (bf16[4,208,384]{2,1,0:T(8,128)(2,1)S(1)}, bf16[4,208,384]{2,1,0:T(8,128)(2,1)}, u32[]{:S(2)}, u32[]{:S(2)}) collective-permute-start(bf16[4,208,384]{2,1,0:T(8,128)(2,1)S(1)} %pad_maximum_fusion.3.refs_0_), channel_id=1, source_target_pairs={{0,1},{1,0},{2,3},{3,2},{4,5},{5,4},{6,7},{7,6},{8,9},{9,8},{10,11... | collective-permute-start | bytes 1916936 | tf_op jit(solution)/shard_map/ppermute | solution.py:690
  46.9 21.6 %collective-permute-start.13 = (bf16[4,208,384]{2,1,0:T(8,128)(2,1)S(1)}, bf16[4,208,384]{2,1,0:T(8,128)(2,1)}, u32[]{:S(2)}, u32[]{:S(2)}) collective-permute-start(bf16[4,208,384]{2,1,0:T(8,128)(2,1)S(1)} %pad_maximum_fusion.3.refs_0_), channel_id=1, source_target_pairs={{0,16},{1,17},{2,18},{3,19},{4,20},{5,21},{6,22},{7,23},{8,24},{9,... | collective-permute-start | bytes 1916936 | tf_op jit(solution)/shard_map/ppermute | solution.py:690
  55.6 70.1 %copy-start.2 = (bf16[4,208,384]{2,1,0:T(8,128)(2,1)}, bf16[4,208,384]{2,1,0:T(8,128)(2,1)S(1)}, u32[]{:S(2)}) copy-start(bf16[4,208,384]{2,1,0:T(8,128)(2,1)S(1)} %pad_maximum_fusion.2.refs_0_) | copy-start | bytes 1916932
  55.6 36.5 %collective-permute-start.3 = (bf16[4,208,384]{2,1,0:T(8,128)(2,1)S(1)}, bf16[4,208,384]{2,1,0:T(8,128)(2,1)S(1)}, u32[]{:S(2)}, u32[]{:S(2)}) collective-permute-start(bf16[4,208,384]{2,1,0:T(8,128)(2,1)S(1)} %pad_maximum_fusion.2.refs_0_), channel_id=1, source_target_pairs={{0,1},{1,0},{2,3},{3,2},{4,5},{5,4},{6,7},{7,6},{8,9},{9,8},{10,11... | collective-permute-start | bytes 1916936 | tf_op jit(solution)/shard_map/ppermute | solution.py:690
  57.2 37.4 %collective-permute-start.4 = (bf16[4,208,384]{2,1,0:T(8,128)(2,1)S(1)}, bf16[4,208,384]{2,1,0:T(8,128)(2,1)S(1)}, u32[]{:S(2)}, u32[]{:S(2)}) collective-permute-start(bf16[4,208,384]{2,1,0:T(8,128)(2,1)S(1)} %pad_maximum_fusion.2.refs_0_), channel_id=1, source_target_pairs={{0,16},{1,17},{2,18},{3,19},{4,20},{5,21},{6,22},{7,23},{8,24},{9,... | collective-permute-start | bytes 1916936 | tf_op jit(solution)/shard_map/ppermute | solution.py:690
  68.5 26.8 %collective-permute-start.17 = (bf16[4,208,384]{2,1,0:T(8,128)(2,1)}, bf16[4,208,384]{2,1,0:T(8,128)(2,1)}, u32[]{:S(2)}, u32[]{:S(2)}) collective-permute-start(bf16[4,208,384]{2,1,0:T(8,128)(2,1)} %collective-permute-done.13.refs_1_), channel_id=1, source_target_pairs={{0,8},{1,9},{2,10},{3,11},{4,12},{5,13},{6,14},{7,15},{8,0},{9,1},... | collective-permute-start | bytes 1916936 | tf_op jit(solution)/shard_map/ppermute | solution.py:690
  68.5 37.7 %collective-permute-start.15 = (bf16[4,208,384]{2,1,0:T(8,128)(2,1)}, bf16[4,208,384]{2,1,0:T(8,128)(2,1)}, u32[]{:S(2)}, u32[]{:S(2)}) collective-permute-start(bf16[4,208,384]{2,1,0:T(8,128)(2,1)} %collective-permute-done.13.refs_1_), channel_id=1, source_target_pairs={{0,1},{1,0},{2,3},{3,2},{4,5},{5,4},{6,7},{7,6},{8,9},{9,8},{10,11... | collective-permute-start | bytes 1916936 | tf_op jit(solution)/shard_map/ppermute | solution.py:690
  68.6 26.2 %collective-permute-start.18 = (bf16[4,208,384]{2,1,0:T(8,128)(2,1)}, bf16[4,208,384]{2,1,0:T(8,128)(2,1)}, u32[]{:S(2)}, u32[]{:S(2)}) collective-permute-start(bf16[4,208,384]{2,1,0:T(8,128)(2,1)} %collective-permute-done.14.refs_2_), channel_id=1, source_target_pairs={{0,8},{1,9},{2,10},{3,11},{4,12},{5,13},{6,14},{7,15},{8,0},{9,1},... | collective-permute-start | bytes 1916936 | tf_op jit(solution)/shard_map/ppermute | solution.py:690
  92.1 33.5 %copy-start.6 = (bf16[4,208,384]{2,1,0:T(8,128)(2,1)}, bf16[4,208,384]{2,1,0:T(8,128)(2,1)S(1)}, u32[]{:S(2)}) copy-start(bf16[4,208,384]{2,1,0:T(8,128)(2,1)S(1)} %collective-permute-done.3.refs_1_) | copy-start | bytes 1916932
  92.1 15.0 %collective-permute-start.5 = (bf16[4,208,384]{2,1,0:T(8,128)(2,1)S(1)}, bf16[4,208,384]{2,1,0:T(8,128)(2,1)S(1)}, u32[]{:S(2)}, u32[]{:S(2)}) collective-permute-start(bf16[4,208,384]{2,1,0:T(8,128)(2,1)S(1)} %collective-permute-done.3.refs_1_), channel_id=1, source_target_pairs={{0,16},{1,17},{2,18},{3,19},{4,20},{5,21},{6,22},{7,23},{8,24},{9,... | collective-permute-start | bytes 1916936 | tf_op jit(solution)/shard_map/ppermute | solution.py:690
  94.4 31.3 %copy-start.20 = (s32[4,4]{1,0:T(4,128)}, s32[4,4]{1,0:T(4,128)S(1)}, u32[]{:S(2)}) copy-start(s32[4,4]{1,0:T(4,128)S(1)} %sub.25.spot_ref) | copy-start | bytes 196
  94.7 31.0 %copy-start.7 = (bf16[4,208,384]{2,1,0:T(8,128)(2,1)}, bf16[4,208,384]{2,1,0:T(8,128)(2,1)S(1)}, u32[]{:S(2)}) copy-start(bf16[4,208,384]{2,1,0:T(8,128)(2,1)S(1)} %collective-permute-done.4.refs_2_) | copy-start | bytes 1916932
  94.7 31.0 %collective-permute-start.6 = (bf16[4,208,384]{2,1,0:T(8,128)(2,1)S(1)}, bf16[4,208,384]{2,1,0:T(8,128)(2,1)}, u32[]{:S(2)}, u32[]{:S(2)}) collective-permute-start(bf16[4,208,384]{2,1,0:T(8,128)(2,1)S(1)} %pad_maximum_fusion.2.refs_0_), channel_id=1, source_target_pairs={{0,8},{1,9},{2,10},{3,11},{4,12},{5,13},{6,14},{7,15},{8,0},{9,1},... | collective-permute-start | bytes 1916936 | tf_op jit(solution)/shard_map/ppermute | solution.py:690
  94.8 30.9 %collective-permute-start.7 = (bf16[4,208,384]{2,1,0:T(8,128)(2,1)S(1)}, bf16[4,208,384]{2,1,0:T(8,128)(2,1)}, u32[]{:S(2)}, u32[]{:S(2)}) collective-permute-start(bf16[4,208,384]{2,1,0:T(8,128)(2,1)S(1)} %collective-permute-done.3.refs_1_), channel_id=1, source_target_pairs={{0,8},{1,9},{2,10},{3,11},{4,12},{5,13},{6,14},{7,15},{8,0},{9,1},... | collective-permute-start | bytes 1916936 | tf_op jit(solution)/shard_map/ppermute | solution.py:690
  95.3 30.4 %collective-permute-start.8 = (bf16[4,208,384]{2,1,0:T(8,128)(2,1)S(1)}, bf16[4,208,384]{2,1,0:T(8,128)(2,1)}, u32[]{:S(2)}, u32[]{:S(2)}) collective-permute-start(bf16[4,208,384]{2,1,0:T(8,128)(2,1)S(1)} %collective-permute-done.4.refs_2_), channel_id=1, source_target_pairs={{0,8},{1,9},{2,10},{3,11},{4,12},{5,13},{6,14},{7,15},{8,0},{9,1},... | collective-permute-start | bytes 1916936 | tf_op jit(solution)/shard_map/ppermute | solution.py:690
  106.2 4.7 collective-permute-start.19
  107.1 18.6 %collective-permute-start.9 = (bf16[4,208,384]{2,1,0:T(8,128)(2,1)S(1)}, bf16[4,208,384]{2,1,0:T(8,128)(2,1)}, u32[]{:S(2)}, u32[]{:S(2)}) collective-permute-start(bf16[4,208,384]{2,1,0:T(8,128)(2,1)S(1)} %collective-permute-done.5.refs_3_), channel_id=1, source_target_pairs={{0,8},{1,9},{2,10},{3,11},{4,12},{5,13},{6,14},{7,15},{8,0},{9,1},... | collective-permute-start | bytes 1916936 | tf_op jit(solution)/shard_map/ppermute | solution.py:690
  205.9 20.4 %copy-start.27 = (s32[32]{0:T(128)S(1)}, s32[32]{0:T(128)}, u32[]{:S(2)}) copy-start(s32[32]{0:T(128)} %constant.136.clone) | copy-start | bytes 388
  206.8 23.1 %copy-start.12 = (bf16[1,32,768]{2,1,0:T(8,128)(2,1)}, bf16[1,32,768]{2,1,0:T(8,128)(2,1)S(1)}, u32[]{:S(2)}) copy-start(bf16[1,32,768]{2,1,0:T(8,128)(2,1)S(1)} %get-tuple-element.263.own_ref) | copy-start | bytes 147460
  206.8 5.7 %collective-permute-start.21 = (bf16[32,768]{1,0:T(8,128)(2,1)S(1)}, bf16[32,768]{1,0:T(8,128)(2,1)S(1)}, u32[]{:S(2)}, u32[]{:S(2)}) collective-permute-start(bf16[32,768]{1,0:T(8,128)(2,1)S(1)} %get-tuple-element.264), channel_id=1, source_target_pairs={{0,4},{1,5},{2,6},{3,7},{4,0},{5,1},{6,2},{7,3},{8,12},{9,13},{10,... | collective-permute-start | bytes 147464 | tf_op jit(solution)/shard_map/ppermute | solution.py:690
  208.4 4.5 collective-permute-start.20
  208.9 5.9 %collective-permute-start.22 = (bf16[32,768]{1,0:T(8,128)(2,1)S(1)}, bf16[32,768]{1,0:T(8,128)(2,1)S(1)}, u32[]{:S(2)}, u32[]{:S(2)}) collective-permute-start(bf16[32,768]{1,0:T(8,128)(2,1)S(1)} %get-tuple-element.264), channel_id=1, source_target_pairs={{0,6},{1,7},{2,4},{3,5},{4,2},{5,3},{6,0},{7,1},{8,14},{9,15},{10,... | collective-permute-start | bytes 147464 | tf_op jit(solution)/shard_map/ppermute | solution.py:690
  214.8 7.0 %collective-permute-start.24 = (bf16[4,32,768]{2,1,0:T(8,128)(2,1)S(1)}, bf16[4,32,768]{2,1,0:T(8,128)(2,1)S(1)}, u32[]{:S(2)}, u32[]{:S(2)}) collective-permute-start(bf16[4,32,768]{2,1,0:T(8,128)(2,1)S(1)} %get-tuple-element.262), channel_id=1, source_target_pairs={{0,16},{1,17},{2,18},{3,19},{4,20},{5,21},{6,22},{7,23},{8,24},{9,... | collective-permute-start | bytes 589832 | tf_op jit(solution)/shard_map/ppermute | solution.py:690
  216.3 7.7 %collective-permute-start.23 = (bf16[4,32,768]{2,1,0:T(8,128)(2,1)S(1)}, bf16[4,32,768]{2,1,0:T(8,128)(2,1)S(1)}, u32[]{:S(2)}, u32[]{:S(2)}) collective-permute-start(bf16[4,32,768]{2,1,0:T(8,128)(2,1)S(1)} %get-tuple-element.262), channel_id=1, source_target_pairs={{0,1},{1,0},{2,3},{3,2},{4,5},{5,4},{6,7},{7,6},{8,9},{9,8},{10,11... | collective-permute-start | bytes 589832 | tf_op jit(solution)/shard_map/ppermute | solution.py:690
  216.9 9.2 %collective-permute-start.25 = (bf16[4,32,768]{2,1,0:T(8,128)(2,1)S(1)}, bf16[4,32,768]{2,1,0:T(8,128)(2,1)S(1)}, u32[]{:S(2)}, u32[]{:S(2)}) collective-permute-start(bf16[4,32,768]{2,1,0:T(8,128)(2,1)S(1)} %get-tuple-element.262), channel_id=1, source_target_pairs={{0,17},{1,16},{2,19},{3,18},{4,21},{5,20},{6,23},{7,22},{8,25},{9,... | collective-permute-start | bytes 589832 | tf_op jit(solution)/shard_map/ppermute | solution.py:690
  226.2 2.4 collective-permute-start.26
  295.8 14.2 %collective-permute-start.27 = (bf16[2,2,4,384,384]{4,3,2,1,0:T(8,128)(2,1)}, bf16[2,2,4,384,384]{4,3,2,1,0:T(8,128)(2,1)}, u32[]{:S(2)}, u32[]{:S(2)}) collective-permute-start(bf16[2,2,4,384,384]{4,3,2,1,0:T(8,128)(2,1)} %get-tuple-element.165), channel_id=1, source_target_pairs={{0,8},{1,9},{2,10},{3,11},{4,12},{5,13},{6,14},{7,15},{8,0},{9,1},... | collective-permute-start | bytes 14155784 | tf_op jit(solution)/shard_map/ppermute | solution.py:690
  314.3 28.5 %collective-permute-start.29 = (bf16[2,4,192,384]{3,2,1,0:T(8,128)(2,1)}, bf16[2,4,192,384]{3,2,1,0:T(8,128)(2,1)S(1)}, u32[]{:S(2)}, u32[]{:S(2)}) collective-permute-start(bf16[2,4,192,384]{3,2,1,0:T(8,128)(2,1)} %get-tuple-element.235), channel_id=1, source_target_pairs={{0,1},{1,0},{2,3},{3,2},{4,5},{5,4},{6,7},{7,6},{8,9},{9,8},{10,11... | collective-permute-start | bytes 3538952 | tf_op jit(solution)/shard_map/ppermute | solution.py:690
  315.8 28.0 %collective-permute-start.28 = (bf16[2,4,192,384]{3,2,1,0:T(8,128)(2,1)S(1)}, bf16[2,4,192,384]{3,2,1,0:T(8,128)(2,1)S(1)}, u32[]{:S(2)}, u32[]{:S(2)}) collective-permute-start(bf16[2,4,192,384]{3,2,1,0:T(8,128)(2,1)S(1)} %get-tuple-element.236), channel_id=1, source_target_pairs={{0,16},{1,17},{2,18},{3,19},{4,20},{5,21},{6,22},{7,23},{8,24},{9,... | collective-permute-start | bytes 3538952 | tf_op jit(solution)/shard_map/ppermute | solution.py:690
  346.2 30.3 %collective-permute-start.30 = (bf16[2,2,4,208,384]{4,3,2,1,0:T(8,128)(2,1)}, bf16[2,2,4,208,384]{4,3,2,1,0:T(8,128)(2,1)}, u32[]{:S(2)}, u32[]{:S(2)}) collective-permute-start(bf16[2,2,4,208,384]{4,3,2,1,0:T(8,128)(2,1)} %get-tuple-element.178), channel_id=1, source_target_pairs={{0,8},{1,9},{2,10},{3,11},{4,12},{5,13},{6,14},{7,15},{8,0},{9,1},... | collective-permute-start | bytes 7667720 | tf_op jit(solution)/shard_map/ppermute | solution.py:690
  346.3 24.2 %collective-permute-start.32 = (bf16[4,192,384]{2,1,0:T(8,128)(2,1)S(1)}, bf16[4,192,384]{2,1,0:T(8,128)(2,1)S(1)}, u32[]{:S(2)}, u32[]{:S(2)}) collective-permute-start(bf16[4,192,384]{2,1,0:T(8,128)(2,1)S(1)} %get-tuple-element.233), channel_id=1, source_target_pairs={{0,16},{1,17},{2,18},{3,19},{4,20},{5,21},{6,22},{7,23},{8,24},{9,... | collective-permute-start | bytes 1769480 | tf_op jit(solution)/shard_map/ppermute | solution.py:690
  347.0 23.9 %collective-permute-start.31 = (bf16[4,192,384]{2,1,0:T(8,128)(2,1)S(1)}, bf16[4,192,384]{2,1,0:T(8,128)(2,1)}, u32[]{:S(2)}, u32[]{:S(2)}) collective-permute-start(bf16[4,192,384]{2,1,0:T(8,128)(2,1)S(1)} %get-tuple-element.234), channel_id=1, source_target_pairs={{0,1},{1,0},{2,3},{3,2},{4,5},{5,4},{6,7},{7,6},{8,9},{9,8},{10,11... | collective-permute-start | bytes 1769480 | tf_op jit(solution)/shard_map/ppermute | solution.py:690
  378.7 23.1 %collective-permute-start.33 = (bf16[2,4,112,384]{3,2,1,0:T(8,128)(2,1)}, bf16[2,4,112,384]{3,2,1,0:T(8,128)(2,1)}, u32[]{:S(2)}, u32[]{:S(2)}) collective-permute-start(bf16[2,4,112,384]{3,2,1,0:T(8,128)(2,1)} %fusion.4), channel_id=1, source_target_pairs={{0,16},{1,17},{2,18},{3,19},{4,20},{5,21},{6,22},{7,23},{8,24},{9,... | collective-permute-start | bytes 2064392 | tf_op jit(solution)/shard_map/ppermute | solution.py:690
  382.1 17.5 %collective-permute-start.34 = (bf16[2,4,96,384]{3,2,1,0:T(8,128)(2,1)}, bf16[2,4,96,384]{3,2,1,0:T(8,128)(2,1)}, u32[]{:S(2)}, u32[]{:S(2)}) collective-permute-start(bf16[2,4,96,384]{3,2,1,0:T(8,128)(2,1)} %fusion.12), channel_id=1, source_target_pairs={{0,1},{1,0},{2,3},{3,2},{4,5},{5,4},{6,7},{7,6},{8,9},{9,8},{10,11... | collective-permute-start | bytes 1769480 | tf_op jit(solution)/shard_map/ppermute | solution.py:690
  382.8 21.0 %copy-start.22 = (f32[8,1]{1,0:T(8,128)S(1)}, f32[8,1]{1,0:T(8,128)}, u32[]{:S(2)}) copy-start(f32[8,1]{1,0:T(8,128)} %get-tuple-element.141) | copy-start | bytes 100
  403.8 13.2 %collective-permute-start.37 = (bf16[2,2,4,208,384]{4,3,2,1,0:T(8,128)(2,1)}, bf16[2,2,4,208,384]{4,3,2,1,0:T(8,128)(2,1)}, u32[]{:S(2)}, u32[]{:S(2)}) collective-permute-start(bf16[2,2,4,208,384]{4,3,2,1,0:T(8,128)(2,1)} %get-tuple-element.202), channel_id=1, source_target_pairs={{0,8},{1,9},{2,10},{3,11},{4,12},{5,13},{6,14},{7,15},{8,0},{9,1},... | collective-permute-start | bytes 7667720 | tf_op jit(solution)/shard_map/ppermute | solution.py:690
  404.4 53.5 %collective-permute-start.41 = (bf16[384,384]{1,0:T(8,128)(2,1)}, bf16[384,384]{1,0:T(8,128)(2,1)}, u32[]{:S(2)}, u32[]{:S(2)}) collective-permute-start(bf16[384,384]{1,0:T(8,128)(2,1)} %pad_maximum_fusion.6), channel_id=1, source_target_pairs={{0,2},{1,3},{2,0},{3,1},{4,6},{5,7},{6,4},{7,5},{8,10},{9,11},{10,... | collective-permute-start | bytes 884744 | tf_op jit(solution)/shard_map/ppermute | solution.py:690
  405.4 51.0 %collective-permute-start.42 = (bf16[384,384]{1,0:T(8,128)(2,1)}, bf16[384,384]{1,0:T(8,128)(2,1)}, u32[]{:S(2)}, u32[]{:S(2)}) collective-permute-start(bf16[384,384]{1,0:T(8,128)(2,1)} %pad_maximum_fusion.7), channel_id=1, source_target_pairs={{0,4},{1,5},{2,6},{3,7},{4,0},{5,1},{6,2},{7,3},{8,12},{9,13},{10,... | collective-permute-start | bytes 884744 | tf_op jit(solution)/shard_map/ppermute | solution.py:690
  407.4 16.8 %collective-permute-start.35 = (bf16[4,112,384]{2,1,0:T(8,128)(2,1)}, bf16[4,112,384]{2,1,0:T(8,128)(2,1)S(1)}, u32[]{:S(2)}, u32[]{:S(2)}) collective-permute-start(bf16[4,112,384]{2,1,0:T(8,128)(2,1)} %fusion.7), channel_id=1, source_target_pairs={{0,1},{1,0},{2,3},{3,2},{4,5},{5,4},{6,7},{7,6},{8,9},{9,8},{10,11... | collective-permute-start | bytes 1032200 | tf_op jit(solution)/shard_map/ppermute | solution.py:690
  409.8 12.9 %collective-permute-start.36 = (bf16[4,96,384]{2,1,0:T(8,128)(2,1)}, bf16[4,96,384]{2,1,0:T(8,128)(2,1)S(1)}, u32[]{:S(2)}, u32[]{:S(2)}) collective-permute-start(bf16[4,96,384]{2,1,0:T(8,128)(2,1)} %fusion.18), channel_id=1, source_target_pairs={{0,16},{1,17},{2,18},{3,19},{4,20},{5,21},{6,22},{7,23},{8,24},{9,... | collective-permute-start | bytes 884744 | tf_op jit(solution)/shard_map/ppermute | solution.py:690
  419.4 19.0 %collective-permute-start.44 = (bf16[2,4,112,384]{3,2,1,0:T(8,128)(2,1)}, bf16[2,4,112,384]{3,2,1,0:T(8,128)(2,1)}, u32[]{:S(2)}, u32[]{:S(2)}) collective-permute-start(bf16[2,4,112,384]{3,2,1,0:T(8,128)(2,1)} %fusion.5), channel_id=1, source_target_pairs={{0,16},{1,17},{2,18},{3,19},{4,20},{5,21},{6,22},{7,23},{8,24},{9,... | collective-permute-start | bytes 2064392 | tf_op jit(solution)/shard_map/ppermute | solution.py:690
  422.7 15.6 %collective-permute-start.45 = (bf16[2,4,96,384]{3,2,1,0:T(8,128)(2,1)}, bf16[2,4,96,384]{3,2,1,0:T(8,128)(2,1)}, u32[]{:S(2)}, u32[]{:S(2)}) collective-permute-start(bf16[2,4,96,384]{3,2,1,0:T(8,128)(2,1)} %fusion.13), channel_id=1, source_target_pairs={{0,1},{1,0},{2,3},{3,2},{4,5},{5,4},{6,7},{7,6},{8,9},{9,8},{10,11... | collective-permute-start | bytes 1769480 | tf_op jit(solution)/shard_map/ppermute | solution.py:690
  439.6 10.1 %collective-permute-start.47 = (bf16[4,96,384]{2,1,0:T(8,128)(2,1)S(1)}, bf16[4,96,384]{2,1,0:T(8,128)(2,1)S(1)}, u32[]{:S(2)}, u32[]{:S(2)}) collective-permute-start(bf16[4,96,384]{2,1,0:T(8,128)(2,1)S(1)} %fusion.17), channel_id=1, source_target_pairs={{0,16},{1,17},{2,18},{3,19},{4,20},{5,21},{6,22},{7,23},{8,24},{9,... | collective-permute-start | bytes 884744 | tf_op jit(solution)/shard_map/ppermute | solution.py:690
  441.5 9.9 %collective-permute-start.46 = (bf16[4,112,384]{2,1,0:T(8,128)(2,1)S(1)}, bf16[4,112,384]{2,1,0:T(8,128)(2,1)S(1)}, u32[]{:S(2)}, u32[]{:S(2)}) collective-permute-start(bf16[4,112,384]{2,1,0:T(8,128)(2,1)S(1)} %fusion.6), channel_id=1, source_target_pairs={{0,1},{1,0},{2,3},{3,2},{4,5},{5,4},{6,7},{7,6},{8,9},{9,8},{10,11... | collective-permute-start | bytes 1032200 | tf_op jit(solution)/shard_map/ppermute | solution.py:690
  442.5 15.6 %collective-permute-start.43 = (bf16[384,384]{1,0:T(8,128)(2,1)S(1)}, bf16[384,384]{1,0:T(8,128)(2,1)S(1)}, u32[]{:S(2)}, u32[]{:S(2)}) collective-permute-start(bf16[384,384]{1,0:T(8,128)(2,1)S(1)} %pad_maximum_fusion.8), channel_id=1, source_target_pairs={{0,6},{1,7},{2,4},{3,5},{4,2},{5,3},{6,0},{7,1},{8,14},{9,15},{10,... | collective-permute-start | bytes 884744 | tf_op jit(solution)/shard_map/ppermute | solution.py:690
  449.8 23.2 %collective-permute-start.38 = (bf16[208,384]{1,0:T(8,128)(2,1)S(1)}, bf16[208,384]{1,0:T(8,128)(2,1)S(1)}, u32[]{:S(2)}, u32[]{:S(2)}) collective-permute-start(bf16[208,384]{1,0:T(8,128)(2,1)S(1)} %copy-done.18), channel_id=1, source_target_pairs={{0,2},{1,3},{2,0},{3,1},{4,6},{5,7},{6,4},{7,5},{8,10},{9,11},{10,... | collective-permute-start | bytes 479240 | tf_op jit(solution)/shard_map/ppermute | solution.py:690
  451.3 21.7 %collective-permute-start.39 = (bf16[208,384]{1,0:T(8,128)(2,1)S(1)}, bf16[208,384]{1,0:T(8,128)(2,1)S(1)}, u32[]{:S(2)}, u32[]{:S(2)}) collective-permute-start(bf16[208,384]{1,0:T(8,128)(2,1)S(1)} %pad_maximum_fusion.11), channel_id=1, source_target_pairs={{0,4},{1,5},{2,6},{3,7},{4,0},{5,1},{6,2},{7,3},{8,12},{9,13},{10,... | collective-permute-start | bytes 479240 | tf_op jit(solution)/shard_map/ppermute | solution.py:690
  456.4 16.6 %collective-permute-start.40 = (bf16[208,384]{1,0:T(8,128)(2,1)S(1)}, bf16[208,384]{1,0:T(8,128)(2,1)S(1)}, u32[]{:S(2)}, u32[]{:S(2)}) collective-permute-start(bf16[208,384]{1,0:T(8,128)(2,1)S(1)} %pad_maximum_fusion.12), channel_id=1, source_target_pairs={{0,6},{1,7},{2,4},{3,5},{4,2},{5,3},{6,0},{7,1},{8,14},{9,15},{10,... | collective-permute-start | bytes 479240 | tf_op jit(solution)/shard_map/ppermute | solution.py:690
  457.9 30.4 %collective-permute-start.48 = (bf16[208,384]{1,0:T(8,128)(2,1)S(1)}, bf16[208,384]{1,0:T(8,128)(2,1)S(1)}, u32[]{:S(2)}, u32[]{:S(2)}) collective-permute-start(bf16[208,384]{1,0:T(8,128)(2,1)S(1)} %pad_maximum_fusion.13), channel_id=1, source_target_pairs={{0,2},{1,3},{2,0},{3,1},{4,6},{5,7},{6,4},{7,5},{8,10},{9,11},{10,... | collective-permute-start | bytes 479240 | tf_op jit(solution)/shard_map/ppermute | solution.py:690
  473.1 15.2 %collective-permute-start.49 = (bf16[208,384]{1,0:T(8,128)(2,1)S(1)}, bf16[208,384]{1,0:T(8,128)(2,1)S(1)}, u32[]{:S(2)}, u32[]{:S(2)}) collective-permute-start(bf16[208,384]{1,0:T(8,128)(2,1)S(1)} %pad_maximum_fusion.14), channel_id=1, source_target_pairs={{0,4},{1,5},{2,6},{3,7},{4,0},{5,1},{6,2},{7,3},{8,12},{9,13},{10,... | collective-permute-start | bytes 479240 | tf_op jit(solution)/shard_map/ppermute | solution.py:690
  476.9 11.5 %collective-permute-start.50 = (bf16[208,384]{1,0:T(8,128)(2,1)S(1)}, bf16[208,384]{1,0:T(8,128)(2,1)S(1)}, u32[]{:S(2)}, u32[]{:S(2)}) collective-permute-start(bf16[208,384]{1,0:T(8,128)(2,1)S(1)} %pad_maximum_fusion.15), channel_id=1, source_target_pairs={{0,6},{1,7},{2,4},{3,5},{4,2},{5,3},{6,0},{7,1},{8,14},{9,15},{10,... | collective-permute-start | bytes 479240 | tf_op jit(solution)/shard_map/ppermute | solution.py:690
  (17 other events, 101.6 us)
Sparse Core Ops, SparseCore 0:
  11.6 157.6 all-gather.2
  296.2 163.5 reduce-scatter.1

commit v4 on v3

--- a/solution.py
+++ b/solution.py
@@ -286,7 +286,9 @@
     )(here, spots, *packs, xhat, vec, bup)
 
 
-def loss_kernel(scale, q_count, p_count, ids_ref, own_ids_ref, heads_ref, own_ref, loss_ref, gq_ref, gp_ref):
+def loss_kernel(scale, q_count, p_count, ids_ref, own_ids_ref, own_ref, *refs):
+    *heads, loss_ref, gq_ref, gp_ref = refs
+
     def split_mm(dot, left, right):
         high = left.astype(BF16)
         rest = left - high.astype(F32)
@@ -311,7 +313,7 @@
         code = wide[:, p_count + q_count :, :128].reshape(-1, 128)
         return p_rows, q_rows, (code[:, 0:1] * 256.0 + code[:, 1:2]).astype(jnp.int32)
 
-    p_all, q_all, hit_all = parts(heads_ref[...])
+    p_all, q_all, hit_all = parts(jnp.concatenate([ref[...] for ref in heads]))
     p_own, q_own, hit_own = parts(own_ref[...])
     norm_all = log_norm(mm_nt(q_all, p_all) * scale)
     own_rows = mm_nt(q_own, p_all) * scale
@@ -327,7 +329,7 @@
 
 
 def loss_part(ids, own_ids, heads, own, q_spots, p_spots):
-    d = heads.shape[2]
+    d = own.shape[2]
     q_count, p_count = math.prod(q_spots), math.prod(p_spots)
     return pl.pallas_call(
         functools.partial(loss_kernel, 3.0 / math.sqrt(d), q_count, p_count),
@@ -338,7 +340,7 @@
         ],
         compiler_params=pltpu.CompilerParams(vmem_limit_bytes=60 * MIB),
         name="loss_part",
-    )(ids, own_ids, heads, own)
+    )(ids, own_ids, own, *heads)
 
 
 def ffn_bwd_kernel(place, goal, steps, here_ref, spot_ref, *refs):
@@ -482,16 +484,17 @@
         v2 = qkv_ref[:, v_lanes]
         g2 = att_grad[:, lanes]
         dq, dk, dv = [], [], []
+        q_t, k_t, g_t = q2.T, k2.T, g2.T
         for h in range(2):
-            scores = mm_nt(k2 * keep[h], q2) + blocked
+            scores = mm(k2 * keep[h], q_t) + blocked
             terms = jnp.exp(scores - jnp.max(scores, axis=0, keepdims=True))
             prob = terms * (1.0 / jnp.sum(terms, axis=0, keepdims=True))
-            weighed = prob * mm_nt(v2 * keep[h], g2)
+            weighed = prob * mm(v2 * keep[h], g_t)
             sgrad = (weighed - prob * jnp.sum(weighed, axis=0, keepdims=True)).astype(BF16)
             dv.append(mm(prob.astype(BF16), g2))
             dk.append(mm(sgrad, q2))
-            dq.append(mm_tn(sgrad, k2))
-        proj[:, lanes] = (jnp.where(low_half, dq[0], dq[1]) * (HD ** -0.5)).astype(BF16)
+            dq.append(mm(k_t[h * HD : (h + 1) * HD], sgrad))
+        proj[:, lanes] = (jnp.concatenate(dq, axis=0) * (HD ** -0.5)).astype(BF16).T
         proj[:, k_lanes] = jnp.where(low_half, dk[0], dk[1]).astype(BF16)
         proj[:, v_lanes] = jnp.where(low_half, dv[0], dv[1]).astype(BF16)
     gvec[4:5, :] += col_sum(proj[:, :d].astype(F32))
@@ -710,7 +713,8 @@
 def gather_heads(block):
     near = jnp.stack([block] + [swap(block, way) for way in ("z1", "z2", "z3")])
     wide = jnp.stack([near] + [swap(near, way) for way in ("x", "y", "xy")])
-    return jnp.stack([wide, swap(wide, "core")]).reshape((-1,) + block.shape)
+    wide = wide.reshape((-1,) + block.shape)
+    return [wide, swap(wide, "core")]
 
 
 HEAD_ORDER = [c ^ s ^ z for c in (0, 8) for s in (0, 1, 16, 17) for z in (0, 2, 4, 6)]
@@ -858,7 +862,7 @@
         done[e] = line.run(
             lambda *packs, e=e: ffn_fwd(ffn_into[e], here, spots[e], packs, half[e][2], half[e][6], half[e][7]), *ffn_w[e])
     own = jnp.concatenate([done[1][5].reshape(p_count, d).astype(BF16), done[0][5].reshape(q_count, d).astype(BF16), code])
-    heads = gather_heads(own) if near else lax.all_gather(own, BOTH, axis=0)
+    heads = gather_heads(own) if near else [lax.all_gather(own, BOTH, axis=0)]
     losses, *gcls = loss_part(ids, own_ids, heads, own[None], spots[0].shape, spots[1].shape)
 
     def ffn_step(e, goal, cot):
@@ -902,6 +906,7 @@
         attn_q.step(1, line)
         attn_p = Scatter(*line.run(lambda *rows: attn_weights(1, goals, rows, gbup_p), *rows_p), cut)
         attn_q.step(2, line)
+        sums = [ffn_p.total(line)]
         attn_p.step(0, line)
         gx_q = line.run(lambda proj: input_grad(proj, half[0][4], dh_q), rows_q[0])
         attn_p.step(1, line)
@@ -909,8 +914,8 @@
         gx_p = line.run(lambda proj: input_grad(proj, half[1][4], dh_p), rows_p[0])
         gx = (gx_q, gx_p)
         attn_p.step(2, line)
+        sums.append(attn_q.total(line))
         attn_p.step(3, line)
-        sums = [ffn_p.total(line), attn_q.total(line)]
         sum_q = line.wait((sum_q,))[0]
         sums.append(attn_p.total(line))
         ffn_sum = [sum_q.astype(F32), sums[0]]

time: 508 us -> 505 us (level)
  waiting for transfers between devices: 146 us -> 129 us
  starting transfers between devices: 65.8 us -> 71.8 us
  other arithmetic: 51.2 us -> 56.7 us
    ppermute x51, waiting for transfers between devices: 124 us -> 107 us  [swap(): return lax.ppermute(block, BOTH, [(i, i ^ BITS[way]) for i in range(32)])]
    ppermute x51, starting transfers between devices: 65.7 us -> 71.7 us  [swap(): return lax.ppermute(block, BOTH, [(i, i ^ BITS[way]) for i in range(32)])]
    another operation x9 -> x6, other arithmetic: 13 us -> 11.6 us
  transfers between devices with their start and end apart: 53 -> 53, of which waited for: 26 -> 24; matrix products, arithmetic and copies ran while one was open for 9% -> 11% of each run, Pallas kernels for 23% -> 23%
where the time goes in v4:
time: 505 us; the launch traced here: 495 us
  Pallas kernels  215 us (43%)
  waiting for transfers between devices  129 us (26%)
  starting transfers between devices  71.8 us (14%)
  other arithmetic  56.7 us (11%)
  between operations  15.1 us (3%)
  local copies, waits for them, and re-layouts  7.42 us (1%)
    ppermute x51, waiting for transfers between devices, swap(): return lax.ppermute(block, BOTH, [(i, i ^ BITS[way]) for i in range(32)])  107 us
    ppermute x51, starting transfers between devices, swap(): return lax.ppermute(block, BOTH, [(i, i ^ BITS[way]) for i in range(32)])  71.7 us
    pallas_call x2, Pallas kernels, ffn_bwd(): pl.pallas_call(functools.partial(ffn_bwd_kernel, place, goal, steps), gri...  62.3 us
    pallas_call x3, Pallas kernels, attn_bwd(): pl.pallas_call(kernel, grid=(last - first,), in_specs=[row(d), row(3 * d)...  41.8 us
    pallas_call x2, Pallas kernels, attn_fwd(): pl.pallas_call(functools.partial(attn_fwd_kernel, dims, place), grid=(ste...  36.3 us
    pallas_call x2, Pallas kernels, ffn_fwd(): pl.pallas_call(functools.partial(ffn_fwd_kernel, place), grid=(steps,), i...  35.3 us
    convert_element_type x10, other arithmetic, step(): parts = [self.sum(part, 1).astype(BF16) for part in range(2)]  23.3 us
    all_gather x1, waiting for transfers between devices, body(): lax.all_gather(ffn_pack, BOTH, axis=0).reshape((npb, npa) + ffn_pack.shape)  22 us
  transfers between devices with their start and end apart: 53, of which 24 were waited for; matrix products, arithmetic and copies ran while one was open for 11% of the time, Pallas kernels for 23%

profile of v4, /device:TPU:0, one launch (start us, length us, event | category | flops | bytes accessed | tf_op | source)
XLA Modules:
  0.0 494.7 jit_solution(3216325297559774938)
XLA Ops:
  8.3 1.8 pad_maximum_fusion.4
  10.5 5.1 %collective-permute-start.12 = (bf16[208,384]{1,0:T(8,128)(2,1)S(1)}, bf16[208,384]{1,0:T(8,128)(2,1)S(1)}, u32[]{:S(2)}, u32[]{:S(2)}) collective-permute-start(bf16[208,384]{1,0:T(8,128)(2,1)S(1)} %get-tuple-element.255), channel_id=1, source_target_pairs={{0,6},{1,7},{2,4},{3,5},{4,2},{5,3},{6,0},{7,1},{8,14},{9,15},{10,... | collective-permute-start | bytes 479240 | tf_op jit(solution)/shard_map/ppermute | solution.py:693
  16.2 3.7 collective-permute-start.2
  20.6 9.3 %collective-permute-start = (bf16[208,384]{1,0:T(8,128)(2,1)S(1)}, bf16[208,384]{1,0:T(8,128)(2,1)S(1)}, u32[]{:S(2)}, u32[]{:S(2)}) collective-permute-start(bf16[208,384]{1,0:T(8,128)(2,1)S(1)} %get-tuple-element.254), channel_id=1, source_target_pairs={{0,2},{1,3},{2,0},{3,1},{4,6},{5,7},{6,4},{7,5},{8,10},{9,11},{10,... | collective-permute-start | bytes 479240 | tf_op jit(solution)/shard_map/ppermute | solution.py:693
  30.0 14.7 %collective-permute-done.11 = bf16[208,384]{1,0:T(8,128)(2,1)S(1)} collective-permute-done((bf16[208,384]{1,0:T(8,128)(2,1)S(1)}, bf16[208,384]{1,0:T(8,128)(2,1)S(1)}, u32[]{:S(2)}, u32[]{:S(2)}) %collective-permute-start.11) | collective-permute-done | bytes 159776 | tf_op jit(solution)/shard_map/ppermute | solution.py:693
  44.9 2.0 collective-permute-start.14
  46.9 1.6 collective-permute-start.13
  48.5 7.0 %collective-permute-done.1 = bf16[208,384]{1,0:T(8,128)(2,1)S(1)} collective-permute-done((bf16[208,384]{1,0:T(8,128)(2,1)S(1)}, bf16[208,384]{1,0:T(8,128)(2,1)S(1)}, u32[]{:S(2)}, u32[]{:S(2)}) %collective-permute-start.1) | collective-permute-done | bytes 159776 | tf_op jit(solution)/shard_map/ppermute | solution.py:693
  55.6 1.6 collective-permute-start.3
  57.2 1.5 collective-permute-start.4
  58.8 9.7 %collective-permute-done.13.refs_1_ = bf16[4,208,384]{2,1,0:T(8,128)(2,1)} collective-permute-done((bf16[4,208,384]{2,1,0:T(8,128)(2,1)S(1)}, bf16[4,208,384]{2,1,0:T(8,128)(2,1)}, u32[]{:S(2)}, u32[]{:S(2)}) %collective-permute-start.13) | collective-permute-done | bytes 639008 | tf_op jit(solution)/shard_map/ppermute | solution.py:693
  69.3 22.8 %collective-permute-done.3.refs_1_ = bf16[4,208,384]{2,1,0:T(8,128)(2,1)S(1)} collective-permute-done((bf16[4,208,384]{2,1,0:T(8,128)(2,1)S(1)}, bf16[4,208,384]{2,1,0:T(8,128)(2,1)S(1)}, u32[]{:S(2)}, u32[]{:S(2)}) %collective-permute-start.3) | collective-permute-done | bytes 639008 | tf_op jit(solution)/shard_map/ppermute | solution.py:693
  92.1 1.9 collective-permute-start.5
  95.3 10.8 %collective-permute-done.15.refs_3_ = bf16[4,208,384]{2,1,0:T(8,128)(2,1)} collective-permute-done((bf16[4,208,384]{2,1,0:T(8,128)(2,1)}, bf16[4,208,384]{2,1,0:T(8,128)(2,1)}, u32[]{:S(2)}, u32[]{:S(2)}) %collective-permute-start.15) | collective-permute-done | bytes 639008 | tf_op jit(solution)/shard_map/ppermute | solution.py:693
  110.9 14.7 %attn_fwd.2 = (bf16[512,2304]{1,0:T(8,128)(2,1)}, bf16[512,768]{1,0:T(8,128)(2,1)}, f32[512,768]{1,0:T(8,128)}, f32[512,1]{1,0:T(8,128)}, bf16[768,2304]{1,0:T(8...) custom-call(s32[4]{0:T(128)} %pad_add_fusion.2.here_ref, ...), custom_call_target="tpu_custom_call" | custom-call | flops 1 | bytes 1 | tf_op jit(solution)/shard_map/attn_fwd/pallas_call | solution.py:154
  125.7 21.6 %attn_fwd.3 = (bf16[1024,2304]{1,0:T(8,128)(2,1)}, bf16[1024,768]{1,0:T(8,128)(2,1)}, f32[1024,768]{1,0:T(8,128)}, f32[1024,1]{1,0:T(8,128)}, bf16[768,2304]{1,0...) custom-call(s32[4]{0:T(128)} %pad_add_fusion.2.here_ref, ...), custom_call_target="tpu_custom_call" | custom-call | flops 1 | bytes 1 | tf_op jit(solution)/shard_map/attn_fwd/pallas_call | solution.py:154
  147.3 22.0 %all-gather.3.cloned.1.call-done = bf16[64,384,384]{2,1,0:T(8,128)(2,1)} async-done(((bf16[2,384,384]{2,1,0:T(8,128)(2,1)}), bf16[64,384,384]{2,1,0:T(8,128)(2,1)}) %all-gather.3.cloned.1.call-update) | async-done | bytes 18874384 | tf_op jit(solution)/shard_map/all_gather | solution.py:811
  169.9 13.2 %ffn_fwd.2 = (bf16[512,3072]{1,0:T(8,128)(2,1)}, bf16[512,3072]{1,0:T(8,128)(2,1)}, f32[512,768]{1,0:T(8,128)}, f32[512,1]{1,0:T(8,128)}, bf16[512,768]{1,0:T(8,128)(2,1)}, /*index=5*/f32[2,4,768]{2,1,0:T(4,128)}) custom-call(s32[4]{0:T(128)} %pad_add_fusion.2.here_ref, s32[2,4]{1,0:T(2,128)} %broadcast_in_dim.14.spot_ref, ...), custom_call_target="tpu_custom_call" | custom-call | flops 1 | bytes 1 | tf_op jit(solution)/shard_map/ffn_fwd/pallas_call | solution.py:268
  183.9 22.1 %ffn_fwd.3 = (bf16[1024,3072]{1,0:T(8,128)(2,1)}, bf16[1024,3072]{1,0:T(8,128)(2,1)}, f32[1024,768]{1,0:T(8,128)}, f32[1024,1]{1,0:T(8,128)}, bf16[1024,768]{1,0:T(8,128)(2,1)}, /*index=5*/f32[4,4,768]{2,1,0:T(4,128)}) custom-call(s32[4]{0:T(128)} %pad_add_fusion.2.here_ref, s32[4,4]{1,0:T(4,128)} %copy-done.22, bf16[4,8,2,384,384]{4,3,2,1,0:T(8,128)(2,1)} %bitcast.291, ...), custom_call_target="tpu_custom_call" | custom-call | flops 1 | bytes 1 | tf_op jit(solution)/shard_map/ffn_fwd/pallas_call | solution.py:268
  206.8 1.6 collective-permute-start.21
  208.9 2.4 collective-permute-start.22
  212.9 1.9 collective-permute-done.22
  214.8 1.5 collective-permute-start.24
  218.3 3.4 collective-permute-done.24
  221.8 2.2 collective-permute-done.23
  224.0 2.1 collective-permute-done.25
  229.5 3.7 loss_part.1
  233.1 24.0 %ffn_bwd.2 = (f32[512,768]{1,0:T(8,128)}, bf16[4,8,384,384]{3,2,1,0:T(8,128)(2,1)}, f32[8,768]{1,0:T(8,128)}, f32[4,768]{1,0:T(4,128)}) custom-call(s32[4]{0:T(128)} %pad_add_fusion.2.here_ref, s32[2,4]{1,0:T(2,128)} %broadcast_in_dim.14.spot_ref, bf16[4,8,2,384,384]{4,3,2,1,0:T(8,128)(2,1)} %bitcast.292, bf16[512,768]{1,0:T(8,128)(2,1)} %bitcast.311, ...), custom_call_target="tpu_custom_call" | custom-call | flops 1 | bytes 1 | tf_op jit(solution)/shard_map/ffn_bwd/pallas_call | solution.py:442
  257.1 38.3 %ffn_bwd.3 = (f32[1024,768]{1,0:T(8,128)}, bf16[2,2,4,384,384]{4,3,2,1,0:T(8,128)(2,1)}, bf16[2,2,4,384,384]{4,3,2,1,0:T(8,128)(2,1)}, f32[8,768]{1,0:T(8,128)}, f32[4,768]{1,0:T(4,128)}) custom-call(s32[4]{0:T(128)} %pad_add_fusion.2.here_ref, s32[4,4]{1,0:T(4,128)} %copy-done.22, bf16[4,8,2,384,384]{4,3,2,1,0:T(8,128)(2,1)} %bitcast.293, ...), custom_call_target="tpu_custom_call" | custom-call | flops 1 | bytes 1 | tf_op jit(solution)/shard_map/ffn_bwd/pallas_call | solution.py:442
  295.7 13.8 %attn_bwd.3 = (bf16[512,2304]{1,0:T(8,128)(2,1)}, bf16[512,768]{1,0:T(8,128)(2,1)}, f32[8,768]{1,0:T(8,128)}) custom-call(f32[512,768]{1,0:T(8,128)} %get-tuple-element.156.refs_0_.dh_ref, bf16[512,2304]{1,0:T(8,128)(2,1)} %get-tuple-element.117.refs_1_, bf16[768,768]{1,0:T(8,128)(2,1)} %get-tuple-element.157.refs_2_, s32[2,256,2]{2,1,0:T(8,128)} %copy.50.refs_9_.refs_3_, ...), custom_call_target="tpu_custom_call" | custom-call | flops 1 | bytes 1 | tf_op jit(solution)/shard_map/attn_bwd/pallas_call | solution.py:512
  309.5 4.3 fusion.1
  315.7 8.5 %attn_grad.2 = (bf16[2,2,4,208,384]{4,3,2,1,0:T(8,128)(2,1)}, bf16[2,2,4,208,384]{4,3,2,1,0:T(8,128)(2,1)}) custom-call(s32[4]{0:T(128)} %pad_add_fusion.2.here_ref, bf16[512,768]{1,0:T(8,128)(2,1)} %bitcast.308, bf16[512,768]{1,0:T(8,128)(2,1)} %get-tuple-element.164.att_ref, bf16[512,2304]{1,0:T(8,128)(2,1)} %get-tuple-element.201.proj_ref, ...), custom_call_target="tpu_custom_call" | custom-call | flops 1 | bytes 1 | tf_op jit(solution)/shard_map/attn_grad/pallas_call | solution.py:588
  324.2 14.2 %attn_bwd.4 = (bf16[1024,2304]{1,0:T(8,128)(2,1)}, bf16[1024,768]{1,0:T(8,128)(2,1)}, f32[8,768]{1,0:T(8,128)}) custom-call(f32[1024,768]{1,0:T(8,128)} %get-tuple-element.172.refs_0_.dh_ref, bf16[1024,2304]{1,0:T(8,128)(2,1)} %get-tuple-element.127.refs_1_, bf16[768,768]{1,0:T(8,128)(2,1)} %get-tuple-element.173.refs_2_, ...), custom_call_target="tpu_custom_call" | custom-call | flops 1 | bytes 1 | tf_op jit(solution)/shard_map/attn_bwd/pallas_call | solution.py:512
  338.4 3.8 collective-permute-done.29
  343.1 2.5 fusion.2
  347.8 13.8 %attn_bwd.5 = (bf16[1024,2304]{1,0:T(8,128)(2,1)}, bf16[1024,768]{1,0:T(8,128)(2,1)}, f32[8,768]{1,0:T(8,128)}) custom-call(f32[1024,768]{1,0:T(8,128)} %get-tuple-element.172.refs_0_.dh_ref, bf16[1024,2304]{1,0:T(8,128)(2,1)} %get-tuple-element.127.refs_1_, ...), custom_call_target="tpu_custom_call", output_to_operand_aliasing={{0}: (6, {}), {1}: (7, {})} | custom-call | flops 1 | bytes 1 | tf_op jit(solution)/shard_map/attn_bwd/pallas_call | solution.py:512
  361.7 8.2 %collective-permute-done.31 = bf16[4,192,384]{2,1,0:T(8,128)(2,1)S(1)} collective-permute-done((bf16[4,192,384]{2,1,0:T(8,128)(2,1)S(1)}, bf16[4,192,384]{2,1,0:T(8,128)(2,1)S(1)}, u32[]{:S(2)}, u32[]{:S(2)}) %collective-permute-start.31) | collective-permute-done | bytes 589856 | tf_op jit(solution)/shard_map/ppermute | solution.py:693
  371.0 1.6 fusion.23
  372.7 1.9 fusion.24
  375.4 2.1 fusion.4
  378.9 2.1 fusion.12
  382.3 2.7 collective-permute-start.33
  385.7 1.7 collective-permute-start.34
  387.4 11.7 %attn_grad.3 = (bf16[2,2,4,208,384]{4,3,2,1,0:T(8,128)(2,1)}, bf16[2,2,4,208,384]{4,3,2,1,0:T(8,128)(2,1)}) custom-call(s32[4]{0:T(128)} %pad_add_fusion.2.here_ref, bf16[1024,768]{1,0:T(8,128)(2,1)} %bitcast.303, bf16[1024,768]{1,0:T(8,128)(2,1)} %get-tuple-element.189.att_ref, bf16[1024,2304]{1,0:T(8,128)(2,1)} %get-tuple-element.209.proj_ref, ...), custom_call_target="tpu_custom_call" | custom-call | flops 1 | bytes 1 | tf_op jit(solution)/shard_map/attn_grad/pallas_call | solution.py:588
  399.3 2.0 collective-permute-done.36
  401.4 2.0 fusion.7
  403.4 2.6 collective-permute-done.33
  407.4 1.6 collective-permute-start.38
  409.0 1.9 fusion.18
  411.7 5.8 %input_grad.2 = f32[512,768]{1,0:T(8,128)} custom-call(bf16[512,2304]{1,0:T(8,128)(2,1)} %get-tuple-element.201.proj_ref, bf16[768,2304]{1,0:T(8,128)(2,1)} %get-tuple-element.202.weight_ref, f32[512,768]{1,0:T(8,128)} %get-tuple-element.156.refs_0_.dh_ref), custom_call_target="tpu_custom_call" | custom-call | flops 1 | bytes 1 | tf_op jit(solution)/shard_map/input_grad/pallas_call | solution.py:611
  417.5 2.3 fusion.13
  420.7 2.4 fusion.5
  423.8 1.9 fusion.33
  425.7 1.9 fusion.39
  428.3 10.5 %collective-permute-start.41 = (bf16[208,384]{1,0:T(8,128)(2,1)}, bf16[208,384]{1,0:T(8,128)(2,1)S(1)}, u32[]{:S(2)}, u32[]{:S(2)}) collective-permute-start(bf16[208,384]{1,0:T(8,128)(2,1)} %pad_maximum_fusion.9), channel_id=1, source_target_pairs={{0,2},{1,3},{2,0},{3,1},{4,6},{5,7},{6,4},{7,5},{8,10},{9,11},{10,... | collective-permute-start | bytes 479240 | tf_op jit(solution)/shard_map/ppermute | solution.py:693
  443.0 9.3 %input_grad.3 = f32[1024,768]{1,0:T(8,128)} custom-call(bf16[1024,2304]{1,0:T(8,128)(2,1)} %get-tuple-element.209.proj_ref, bf16[768,2304]{1,0:T(8,128)(2,1)} %get-tuple-element.210.weight_ref, f32[1024,768]{1,0:T(8,128)} %get-tuple-element.172.refs_0_.dh_ref), custom_call_target="tpu_custom_call" | custom-call | flops 1 | bytes 1 | tf_op jit(solution)/shard_map/input_grad/pallas_call | solution.py:611
  452.4 1.9 fusion.6
  455.2 1.9 fusion.17
  461.0 4.0 collective-permute-done.47
  465.0 2.1 fusion.36
  467.1 2.2 fusion.30
  471.1 2.0 collective-permute-start.49
  474.0 1.7 collective-permute-start.50
  478.5 6.0 %collective-permute-done.49 = bf16[208,384]{1,0:T(8,128)(2,1)S(1)} collective-permute-done((bf16[208,384]{1,0:T(8,128)(2,1)S(1)}, bf16[208,384]{1,0:T(8,128)(2,1)S(1)}, u32[]{:S(2)}, u32[]{:S(2)}) %collective-permute-start.49) | collective-permute-done | bytes 159776 | tf_op jit(solution)/shard_map/ppermute | solution.py:693
  (194 shorter events, 52.4 us)
Async XLA Ops:
  7.2 162.1 %all-gather.3.cloned.1.call-start = ((), (), s32[]{:S(2)}) async-start(), calls=%async_computation.2 | async-start | bytes 19464192 | tf_op jit(solution)/shard_map/all_gather | solution.py:811
  10.2 47.0 %copy-start.28 = (s32[8]{0:T(128)S(1)}, s32[8]{0:T(128)}, u32[]{:S(2)}) copy-start(s32[8]{0:T(128)} %param.18) | copy-start | bytes 100
  10.2 83.8 %copy-start.26 = (s32[64]{0:T(128)S(1)}, s32[64]{0:T(128)}, u32[]{:S(2)}) copy-start(s32[64]{0:T(128)} %param.20) | copy-start | bytes 772
  10.2 84.0 %copy-start.23 = (s32[4,4]{1,0:T(4,128)S(1)}, s32[4,4]{1,0:T(4,128)}, u32[]{:S(2)}) copy-start(s32[4,4]{1,0:T(4,128)} %param.19) | copy-start | bytes 196
  10.2 459.9 %reduce-scatter.2.cloned.1.call-start = ((), (), s32[]{:S(2)}) async-start(), calls=%async_computation.1 | async-start | bytes 9732096 | tf_op jit(solution)/shard_map/reduce_scatter | solution.py:883
  10.5 10.2 %collective-permute-start.12 = (bf16[208,384]{1,0:T(8,128)(2,1)S(1)}, bf16[208,384]{1,0:T(8,128)(2,1)S(1)}, u32[]{:S(2)}, u32[]{:S(2)}) collective-permute-start(bf16[208,384]{1,0:T(8,128)(2,1)S(1)} %get-tuple-element.255), channel_id=1, source_target_pairs={{0,6},{1,7},{2,4},{3,5},{4,2},{5,3},{6,0},{7,1},{8,14},{9,15},{10,... | collective-permute-start | bytes 479240 | tf_op jit(solution)/shard_map/ppermute | solution.py:693
  15.6 29.1 %collective-permute-start.11 = (bf16[208,384]{1,0:T(8,128)(2,1)S(1)}, bf16[208,384]{1,0:T(8,128)(2,1)S(1)}, u32[]{:S(2)}, u32[]{:S(2)}) collective-permute-start(bf16[208,384]{1,0:T(8,128)(2,1)S(1)} %get-tuple-element.255), channel_id=1, source_target_pairs={{0,4},{1,5},{2,6},{3,7},{4,0},{5,1},{6,2},{7,3},{8,12},{9,13},{10,... | collective-permute-start | bytes 479240 | tf_op jit(solution)/shard_map/ppermute | solution.py:693
  15.6 29.1 %collective-permute-start.10 = (bf16[208,384]{1,0:T(8,128)(2,1)S(1)}, bf16[208,384]{1,0:T(8,128)(2,1)S(1)}, u32[]{:S(2)}, u32[]{:S(2)}) collective-permute-start(bf16[208,384]{1,0:T(8,128)(2,1)S(1)} %get-tuple-element.255), channel_id=1, source_target_pairs={{0,2},{1,3},{2,0},{3,1},{4,6},{5,7},{6,4},{7,5},{8,10},{9,11},{10,... | collective-permute-start | bytes 479240 | tf_op jit(solution)/shard_map/ppermute | solution.py:693
  16.2 30.6 %collective-permute-start.2 = (bf16[208,384]{1,0:T(8,128)(2,1)S(1)}, bf16[208,384]{1,0:T(8,128)(2,1)S(1)}, u32[]{:S(2)}, u32[]{:S(2)}) collective-permute-start(bf16[208,384]{1,0:T(8,128)(2,1)S(1)} %get-tuple-element.254), channel_id=1, source_target_pairs={{0,6},{1,7},{2,4},{3,5},{4,2},{5,3},{6,0},{7,1},{8,14},{9,15},{10,... | collective-permute-start | bytes 479240 | tf_op jit(solution)/shard_map/ppermute | solution.py:693
  20.0 35.5 %collective-permute-start.1 = (bf16[208,384]{1,0:T(8,128)(2,1)S(1)}, bf16[208,384]{1,0:T(8,128)(2,1)S(1)}, u32[]{:S(2)}, u32[]{:S(2)}) collective-permute-start(bf16[208,384]{1,0:T(8,128)(2,1)S(1)} %get-tuple-element.254), channel_id=1, source_target_pairs={{0,4},{1,5},{2,6},{3,7},{4,0},{5,1},{6,2},{7,3},{8,12},{9,13},{10,... | collective-permute-start | bytes 479240 | tf_op jit(solution)/shard_map/ppermute | solution.py:693
  20.6 34.8 %collective-permute-start = (bf16[208,384]{1,0:T(8,128)(2,1)S(1)}, bf16[208,384]{1,0:T(8,128)(2,1)S(1)}, u32[]{:S(2)}, u32[]{:S(2)}) collective-permute-start(bf16[208,384]{1,0:T(8,128)(2,1)S(1)} %get-tuple-element.254), channel_id=1, source_target_pairs={{0,2},{1,3},{2,0},{3,1},{4,6},{5,7},{6,4},{7,5},{8,10},{9,11},{10,... | collective-permute-start | bytes 479240 | tf_op jit(solution)/shard_map/ppermute | solution.py:693
  44.8 66.1 %copy-start.4 = (bf16[4,208,384]{2,1,0:T(8,128)(2,1)}, bf16[4,208,384]{2,1,0:T(8,128)(2,1)S(1)}, u32[]{:S(2)}) copy-start(bf16[4,208,384]{2,1,0:T(8,128)(2,1)S(1)} %pad_maximum_fusion.2.refs_0_) | copy-start | bytes 1916932
  44.8 23.7 %collective-permute-start.16 = (bf16[4,208,384]{2,1,0:T(8,128)(2,1)S(1)}, bf16[4,208,384]{2,1,0:T(8,128)(2,1)S(1)}, u32[]{:S(2)}, u32[]{:S(2)}) collective-permute-start(bf16[4,208,384]{2,1,0:T(8,128)(2,1)S(1)} %pad_maximum_fusion.2.refs_0_), channel_id=1, source_target_pairs={{0,8},{1,9},{2,10},{3,11},{4,12},{5,13},{6,14},{7,15},{8,0},{9,1},... | collective-permute-start | bytes 1916936 | tf_op jit(solution)/shard_map/ppermute | solution.py:693
  44.9 23.7 %collective-permute-start.14 = (bf16[4,208,384]{2,1,0:T(8,128)(2,1)S(1)}, bf16[4,208,384]{2,1,0:T(8,128)(2,1)}, u32[]{:S(2)}, u32[]{:S(2)}) collective-permute-start(bf16[4,208,384]{2,1,0:T(8,128)(2,1)S(1)} %pad_maximum_fusion.2.refs_0_), channel_id=1, source_target_pairs={{0,1},{1,0},{2,3},{3,2},{4,5},{5,4},{6,7},{7,6},{8,9},{9,8},{10,11... | collective-permute-start | bytes 1916936 | tf_op jit(solution)/shard_map/ppermute | solution.py:693
  46.9 21.6 %collective-permute-start.13 = (bf16[4,208,384]{2,1,0:T(8,128)(2,1)S(1)}, bf16[4,208,384]{2,1,0:T(8,128)(2,1)}, u32[]{:S(2)}, u32[]{:S(2)}) collective-permute-start(bf16[4,208,384]{2,1,0:T(8,128)(2,1)S(1)} %pad_maximum_fusion.2.refs_0_), channel_id=1, source_target_pairs={{0,16},{1,17},{2,18},{3,19},{4,20},{5,21},{6,22},{7,23},{8,24},{9,... | collective-permute-start | bytes 1916936 | tf_op jit(solution)/shard_map/ppermute | solution.py:693
  55.6 70.1 %copy-start.3 = (bf16[4,208,384]{2,1,0:T(8,128)(2,1)}, bf16[4,208,384]{2,1,0:T(8,128)(2,1)S(1)}, u32[]{:S(2)}) copy-start(bf16[4,208,384]{2,1,0:T(8,128)(2,1)S(1)} %pad_maximum_fusion.1.refs_0_) | copy-start | bytes 1916932
  55.6 36.5 %collective-permute-start.3 = (bf16[4,208,384]{2,1,0:T(8,128)(2,1)S(1)}, bf16[4,208,384]{2,1,0:T(8,128)(2,1)S(1)}, u32[]{:S(2)}, u32[]{:S(2)}) collective-permute-start(bf16[4,208,384]{2,1,0:T(8,128)(2,1)S(1)} %pad_maximum_fusion.1.refs_0_), channel_id=1, source_target_pairs={{0,1},{1,0},{2,3},{3,2},{4,5},{5,4},{6,7},{7,6},{8,9},{9,8},{10,11... | collective-permute-start | bytes 1916936 | tf_op jit(solution)/shard_map/ppermute | solution.py:693
  57.2 37.4 %collective-permute-start.4 = (bf16[4,208,384]{2,1,0:T(8,128)(2,1)S(1)}, bf16[4,208,384]{2,1,0:T(8,128)(2,1)S(1)}, u32[]{:S(2)}, u32[]{:S(2)}) collective-permute-start(bf16[4,208,384]{2,1,0:T(8,128)(2,1)S(1)} %pad_maximum_fusion.1.refs_0_), channel_id=1, source_target_pairs={{0,16},{1,17},{2,18},{3,19},{4,20},{5,21},{6,22},{7,23},{8,24},{9,... | collective-permute-start | bytes 1916936 | tf_op jit(solution)/shard_map/ppermute | solution.py:693
  68.5 26.8 %collective-permute-start.17 = (bf16[4,208,384]{2,1,0:T(8,128)(2,1)}, bf16[4,208,384]{2,1,0:T(8,128)(2,1)}, u32[]{:S(2)}, u32[]{:S(2)}) collective-permute-start(bf16[4,208,384]{2,1,0:T(8,128)(2,1)} %collective-permute-done.13.refs_1_), channel_id=1, source_target_pairs={{0,8},{1,9},{2,10},{3,11},{4,12},{5,13},{6,14},{7,15},{8,0},{9,1},... | collective-permute-start | bytes 1916936 | tf_op jit(solution)/shard_map/ppermute | solution.py:693
  68.5 37.7 %collective-permute-start.15 = (bf16[4,208,384]{2,1,0:T(8,128)(2,1)}, bf16[4,208,384]{2,1,0:T(8,128)(2,1)}, u32[]{:S(2)}, u32[]{:S(2)}) collective-permute-start(bf16[4,208,384]{2,1,0:T(8,128)(2,1)} %collective-permute-done.13.refs_1_), channel_id=1, source_target_pairs={{0,1},{1,0},{2,3},{3,2},{4,5},{5,4},{6,7},{7,6},{8,9},{9,8},{10,11... | collective-permute-start | bytes 1916936 | tf_op jit(solution)/shard_map/ppermute | solution.py:693
  68.6 26.2 %collective-permute-start.18 = (bf16[4,208,384]{2,1,0:T(8,128)(2,1)}, bf16[4,208,384]{2,1,0:T(8,128)(2,1)}, u32[]{:S(2)}, u32[]{:S(2)}) collective-permute-start(bf16[4,208,384]{2,1,0:T(8,128)(2,1)} %collective-permute-done.14.refs_2_), channel_id=1, source_target_pairs={{0,8},{1,9},{2,10},{3,11},{4,12},{5,13},{6,14},{7,15},{8,0},{9,1},... | collective-permute-start | bytes 1916936 | tf_op jit(solution)/shard_map/ppermute | solution.py:693
  92.1 33.5 %copy-start.11 = (bf16[4,208,384]{2,1,0:T(8,128)(2,1)}, bf16[4,208,384]{2,1,0:T(8,128)(2,1)S(1)}, u32[]{:S(2)}) copy-start(bf16[4,208,384]{2,1,0:T(8,128)(2,1)S(1)} %collective-permute-done.3.refs_1_) | copy-start | bytes 1916932
  92.1 15.0 %collective-permute-start.5 = (bf16[4,208,384]{2,1,0:T(8,128)(2,1)S(1)}, bf16[4,208,384]{2,1,0:T(8,128)(2,1)S(1)}, u32[]{:S(2)}, u32[]{:S(2)}) collective-permute-start(bf16[4,208,384]{2,1,0:T(8,128)(2,1)S(1)} %collective-permute-done.3.refs_1_), channel_id=1, source_target_pairs={{0,16},{1,17},{2,18},{3,19},{4,20},{5,21},{6,22},{7,23},{8,24},{9,... | collective-permute-start | bytes 1916936 | tf_op jit(solution)/shard_map/ppermute | solution.py:693
  94.4 31.3 %copy-start.22 = (s32[4,4]{1,0:T(4,128)}, s32[4,4]{1,0:T(4,128)S(1)}, u32[]{:S(2)}) copy-start(s32[4,4]{1,0:T(4,128)S(1)} %sub.25.spot_ref) | copy-start | bytes 196
  94.7 31.0 %copy-start.12 = (bf16[4,208,384]{2,1,0:T(8,128)(2,1)}, bf16[4,208,384]{2,1,0:T(8,128)(2,1)S(1)}, u32[]{:S(2)}) copy-start(bf16[4,208,384]{2,1,0:T(8,128)(2,1)S(1)} %collective-permute-done.4.refs_2_) | copy-start | bytes 1916932
  94.7 31.0 %collective-permute-start.6 = (bf16[4,208,384]{2,1,0:T(8,128)(2,1)S(1)}, bf16[4,208,384]{2,1,0:T(8,128)(2,1)}, u32[]{:S(2)}, u32[]{:S(2)}) collective-permute-start(bf16[4,208,384]{2,1,0:T(8,128)(2,1)S(1)} %pad_maximum_fusion.1.refs_0_), channel_id=1, source_target_pairs={{0,8},{1,9},{2,10},{3,11},{4,12},{5,13},{6,14},{7,15},{8,0},{9,1},... | collective-permute-start | bytes 1916936 | tf_op jit(solution)/shard_map/ppermute | solution.py:693
  94.8 30.9 %collective-permute-start.7 = (bf16[4,208,384]{2,1,0:T(8,128)(2,1)S(1)}, bf16[4,208,384]{2,1,0:T(8,128)(2,1)}, u32[]{:S(2)}, u32[]{:S(2)}) collective-permute-start(bf16[4,208,384]{2,1,0:T(8,128)(2,1)S(1)} %collective-permute-done.3.refs_1_), channel_id=1, source_target_pairs={{0,8},{1,9},{2,10},{3,11},{4,12},{5,13},{6,14},{7,15},{8,0},{9,1},... | collective-permute-start | bytes 1916936 | tf_op jit(solution)/shard_map/ppermute | solution.py:693
  95.3 30.4 %collective-permute-start.8 = (bf16[4,208,384]{2,1,0:T(8,128)(2,1)S(1)}, bf16[4,208,384]{2,1,0:T(8,128)(2,1)}, u32[]{:S(2)}, u32[]{:S(2)}) collective-permute-start(bf16[4,208,384]{2,1,0:T(8,128)(2,1)S(1)} %collective-permute-done.4.refs_2_), channel_id=1, source_target_pairs={{0,8},{1,9},{2,10},{3,11},{4,12},{5,13},{6,14},{7,15},{8,0},{9,1},... | collective-permute-start | bytes 1916936 | tf_op jit(solution)/shard_map/ppermute | solution.py:693
  106.2 4.7 collective-permute-start.19
  107.1 18.6 %copy-start.13 = (bf16[4,208,384]{2,1,0:T(8,128)(2,1)}, bf16[4,208,384]{2,1,0:T(8,128)(2,1)S(1)}, u32[]{:S(2)}) copy-start(bf16[4,208,384]{2,1,0:T(8,128)(2,1)S(1)} %collective-permute-done.5.refs_3_) | copy-start | bytes 1916932
  107.1 18.6 %collective-permute-start.9 = (bf16[4,208,384]{2,1,0:T(8,128)(2,1)S(1)}, bf16[4,208,384]{2,1,0:T(8,128)(2,1)}, u32[]{:S(2)}, u32[]{:S(2)}) collective-permute-start(bf16[4,208,384]{2,1,0:T(8,128)(2,1)S(1)} %collective-permute-done.5.refs_3_), channel_id=1, source_target_pairs={{0,8},{1,9},{2,10},{3,11},{4,12},{5,13},{6,14},{7,15},{8,0},{9,1},... | collective-permute-start | bytes 1916936 | tf_op jit(solution)/shard_map/ppermute | solution.py:693
  205.9 20.4 %copy-start.29 = (s32[32]{0:T(128)S(1)}, s32[32]{0:T(128)}, u32[]{:S(2)}) copy-start(s32[32]{0:T(128)} %constant.136.clone) | copy-start | bytes 388
  206.8 21.8 %copy-start.17 = (bf16[1,32,768]{2,1,0:T(8,128)(2,1)}, bf16[1,32,768]{2,1,0:T(8,128)(2,1)S(1)}, u32[]{:S(2)}) copy-start(bf16[1,32,768]{2,1,0:T(8,128)(2,1)S(1)} %get-tuple-element.262.own_ref) | copy-start | bytes 147460
  206.8 5.7 %collective-permute-start.21 = (bf16[32,768]{1,0:T(8,128)(2,1)S(1)}, bf16[32,768]{1,0:T(8,128)(2,1)S(1)}, u32[]{:S(2)}, u32[]{:S(2)}) collective-permute-start(bf16[32,768]{1,0:T(8,128)(2,1)S(1)} %get-tuple-element.261), channel_id=1, source_target_pairs={{0,4},{1,5},{2,6},{3,7},{4,0},{5,1},{6,2},{7,3},{8,12},{9,13},{10,... | collective-permute-start | bytes 147464 | tf_op jit(solution)/shard_map/ppermute | solution.py:693
  208.4 4.5 collective-permute-start.20
  208.9 5.9 %collective-permute-start.22 = (bf16[32,768]{1,0:T(8,128)(2,1)S(1)}, bf16[32,768]{1,0:T(8,128)(2,1)S(1)}, u32[]{:S(2)}, u32[]{:S(2)}) collective-permute-start(bf16[32,768]{1,0:T(8,128)(2,1)S(1)} %get-tuple-element.261), channel_id=1, source_target_pairs={{0,6},{1,7},{2,4},{3,5},{4,2},{5,3},{6,0},{7,1},{8,14},{9,15},{10,... | collective-permute-start | bytes 147464 | tf_op jit(solution)/shard_map/ppermute | solution.py:693
  214.8 7.0 %collective-permute-start.24 = (bf16[4,32,768]{2,1,0:T(8,128)(2,1)S(1)}, bf16[4,32,768]{2,1,0:T(8,128)(2,1)S(1)}, u32[]{:S(2)}, u32[]{:S(2)}) collective-permute-start(bf16[4,32,768]{2,1,0:T(8,128)(2,1)S(1)} %get-tuple-element.260), channel_id=1, source_target_pairs={{0,16},{1,17},{2,18},{3,19},{4,20},{5,21},{6,22},{7,23},{8,24},{9,... | collective-permute-start | bytes 589832 | tf_op jit(solution)/shard_map/ppermute | solution.py:693
  216.3 7.7 %collective-permute-start.23 = (bf16[4,32,768]{2,1,0:T(8,128)(2,1)S(1)}, bf16[4,32,768]{2,1,0:T(8,128)(2,1)S(1)}, u32[]{:S(2)}, u32[]{:S(2)}) collective-permute-start(bf16[4,32,768]{2,1,0:T(8,128)(2,1)S(1)} %get-tuple-element.260), channel_id=1, source_target_pairs={{0,1},{1,0},{2,3},{3,2},{4,5},{5,4},{6,7},{7,6},{8,9},{9,8},{10,11... | collective-permute-start | bytes 589832 | tf_op jit(solution)/shard_map/ppermute | solution.py:693
  216.9 9.2 %collective-permute-start.25 = (bf16[4,32,768]{2,1,0:T(8,128)(2,1)S(1)}, bf16[4,32,768]{2,1,0:T(8,128)(2,1)S(1)}, u32[]{:S(2)}, u32[]{:S(2)}) collective-permute-start(bf16[4,32,768]{2,1,0:T(8,128)(2,1)S(1)} %get-tuple-element.260), channel_id=1, source_target_pairs={{0,17},{1,16},{2,19},{3,18},{4,21},{5,20},{6,23},{7,22},{8,25},{9,... | collective-permute-start | bytes 589832 | tf_op jit(solution)/shard_map/ppermute | solution.py:693
  226.2 2.4 collective-permute-start.26
  295.4 14.0 %collective-permute-start.27 = (bf16[2,2,4,384,384]{4,3,2,1,0:T(8,128)(2,1)}, bf16[2,2,4,384,384]{4,3,2,1,0:T(8,128)(2,1)}, u32[]{:S(2)}, u32[]{:S(2)}) collective-permute-start(bf16[2,2,4,384,384]{4,3,2,1,0:T(8,128)(2,1)} %get-tuple-element.162), channel_id=1, source_target_pairs={{0,8},{1,9},{2,10},{3,11},{4,12},{5,13},{6,14},{7,15},{8,0},{9,1},... | collective-permute-start | bytes 14155784 | tf_op jit(solution)/shard_map/ppermute | solution.py:693
  313.7 28.5 %collective-permute-start.29 = (bf16[2,4,192,384]{3,2,1,0:T(8,128)(2,1)}, bf16[2,4,192,384]{3,2,1,0:T(8,128)(2,1)S(1)}, u32[]{:S(2)}, u32[]{:S(2)}) collective-permute-start(bf16[2,4,192,384]{3,2,1,0:T(8,128)(2,1)} %get-tuple-element.235), channel_id=1, source_target_pairs={{0,1},{1,0},{2,3},{3,2},{4,5},{5,4},{6,7},{7,6},{8,9},{9,8},{10,11... | collective-permute-start | bytes 3538952 | tf_op jit(solution)/shard_map/ppermute | solution.py:693
  315.1 28.0 %collective-permute-start.28 = (bf16[2,4,192,384]{3,2,1,0:T(8,128)(2,1)S(1)}, bf16[2,4,192,384]{3,2,1,0:T(8,128)(2,1)S(1)}, u32[]{:S(2)}, u32[]{:S(2)}) collective-permute-start(bf16[2,4,192,384]{3,2,1,0:T(8,128)(2,1)S(1)} %get-tuple-element.236), channel_id=1, source_target_pairs={{0,16},{1,17},{2,18},{3,19},{4,20},{5,21},{6,22},{7,23},{8,24},{9,... | collective-permute-start | bytes 3538952 | tf_op jit(solution)/shard_map/ppermute | solution.py:693
  345.6 29.8 %collective-permute-start.35 = (bf16[2,2,4,208,384]{4,3,2,1,0:T(8,128)(2,1)}, bf16[2,2,4,208,384]{4,3,2,1,0:T(8,128)(2,1)}, u32[]{:S(2)}, u32[]{:S(2)}) collective-permute-start(bf16[2,2,4,208,384]{4,3,2,1,0:T(8,128)(2,1)} %get-tuple-element.187), channel_id=1, source_target_pairs={{0,8},{1,9},{2,10},{3,11},{4,12},{5,13},{6,14},{7,15},{8,0},{9,1},... | collective-permute-start | bytes 7667720 | tf_op jit(solution)/shard_map/ppermute | solution.py:693
  345.7 24.2 %collective-permute-start.31 = (bf16[4,192,384]{2,1,0:T(8,128)(2,1)S(1)}, bf16[4,192,384]{2,1,0:T(8,128)(2,1)S(1)}, u32[]{:S(2)}, u32[]{:S(2)}) collective-permute-start(bf16[4,192,384]{2,1,0:T(8,128)(2,1)S(1)} %get-tuple-element.233), channel_id=1, source_target_pairs={{0,16},{1,17},{2,18},{3,19},{4,20},{5,21},{6,22},{7,23},{8,24},{9,... | collective-permute-start | bytes 1769480 | tf_op jit(solution)/shard_map/ppermute | solution.py:693
  346.4 23.8 %collective-permute-start.30 = (bf16[4,192,384]{2,1,0:T(8,128)(2,1)S(1)}, bf16[4,192,384]{2,1,0:T(8,128)(2,1)S(1)}, u32[]{:S(2)}, u32[]{:S(2)}) collective-permute-start(bf16[4,192,384]{2,1,0:T(8,128)(2,1)S(1)} %get-tuple-element.234), channel_id=1, source_target_pairs={{0,1},{1,0},{2,3},{3,2},{4,5},{5,4},{6,7},{7,6},{8,9},{9,8},{10,11... | collective-permute-start | bytes 1769480 | tf_op jit(solution)/shard_map/ppermute | solution.py:693
  377.5 23.8 %collective-permute-start.36 = (bf16[2,4,112,384]{3,2,1,0:T(8,128)(2,1)}, bf16[2,4,112,384]{3,2,1,0:T(8,128)(2,1)S(1)}, u32[]{:S(2)}, u32[]{:S(2)}) collective-permute-start(bf16[2,4,112,384]{3,2,1,0:T(8,128)(2,1)} %fusion.4), channel_id=1, source_target_pairs={{0,16},{1,17},{2,18},{3,19},{4,20},{5,21},{6,22},{7,23},{8,24},{9,... | collective-permute-start | bytes 2064392 | tf_op jit(solution)/shard_map/ppermute | solution.py:693
  381.0 18.3 %collective-permute-start.37 = (bf16[2,4,96,384]{3,2,1,0:T(8,128)(2,1)}, bf16[2,4,96,384]{3,2,1,0:T(8,128)(2,1)}, u32[]{:S(2)}, u32[]{:S(2)}) collective-permute-start(bf16[2,4,96,384]{3,2,1,0:T(8,128)(2,1)} %fusion.12), channel_id=1, source_target_pairs={{0,1},{1,0},{2,3},{3,2},{4,5},{5,4},{6,7},{7,6},{8,9},{9,8},{10,11... | collective-permute-start | bytes 1769480 | tf_op jit(solution)/shard_map/ppermute | solution.py:693
  381.5 24.5 %collective-permute-start.32 = (bf16[384,384]{1,0:T(8,128)(2,1)}, bf16[384,384]{1,0:T(8,128)(2,1)}, u32[]{:S(2)}, u32[]{:S(2)}) collective-permute-start(bf16[384,384]{1,0:T(8,128)(2,1)} %pad_maximum_fusion.5), channel_id=1, source_target_pairs={{0,2},{1,3},{2,0},{3,1},{4,6},{5,7},{6,4},{7,5},{8,10},{9,11},{10,... | collective-permute-start | bytes 884744 | tf_op jit(solution)/shard_map/ppermute | solution.py:693
  382.3 23.8 %collective-permute-start.33 = (bf16[384,384]{1,0:T(8,128)(2,1)}, bf16[384,384]{1,0:T(8,128)(2,1)}, u32[]{:S(2)}, u32[]{:S(2)}) collective-permute-start(bf16[384,384]{1,0:T(8,128)(2,1)} %pad_maximum_fusion.6), channel_id=1, source_target_pairs={{0,4},{1,5},{2,6},{3,7},{4,0},{5,1},{6,2},{7,3},{8,12},{9,13},{10,... | collective-permute-start | bytes 884744 | tf_op jit(solution)/shard_map/ppermute | solution.py:693
  385.7 20.4 %collective-permute-start.34 = (bf16[384,384]{1,0:T(8,128)(2,1)}, bf16[384,384]{1,0:T(8,128)(2,1)}, u32[]{:S(2)}, u32[]{:S(2)}) collective-permute-start(bf16[384,384]{1,0:T(8,128)(2,1)} %pad_maximum_fusion.7), channel_id=1, source_target_pairs={{0,6},{1,7},{2,4},{3,5},{4,2},{5,3},{6,0},{7,1},{8,14},{9,15},{10,... | collective-permute-start | bytes 884744 | tf_op jit(solution)/shard_map/ppermute | solution.py:693
  407.3 10.1 %collective-permute-start.40 = (bf16[2,2,4,208,384]{4,3,2,1,0:T(8,128)(2,1)}, bf16[2,2,4,208,384]{4,3,2,1,0:T(8,128)(2,1)}, u32[]{:S(2)}, u32[]{:S(2)}) collective-permute-start(bf16[2,2,4,208,384]{4,3,2,1,0:T(8,128)(2,1)} %get-tuple-element.205), channel_id=1, source_target_pairs={{0,8},{1,9},{2,10},{3,11},{4,12},{5,13},{6,14},{7,15},{8,0},{9,1},... | collective-permute-start | bytes 7667720 | tf_op jit(solution)/shard_map/ppermute | solution.py:693
  407.4 16.4 %collective-permute-start.38 = (bf16[4,112,384]{2,1,0:T(8,128)(2,1)}, bf16[4,112,384]{2,1,0:T(8,128)(2,1)S(1)}, u32[]{:S(2)}, u32[]{:S(2)}) collective-permute-start(bf16[4,112,384]{2,1,0:T(8,128)(2,1)} %fusion.7), channel_id=1, source_target_pairs={{0,1},{1,0},{2,3},{3,2},{4,5},{5,4},{6,7},{7,6},{8,9},{9,8},{10,11... | collective-permute-start | bytes 1032200 | tf_op jit(solution)/shard_map/ppermute | solution.py:693
  410.9 12.9 %collective-permute-start.39 = (bf16[4,96,384]{2,1,0:T(8,128)(2,1)}, bf16[4,96,384]{2,1,0:T(8,128)(2,1)S(1)}, u32[]{:S(2)}, u32[]{:S(2)}) collective-permute-start(bf16[4,96,384]{2,1,0:T(8,128)(2,1)} %fusion.18), channel_id=1, source_target_pairs={{0,16},{1,17},{2,18},{3,19},{4,20},{5,21},{6,22},{7,23},{8,24},{9,... | collective-permute-start | bytes 884744 | tf_op jit(solution)/shard_map/ppermute | solution.py:693
  419.7 32.6 %collective-permute-start.45 = (bf16[2,4,96,384]{3,2,1,0:T(8,128)(2,1)}, bf16[2,4,96,384]{3,2,1,0:T(8,128)(2,1)}, u32[]{:S(2)}, u32[]{:S(2)}) collective-permute-start(bf16[2,4,96,384]{3,2,1,0:T(8,128)(2,1)} %fusion.13), channel_id=1, source_target_pairs={{0,1},{1,0},{2,3},{3,2},{4,5},{5,4},{6,7},{7,6},{8,9},{9,8},{10,11... | collective-permute-start | bytes 1769480 | tf_op jit(solution)/shard_map/ppermute | solution.py:693
  423.1 29.3 %collective-permute-start.44 = (bf16[2,4,112,384]{3,2,1,0:T(8,128)(2,1)}, bf16[2,4,112,384]{3,2,1,0:T(8,128)(2,1)}, u32[]{:S(2)}, u32[]{:S(2)}) collective-permute-start(bf16[2,4,112,384]{3,2,1,0:T(8,128)(2,1)} %fusion.5), channel_id=1, source_target_pairs={{0,16},{1,17},{2,18},{3,19},{4,20},{5,21},{6,22},{7,23},{8,24},{9,... | collective-permute-start | bytes 2064392 | tf_op jit(solution)/shard_map/ppermute | solution.py:693
  428.3 30.7 %collective-permute-start.41 = (bf16[208,384]{1,0:T(8,128)(2,1)}, bf16[208,384]{1,0:T(8,128)(2,1)S(1)}, u32[]{:S(2)}, u32[]{:S(2)}) collective-permute-start(bf16[208,384]{1,0:T(8,128)(2,1)} %pad_maximum_fusion.9), channel_id=1, source_target_pairs={{0,2},{1,3},{2,0},{3,1},{4,6},{5,7},{6,4},{7,5},{8,10},{9,11},{10,... | collective-permute-start | bytes 479240 | tf_op jit(solution)/shard_map/ppermute | solution.py:693
  439.5 19.5 %collective-permute-start.42 = (bf16[208,384]{1,0:T(8,128)(2,1)}, bf16[208,384]{1,0:T(8,128)(2,1)S(1)}, u32[]{:S(2)}, u32[]{:S(2)}) collective-permute-start(bf16[208,384]{1,0:T(8,128)(2,1)} %pad_maximum_fusion.10), channel_id=1, source_target_pairs={{0,4},{1,5},{2,6},{3,7},{4,0},{5,1},{6,2},{7,3},{8,12},{9,13},{10,... | collective-permute-start | bytes 479240 | tf_op jit(solution)/shard_map/ppermute | solution.py:693
  441.5 17.4 %collective-permute-start.43 = (bf16[208,384]{1,0:T(8,128)(2,1)}, bf16[208,384]{1,0:T(8,128)(2,1)}, u32[]{:S(2)}, u32[]{:S(2)}) collective-permute-start(bf16[208,384]{1,0:T(8,128)(2,1)} %pad_maximum_fusion.11), channel_id=1, source_target_pairs={{0,6},{1,7},{2,4},{3,5},{4,2},{5,3},{6,0},{7,1},{8,14},{9,15},{10,... | collective-permute-start | bytes 479240 | tf_op jit(solution)/shard_map/ppermute | solution.py:693
  454.3 10.6 %collective-permute-start.46 = (bf16[4,112,384]{2,1,0:T(8,128)(2,1)}, bf16[4,112,384]{2,1,0:T(8,128)(2,1)}, u32[]{:S(2)}, u32[]{:S(2)}) collective-permute-start(bf16[4,112,384]{2,1,0:T(8,128)(2,1)} %fusion.6), channel_id=1, source_target_pairs={{0,1},{1,0},{2,3},{3,2},{4,5},{5,4},{6,7},{7,6},{8,9},{9,8},{10,11... | collective-permute-start | bytes 1032200 | tf_op jit(solution)/shard_map/ppermute | solution.py:693
  457.1 7.9 %collective-permute-start.47 = (bf16[4,96,384]{2,1,0:T(8,128)(2,1)}, bf16[4,96,384]{2,1,0:T(8,128)(2,1)}, u32[]{:S(2)}, u32[]{:S(2)}) collective-permute-start(bf16[4,96,384]{2,1,0:T(8,128)(2,1)} %fusion.17), channel_id=1, source_target_pairs={{0,16},{1,17},{2,18},{3,19},{4,20},{5,21},{6,22},{7,23},{8,24},{9,... | collective-permute-start | bytes 884744 | tf_op jit(solution)/shard_map/ppermute | solution.py:693
  469.3 15.2 %collective-permute-start.48 = (bf16[208,384]{1,0:T(8,128)(2,1)S(1)}, bf16[208,384]{1,0:T(8,128)(2,1)S(1)}, u32[]{:S(2)}, u32[]{:S(2)}) collective-permute-start(bf16[208,384]{1,0:T(8,128)(2,1)S(1)} %pad_maximum_fusion.12), channel_id=1, source_target_pairs={{0,2},{1,3},{2,0},{3,1},{4,6},{5,7},{6,4},{7,5},{8,10},{9,11},{10,... | collective-permute-start | bytes 479240 | tf_op jit(solution)/shard_map/ppermute | solution.py:693
  471.1 13.4 %collective-permute-start.49 = (bf16[208,384]{1,0:T(8,128)(2,1)S(1)}, bf16[208,384]{1,0:T(8,128)(2,1)S(1)}, u32[]{:S(2)}, u32[]{:S(2)}) collective-permute-start(bf16[208,384]{1,0:T(8,128)(2,1)S(1)} %pad_maximum_fusion.13), channel_id=1, source_target_pairs={{0,4},{1,5},{2,6},{3,7},{4,0},{5,1},{6,2},{7,3},{8,12},{9,13},{10,... | collective-permute-start | bytes 479240 | tf_op jit(solution)/shard_map/ppermute | solution.py:693
  474.0 10.5 %collective-permute-start.50 = (bf16[208,384]{1,0:T(8,128)(2,1)S(1)}, bf16[208,384]{1,0:T(8,128)(2,1)S(1)}, u32[]{:S(2)}, u32[]{:S(2)}) collective-permute-start(bf16[208,384]{1,0:T(8,128)(2,1)S(1)} %pad_maximum_fusion.14), channel_id=1, source_target_pairs={{0,6},{1,7},{2,4},{3,5},{4,2},{5,3},{6,0},{7,1},{8,14},{9,15},{10,... | collective-permute-start | bytes 479240 | tf_op jit(solution)/shard_map/ppermute | solution.py:693
  (19 other events, 76.9 us)
Sparse Core Ops, SparseCore 0:
  11.6 157.6 all-gather.2
  295.8 156.3 reduce-scatter.1
